TPU v7x, 256 devices: a whole 4x4x8 slice. The times are simulated.
256 devices in a mesh: outer: 8 (over y, x_lo), inner: 32 (over z, x_hi, core).
Axes of the slice: x: 4 (x_hi: 2, x_lo: 2; x = x_hi * 2 + x_lo), y: 4, z: 8, core: 2. Of those that a mesh axis runs over, the one named last changes fastest.
Arguments:
- patches: bfloat16 [65536, 1536], P(('outer', 'inner')), may hold values from -6 to 6
- stem_weight: bfloat16 [1536, 1024], replicated, may hold values from -0.15625 to 0.15625
- ln_gain: float32 [1024], replicated, may hold values from 0.1 to 1.9
- up_weight: bfloat16 [1024, 2048], replicated, may hold values from -0.1875 to 0.1875
- down_weight: bfloat16 [2048, 1024], replicated, may hold values from -0.125 to 0.125
- cotangent: bfloat16 [65536, 1024], P(('outer', 'inner')), may hold values from -0.0234375 to 0.0234375
Outputs:
- grad_stem: float32 [1536, 1024], P('inner')
- grad_up: float32 [1024, 2048], P('inner')
- grad_down: float32 [2048, 1024], P('inner')
All inputs are finite; a program needn't handle non-finite values.
Results may differ from a plain program's by a relative error of at most 0.025.
Values may be sent and summed in bfloat16 or wider, within the bound.
No kernel may reach another device: no remote copies, remote signals or barrier semaphores. Data moves between devices by JAX's collectives and lax.ppermute only.
A program may use at most 128 MiB of HBM per device.

v0:
```python
import math

import jax
import jax.numpy as jnp
from jax import lax
from jax.sharding import PartitionSpec as P


def block_grads(patches, stem_weight, ln_gain, up_weight, down_weight, cotangent):
    embed = jnp.dot(patches, stem_weight, preferred_element_type=jnp.float32).astype(jnp.bfloat16)
    embed_f = embed.astype(jnp.float32)
    center = jnp.mean(embed_f, axis=1, keepdims=True)
    shifted = embed_f - center
    inverse = lax.rsqrt(jnp.mean(shifted * shifted, axis=1, keepdims=True) + 1e-06)
    normal = shifted * inverse
    normed = (normal * ln_gain).astype(jnp.bfloat16)
    preact = jnp.dot(normed, up_weight, preferred_element_type=jnp.float32)
    hidden = jax.nn.gelu(preact, approximate=False).astype(jnp.bfloat16)
    over_rows = (((0,), (0,)), ((), ()))
    over_cols = (((1,), (1,)), ((), ()))
    grad_down = lax.dot_general(hidden, cotangent, over_rows, preferred_element_type=jnp.float32)
    hidden_grad = lax.dot_general(
        cotangent, down_weight, over_cols, preferred_element_type=jnp.float32
    )
    derivative = 0.5 * (1.0 + jax.scipy.special.erf(preact / math.sqrt(2.0))) + preact * jnp.exp(
        -0.5 * preact * preact
    ) / math.sqrt(2.0 * math.pi)
    preact_grad = (hidden_grad * derivative).astype(jnp.bfloat16)
    grad_up = lax.dot_general(normed, preact_grad, over_rows, preferred_element_type=jnp.float32)
    normal_grad = (
        lax.dot_general(preact_grad, up_weight, over_cols, preferred_element_type=jnp.float32)
        * ln_gain
    )
    first_mean = jnp.mean(normal_grad, axis=1, keepdims=True)
    second_mean = jnp.mean(normal_grad * normal, axis=1, keepdims=True)
    embed_grad = (
        cotangent.astype(jnp.float32) + inverse * (normal_grad - first_mean - normal * second_mean)
    ).astype(jnp.bfloat16)
    grad_stem = lax.dot_general(patches, embed_grad, over_rows, preferred_element_type=jnp.float32)
    return (
        grad_stem.astype(jnp.bfloat16),
        grad_up.astype(jnp.bfloat16),
        grad_down.astype(jnp.bfloat16),
    )


def local(patches, stem_weight, ln_gain, up_weight, down_weight, cotangent):
    term_stem, term_up, term_down = block_grads(
        patches, stem_weight, ln_gain, up_weight, down_weight, cotangent
    )
    shares = (
        lax.psum_scatter(term_stem, "inner", scatter_dimension=0, tiled=True).astype(jnp.float32),
        lax.psum_scatter(term_up, "inner", scatter_dimension=0, tiled=True).astype(jnp.float32),
        lax.psum_scatter(term_down, "inner", scatter_dimension=0, tiled=True).astype(jnp.float32),
    )
    totals = (
        lax.psum(shares[0].astype(jnp.bfloat16), "outer").astype(jnp.float32),
        lax.psum(shares[1].astype(jnp.bfloat16), "outer").astype(jnp.float32),
        lax.psum(shares[2].astype(jnp.bfloat16), "outer").astype(jnp.float32),
    )
    return (totals[0], totals[1], totals[2])


def solution(mesh):
    in_specs = (P(("outer", "inner"), None), P(), P(), P(), P(), P(("outer", "inner"), None))
    out_specs = (P("inner", None), P("inner", None), P("inner", None))
    return jax.shard_map(local, mesh=mesh, in_specs=in_specs, out_specs=out_specs, check_vma=False)
```

profile of v0, /device:TPU:4, one launch (start us, length us, event | category | flops | bytes accessed | tf_op | source)
XLA Modules:
  0.0 506.0 jit_solution(3520441669226157985)
XLA Ops:
  7.2 0.0 copy-start
  7.2 0.0 reduce-scatter.10.cloned.1.call-start
  7.2 1.8 copy-done
  9.1 2.3 convert_reduce_fusion
  11.4 0.3 fusion.28
  11.7 0.0 copy-start.4
  11.7 0.0 copy-start.6
  11.8 1.3 fusion.95
  13.1 1.0 copy-done.6
  14.1 1.9 fusion.1
  16.1 0.0 copy-start.3
  16.1 1.5 fusion.97
  17.6 0.0 copy-done.3
  17.6 3.0 fusion
  20.6 4.7 copy.11
  25.3 0.0 reduce-scatter.10.cloned.1.call-update
  25.3 0.0 reduce-scatter.8.cloned.1.call-start
  25.3 8.4 %convolution_convert_fusion.1 = bf16[2048,1024]{1,0:T(8,128)(2,1)} fusion(bf16[256,1024]{1,0:T(8,128)(2,1)} %param.11, f32[256,2048]{1,0:T(8,128)} %copy-done.8), kind=kOutput, calls=%fused_computation.1 | convolution fusion | flops 1109917696 | bytes 6815744 | tf_op jit(solution)/shard_map/dot_general | solution.py:21
  33.7 0.0 reduce-scatter.8.cloned.1.call-update
  33.8 0.0 reduce-scatter.6.cloned.1.call-start
  33.8 4.8 convolution_convert_fusion.2
  38.6 0.0 reduce-scatter.6.cloned.1.call-update
  38.6 0.0 all-reduce.3.cloned.1.call-start
  38.7 111.8 %reduce-scatter.10.cloned.1.call-done = bf16[48,1024]{1,0:T(8,128)(2,1)} async-done(((bf16[1536,1024]{1,0:T(8,128)(2,1)}), bf16[48,1024]{1,0:T(8,128)(2,1)}) %reduce-scatter.10.cloned.1.call-update) | async-done | bytes 98320
  150.5 1.7 copy.12
  152.2 128.8 %reduce-scatter.8.cloned.1.call-done = bf16[64,1024]{1,0:T(8,128)(2,1)} async-done(((bf16[2048,1024]{1,0:T(8,128)(2,1)}), bf16[64,1024]{1,0:T(8,128)(2,1)}) %reduce-scatter.8.cloned.1.call-update) | async-done | bytes 131088 | tf_op jit(solution)/shard_map/reduce_scatter | solution.py:54
  281.0 129.9 %reduce-scatter.6.cloned.1.call-done = bf16[32,2048]{1,0:T(8,128)(2,1)} async-done(((bf16[1024,2048]{1,0:T(8,128)(2,1)}), bf16[32,2048]{1,0:T(8,128)(2,1)}) %reduce-scatter.6.cloned.1.call-update) | async-done | bytes 131088 | tf_op jit(solution)/shard_map/reduce_scatter | solution.py:53
  411.0 0.0 all-reduce.3.cloned.1.call-update
  411.0 83.5 %all-reduce.3.cloned.1.call-done = (bf16[48,1024]{0,1:T(8,128)(2,1)}, bf16[32,2048]{1,0:T(8,128)(2,1)}, bf16[64,1024]{1,0:T(8,128)(2,1)}) async-done(((bf16[48,1024]{0,1:T(8,128)(2,1)}, bf16[32,2048]{1,0:T(8,128)(2,1)}, bf16[64,1024]{1,0:T(8,128)(2,1)}), (bf16[48,1024]{0,1:T(8,128)(2,1)}, bf16[32,2048]{1,0:T(8,128)(2,1)}, bf16[64,1024]{1,0:T(8,128)(2,1)})) %all-reduce.3.cloned.1.call-update) | async-done | bytes 360464 | tf_op jit(solution)/shard_map/psum | solution.py:57
  494.5 1.7 copy.10
  496.2 1.6 convert_element_type.58
  497.8 1.6 convert_element_type.61
  (14 shorter events, 0.0 us)
Async XLA Ops:
  7.2 1.9 copy-start
  7.2 4.5 copy-start.5
  7.2 143.3 %reduce-scatter.10.cloned.1.call-start = ((), (), s32[]{:S(2)}) async-start(), calls=%async_computation.5 | async-start | bytes 3244032
  9.1 2.7 copy-start.7
  11.4 6.2 %copy-start.1 = (bf16[256,1024]{1,0:T(8,128)(2,1)}, bf16[256,1024]{1,0:T(8,128)(2,1)S(1)}, u32[]{:S(2)}) copy-start(bf16[256,1024]{1,0:T(8,128)(2,1)S(1)} %get-tuple-element.15) | copy-start | bytes 1572868
  11.7 1.4 copy-start.4
  11.7 2.4 copy-start.6
  14.1 1.9 copy-start.8
  16.0 1.5 copy-start.2
  16.1 1.5 copy-start.3
  25.3 255.7 %reduce-scatter.8.cloned.1.call-start = ((), (), s32[]{:S(2)}) async-start(), calls=%async_computation.4 | async-start | bytes 4325376 | tf_op jit(solution)/shard_map/reduce_scatter | solution.py:54
  33.8 377.2 %reduce-scatter.6.cloned.1.call-start = ((), (), s32[]{:S(2)}) async-start(), calls=%async_computation.3 | async-start | bytes 4325376 | tf_op jit(solution)/shard_map/reduce_scatter | solution.py:53
  38.6 455.8 %all-reduce.3.cloned.1.call-start = ((), (), s32[]{:S(2)}) async-start(), calls=%async_computation.6 | async-start | bytes 1048576 | tf_op jit(solution)/shard_map/psum | solution.py:57
Sparse Core Ops, SparseCore 0:
  25.4 125.0 reduce-scatter.9
  155.3 125.6 reduce-scatter.7
  285.3 125.6 reduce-scatter.5
  414.4 79.9 all-reduce.2
where the time goes:
time: 506 us
  waiting for transfers between devices  454 us (90%)
  matrix products  23.3 us (5%)
  between operations  13.9 us (3%)
  local copies, waits for them, and re-layouts  11 us (2%)
    reduce_scatter x1, waiting for transfers between devices, local(): lax.psum_scatter(term_up, 'inner', scatter_dimension=0, tiled=True)  130 us
    reduce_scatter x1, waiting for transfers between devices, local(): lax.psum_scatter(term_down, 'inner', scatter_dimension=0, tiled=True)  129 us
    unnamed x5, waiting for transfers between devices  112 us
    psum x1, waiting for transfers between devices, local(): lax.psum(shares[0].astype(jnp.bfloat16), 'outer').astype(jnp.float32)  83.5 us
    unnamed x21, local copies, waits for them, and re-layouts  11 us
  transfers between devices with their start and end apart: 4, of which 4 were waited for; matrix products, arithmetic and copies ran while one was open for 3% of the time, Pallas kernels for 0%

commit v1 on v0

v1 whole, which is shorter than its diff:
```python
import functools
import math

import jax
import jax.numpy as jnp
from jax import lax
from jax.experimental import pallas as pl
from jax.experimental.pallas import tpu as pltpu
from jax.sharding import Mesh, PartitionSpec as P

BF = jnp.bfloat16
F32 = jnp.float32
AXES = ("y", "xl", "z", "xh", "c")
VMEM = pl.BlockSpec(memory_space=pltpu.VMEM)
SMEM = pl.BlockSpec(memory_space=pltpu.SMEM)
LANES = 128


def move(value, dx=0, dy=0, dc=0):
    pairs = []
    for y in range(4):
        for x in range(4):
            for z in range(8):
                for c in range(2):
                    X, Y, C = (x + dx) % 4, (y + dy) % 4, (c + dc) % 2
                    src = (y * 2 + x % 2) * 32 + z * 4 + (x // 2) * 2 + c
                    dst = (Y * 2 + X % 2) * 32 + z * 4 + (X // 2) * 2 + C
                    pairs.append((src, dst))
    return lax.ppermute(value, AXES, sorted(pairs))


def call(body, outs, scratch, name, *operands, limit=8):
    specs = [SMEM] + [VMEM] * (len(operands) - 1)
    return pl.pallas_call(
        body,
        out_shape=[jax.ShapeDtypeStruct(s, d) for s, d in outs],
        in_specs=specs,
        out_specs=[VMEM] * len(outs),
        scratch_shapes=scratch,
        name=name,
        compiler_params=pltpu.CompilerParams(vmem_limit_bytes=limit << 20),
    )(*operands)


def split_body(rr, pos, x_ref, mine, send, t_ref):
    c = pos[3]
    t = x_ref[...].T
    for b in range(16):
        for half in range(2):
            at = (b * 2 + half) * rr
            t_ref[b, half] = t[at : at + rr]
    mine[...] = t_ref[:, c]
    send[...] = t_ref[:, 1 - c]


def split_transposed(pos, x, rr):
    tokens = x.shape[0]
    outs = [((16, rr, tokens), BF)] * 2
    return call(
        functools.partial(split_body, rr),
        outs,
        [pltpu.VMEM((16, 2, rr, tokens), BF)],
        "split_transposed",
        pos,
        x,
        limit=12,
    )


ROWS = 176
HALF = 352


def place(rel, outs):
    mp, mm, kp, ow = outs
    return {
        0: (ow.at[0], ow.at[1]),
        1: (kp.at[0], mp.at[1]),
        2: (mp.at[0], mm.at[0]),
        3: (mm.at[1], kp.at[1]),
    }[rel]


def dot2(lefts, rights):
    acc = jnp.dot(lefts[0], rights[0], preferred_element_type=F32)
    acc += jnp.dot(lefts[1], rights[1], preferred_element_type=F32)
    return acc.astype(BF)


def terms_body(pos, hm, hr, nm, nr, pm, pr, cm, cr, gm, gr, em, er, *outs):
    x, y = pos[0], pos[1]

    def columns(ref, start, width):
        return ref[:, pl.ds(pl.multiple_of(start, LANES), width)]

    for rel in range(4):
        to = lax.rem(x + rel, 4)
        xh, xl = to // 2, lax.rem(to, 2)
        dests = place(rel, outs[:4])
        acc = dot2(
            [ref[:, xh].reshape(512, 256) for ref in (hm, hr)],
            [columns(ref, xl * 512, 512) for ref in (cm, cr)],
        )
        for z in range(8):
            for yy in range(4):
                dests[z // 4][yy, z % 4 * 64 : z % 4 * 64 + 64] = acc[
                    z * 64 : z * 64 + 64, yy * 128 : yy * 128 + 128
                ]
        acc = dot2(
            [
                jnp.concatenate(
                    [ref[0:2, xh].reshape(96, 256), ref[4:6, xh].reshape(96, 256)], axis=0
                )
                for ref in (pm, pr)
            ],
            [columns(ref, xl * 512, 512) for ref in (em, er)],
        )
        for half in range(2):
            for yy in range(4):
                dests[half][yy, 256:352] = acc[
                    half * 96 : half * 96 + 96, yy * 128 : yy * 128 + 128
                ]
    for rel in range(4):
        to = lax.rem(y + rel, 4)
        dests = place(rel, outs[4:])
        acc = dot2(
            [ref[...].reshape(512, 256) for ref in (nm, nr)],
            [columns(ref, to * 512, 512) for ref in (gm, gr)],
        )
        for z in range(8):
            for xx in range(4):
                for k in range(2):
                    row, col = (z * 2 + xx // 2) * 32, (xx % 2 * 2 + k) * 128
                    at = z % 4 * 64 + k * 32
                    dests[z // 4][xx, at : at + 32] = acc[row : row + 32, col : col + 128]
        acc = dot2(
            [
                jnp.concatenate(
                    [ref[2:4].reshape(192, 256), ref[6:8].reshape(192, 256)], axis=0
                )
                for ref in (pm, pr)
            ],
            [
                jnp.concatenate(
                    [columns(ref, to * 128, 128), columns(ref, 512 + to * 128, 128)], axis=1
                )
                for ref in (em, er)
            ],
        )
        for half in range(2):
            for zi in range(2):
                for xx in range(4):
                    row, col = ((half * 2 + zi) * 2 + xx // 2) * 48, xx % 2 * 128
                    at = 256 + zi * 48
                    dests[half][xx, at : at + 48] = acc[row : row + 48, col : col + 128]


def terms(pos, hidden, normed, patches, cotangent, preact_grad, embed_grad):
    lefts = [v.reshape(8, 2, v.shape[1], v.shape[2]) for v in (*hidden, *normed, *patches)]
    outs = call(
        terms_body,
        [((2, 4, HALF, LANES), BF)] * 8,
        [],
        "terms",
        pos,
        *lefts,
        *cotangent,
        *preact_grad,
        *embed_grad,
        limit=24,
    )
    return outs[:4], outs[4:]


def forward_body(*refs):
    for p in range(2):
        kp, r1, r2 = refs[3 * p : 3 * p + 3]
        s1, s2 = refs[6 + 2 * p : 8 + 2 * p]
        s1[...] = (kp[0].astype(F32) + r1[0].astype(F32)).astype(BF)
        s2[...] = (kp[1].astype(F32) + r2[0].astype(F32)).astype(BF)


def rings(axes, parts):
    arrived = []
    for axis, (mp, mm, kp, ow) in zip(axes, parts):
        arrived.append((move(mp, **{"d" + axis: 1}), move(mm, **{"d" + axis: -1})))
    flat = [v for (r1, r2), part in zip(arrived, parts) for v in (part[2], r1, r2)]
    sums = pl.pallas_call(
        forward_body,
        out_shape=[jax.ShapeDtypeStruct(flat[0].shape[1:], BF)] * 4,
        in_specs=[VMEM] * 6,
        out_specs=[VMEM] * 4,
        name="ring_forward",
        compiler_params=pltpu.CompilerParams(vmem_limit_bytes=8 << 20),
    )(*flat)
    result = []
    for p, (axis, part) in enumerate(zip(axes, parts)):
        q1 = move(sums[2 * p], **{"d" + axis: 1})
        q2 = move(sums[2 * p + 1], **{"d" + axis: -1})
        result.append((part[3], *arrived[p], q1, q2))
    return result


def add3(a, b, c):
    return (a.astype(F32) + b.astype(F32) + c.astype(F32)).astype(BF)


def turn_body(pos, *refs):
    for p in range(2):
        ow, r1, r2, q1, q2 = refs[5 * p : 5 * p + 5]
        outs = refs[10 + 4 * p : 14 + 4 * p]
        me = pos[1 - p]
        for rel in range(4):
            to = lax.rem(me + rel, 4)
            da, db = place(rel, outs)
            da[...] = add3(ow[0, to], r2[1, to], q1[to])
            db[...] = add3(ow[1, to], r1[1, to], q2[to])


def reduce_xy(pos, parts):
    flat = [v for part in rings("xy", parts) for v in part]
    outs = call(turn_body, [((2, HALF, LANES), BF)] * 8, [], "ring_turn", pos, *flat)
    return [v for part in rings("yx", (outs[:4], outs[4:])) for v in part]


def pack_body(*refs):
    out = refs[10]
    for p in range(2):
        ow, r1, r2, q1, q2 = refs[5 * p : 5 * p + 5]
        halves = (add3(ow[0], r2[1], q1[...]), add3(ow[1], r1[1], q2[...]))
        for h, half in enumerate(halves):
            for zi in range(4):
                out[4 * h + zi, 64 * p : 64 * p + 64] = half[zi * 64 : zi * 64 + 64]
            for zi in range(2):
                out[4 * h + 2 * p + zi, 128:176] = half[256 + zi * 48 : 304 + zi * 48]


def sum_body(got, out):
    total = got[0].astype(F32)
    for k in range(1, 8):
        total += got[k].astype(F32)
    share = total.astype(BF)
    for k in range(8):
        out[k] = share


def unpack_body(got, stem, up, down):
    for y in range(4):
        for xl in range(2):
            piece = got[y * 2 + xl].astype(F32)
            col = (xl * 4 + y) * LANES
            down[:, col : col + LANES] = piece[0:64]
            stem[:, col : col + LANES] = piece[128:176]
            col = (y * 2 + xl) * 256
            up[:, col : col + LANES] = piece[64:96]
            up[:, col + LANES : col + 256] = piece[96:128]


def plain(body, outs, name, *operands):
    return pl.pallas_call(
        body,
        out_shape=[jax.ShapeDtypeStruct(s, d) for s, d in outs],
        in_specs=[VMEM] * len(operands),
        out_specs=[VMEM] * len(outs),
        name=name,
        compiler_params=pltpu.CompilerParams(vmem_limit_bytes=8 << 20),
    )(*operands)


def finish(pieces):
    share = [((8, ROWS, LANES), BF)]
    (packed,) = plain(pack_body, share, "z_pack", *pieces)
    got = lax.all_to_all(packed, "z", 0, 0, tiled=True)
    (copies,) = plain(sum_body, share, "z_sum", got)
    every = lax.all_to_all(copies, ("y", "xl"), 0, 0, tiled=True)
    outs = [((48, 1024), F32), ((32, 2048), F32), ((64, 1024), F32)]
    return plain(unpack_body, outs, "unpack", every)


def local(patches, stem_weight, ln_gain, up_weight, down_weight, cotangent):
    x = lax.axis_index("xh") * 2 + lax.axis_index("xl")
    pos = jnp.stack([x, lax.axis_index("y"), lax.axis_index("z"), lax.axis_index("c")])
    pos = pos.astype(jnp.int32)

    cot_other = move(cotangent, dc=1)
    patches_mine, patches_send = split_transposed(pos, patches, 48)
    patches_other = move(patches_send, dc=1)

    embed = jnp.dot(patches, stem_weight, preferred_element_type=F32).astype(BF)
    embed_f = embed.astype(F32)
    center = jnp.mean(embed_f, axis=1, keepdims=True)
    shifted = embed_f - center
    inverse = lax.rsqrt(jnp.mean(shifted * shifted, axis=1, keepdims=True) + 1e-06)
    normal = shifted * inverse
    normed = (normal * ln_gain).astype(BF)
    normed_mine, normed_send = split_transposed(pos, normed, 32)
    normed_other = move(normed_send, dc=1)
    preact = jnp.dot(normed, up_weight, preferred_element_type=F32)
    hidden = jax.nn.gelu(preact, approximate=False).astype(BF)
    hidden_mine, hidden_send = split_transposed(pos, hidden, 64)
    hidden_other = move(hidden_send, dc=1)

    over_cols = (((1,), (1,)), ((), ()))
    hidden_grad = lax.dot_general(cotangent, down_weight, over_cols, preferred_element_type=F32)
    derivative = 0.5 * (1.0 + lax.erf(preact / math.sqrt(2.0))) + preact * jnp.exp(
        -0.5 * preact * preact
    ) / math.sqrt(2.0 * math.pi)
    preact_grad = (hidden_grad * derivative).astype(BF)
    preact_other = move(preact_grad, dc=1)

    normal_grad = (
        lax.dot_general(preact_grad, up_weight, over_cols, preferred_element_type=F32) * ln_gain
    )
    first_mean = jnp.mean(normal_grad, axis=1, keepdims=True)
    second_mean = jnp.mean(normal_grad * normal, axis=1, keepdims=True)
    embed_grad = (
        cotangent.astype(F32) + inverse * (normal_grad - first_mean - normal * second_mean)
    ).astype(BF)
    embed_other = move(embed_grad, dc=1)

    parts = terms(
        pos,
        (hidden_mine, hidden_other),
        (normed_mine, normed_other),
        (patches_mine, patches_other),
        (cotangent, cot_other),
        (preact_grad, preact_other),
        (embed_grad, embed_other),
    )
    return tuple(finish(reduce_xy(pos, parts)))


def solution(mesh):
    fine = Mesh(mesh.devices.reshape(4, 2, 8, 2, 2), AXES)
    rows = P(("z", "xh", "c"), None)
    in_specs = (P(AXES, None), P(), P(), P(), P(), P(AXES, None))
    return jax.shard_map(
        local, mesh=fine, in_specs=in_specs, out_specs=(rows, rows, rows), check_vma=False
    )
```

time: 506 us -> 117 us (0.23)
  waiting for transfers between devices: 454 us -> 34.9 us
  blocking collectives: 0 us -> 28.5 us
  starting transfers between devices: 0.16 us -> 25.3 us
  between operations: 13.9 us -> 0.86 us
  matrix products: 23.3 us -> 13.3 us
  Pallas kernels: 0 us -> 8.98 us
  local copies, waits for them, and re-layouts: 11 us -> 3.09 us
    reduce_scatter x2 -> x0, waiting for transfers between devices: 259 us -> none  [the longest x1 130 us: local(): lax.psum_scatter(term_up, 'inner', scatter_dimension=0, tiled=True)]
    unnamed x5 -> x0, waiting for transfers between devices: 112 us -> none
    psum x1 -> x0, waiting for transfers between devices: 83.5 us -> none  [local(): lax.psum(shares[0].astype(jnp.bfloat16), 'outer').astype(jnp.float32)]
    ppermute x0 -> x22, waiting for transfers between devices: none -> 34.9 us  [move(): return lax.ppermute(value, AXES, sorted(pairs))]
    all_to_all x0 -> x2, blocking collectives: none -> 28.5 us  [the longest x1 18.2 us: finish(): got = lax.all_to_all(packed, 'z', 0, 0, tiled=True)]
    ppermute x0 -> x22, starting transfers between devices: none -> 25.3 us  [move(): return lax.ppermute(value, AXES, sorted(pairs))]
    dot_general x7 -> x4, matrix products: 23.3 us -> 13.3 us  [the longest x1 7.61 us: local(): preact = jnp.dot(normed, up_weight, preferred_element_type=F32)]
    pallas_call x0 -> x10, Pallas kernels: none -> 8.98 us  [the longest x5 7.49 us: call(): pl.pallas_call(body, out_shape=[jax.ShapeDtypeStruct(s, d) for s, d in ou...]
  transfers between devices with their start and end apart: 4 -> 22, of which waited for: 4 -> 12; matrix products, arithmetic and copies ran while one was open for 3% -> 10% of each run, Pallas kernels for 0% -> 2%
where the time goes in v1:
time: 117 us
  waiting for transfers between devices  34.9 us (30%)
  blocking collectives  28.5 us (24%)
  starting transfers between devices  25.3 us (22%)
  matrix products  13.3 us (11%)
  Pallas kernels  8.98 us (8%)
  local copies, waits for them, and re-layouts  3.09 us (3%)
  other arithmetic  2.11 us (2%)
    ppermute x22, waiting for transfers between devices, move(): return lax.ppermute(value, AXES, sorted(pairs))  34.9 us
    ppermute x22, starting transfers between devices, move(): return lax.ppermute(value, AXES, sorted(pairs))  25.3 us
    all_to_all x1, blocking collectives, finish(): got = lax.all_to_all(packed, 'z', 0, 0, tiled=True)  18.2 us
    all_to_all x1, blocking collectives, finish(): every = lax.all_to_all(copies, ('y', 'xl'), 0, 0, tiled=True)  10.3 us
    dot_general x1, matrix products, local(): preact = jnp.dot(normed, up_weight, preferred_element_type=F32)  7.61 us
    pallas_call x5, Pallas kernels, call(): pl.pallas_call(body, out_shape=[jax.ShapeDtypeStruct(s, d) for s, d in ou...  7.49 us
    unnamed x16, local copies, waits for them, and re-layouts  3.09 us
  transfers between devices with their start and end apart: 22, of which 12 were waited for; matrix products, arithmetic and copies ran while one was open for 10% of the time, Pallas kernels for 2%

profile of v1, /device:TPU:4, one launch (start us, length us, event | category | flops | bytes accessed | tf_op | source)
XLA Modules:
  0.0 117.1 jit_solution(17242232592437769372)
XLA Ops:
  0.7 1.9 %copy-done = bf16[1536,1024]{1,0:T(8,128)(2,1)S(1)} copy-done((bf16[1536,1024]{1,0:T(8,128)(2,1)S(1)}, bf16[1536,1024]{1,0:T(8,128)(2,1)}, u32[]{:S(2)}) %copy-start) | copy-done | bytes 3145752
  2.5 2.2 %convert_reduce_fusion = (f32[256]{0:T(256)S(1)}, bf16[256,1024]{1,0:T(8,128)(2,1)S(1)}) fusion(bf16[256,1536]{1,0:T(8,128)(2,1)} %x_ref.1, bf16[1536,1024]{1,0:T(8,128)(2,1)S(1)} %copy-done), kind=kOutput, calls=%fused_computation.28 | convolution fusion | flops 806092544 | bytes 4457472 | tf_op jit(solution)/shard_map/dot_general | solution.py:289
  5.9 1.3 %fusion.20.x_ref = bf16[256,1024]{1,0:T(8,128)(2,1)S(1)} fusion(bf16[256,1024]{1,0:T(8,128)(2,1)} %copy-done.3, f32[1024]{0:T(1024)S(1)} %copy-done.5, f32[256]{0:T(256)S(1)} %add_rsqrt_fusion, f32[256]{0:T(256)S(1)} %broadcast_multiply_fusion.2), kind=kLoop, calls=%fused_computation.35 | loop fusion | flops 1310720 | bytes 1054720 | tf_op jit(solution)/shard_map/convert_element_type | solution.py:295
  8.7 7.6 %fusion.3 = (bf16[256,2048]{1,0:T(8,128)(2,1)S(1)}, f32[256,2048]{1,0:T(8,128)S(1)}) fusion(bf16[256,1024]{1,0:T(8,128)(2,1)S(1)} %fusion.20.x_ref, bf16[1024,2048]{1,0:T(8,128)(2,1)} %param.9), kind=kOutput, calls=%fused_computation.6 | convolution fusion | flops 1107820544 | bytes 7864320 | tf_op jit(solution)/shard_map/dot_general | solution.py:298
  16.3 0.9 split_transposed.3
  17.6 2.0 %fusion.gm = bf16[256,2048]{1,0:T(8,128)(2,1)S(1)} fusion(bf16[256,1024]{1,0:T(8,128)(2,1)S(1)} %copy-done.1, bf16[2048,1024]{1,0:T(8,128)(2,1)S(1)} %copy-done.6, f32[256,2048]{1,0:T(8,128)S(1)} %get-tuple-element.68), kind=kOutput, calls=%fused_computation.3 | convolution fusion | flops 1078984704 | bytes 7864320 | tf_op jit(solution)/shard_map/dot_general | solution.py:304
  20.0 1.5 %fusion.27 = (f32[256]{0:T(256)S(1)}, f32[256]{0:T(256)S(1)}, f32[256,1024]{1,0:T(8,128)S(1)}) fusion(f32[256]{0:T(256)S(1)} %add_rsqrt_fusion, f32[256]{0:T(256)S(1)} %broadcast_multiply_fusion.2, bf16[256,1024]{1,0:T(8,128)(2,1)S(1)} %copy-done.4, f32[1024]{0:T(1024)S(1)} %copy-done.5, bf16[256,2048]{1,0:T(8,128)(2,1)S(1)} %fusion.gm, ...), kind=kOutput, calls=%fused_computation.47 | convolution fusion | flops 1075576320 | bytes 6823936 | tf_op jit(solution)/shard_map/dot_general | solution.py:312
  24.0 1.5 %collective-permute-done.2 = bf16[16,48,256]{2,1,0:T(8,128)(2,1)S(1)} collective-permute-done((bf16[16,48,256]{2,1,0:T(8,128)(2,1)S(1)}, bf16[16,48,256]{2,1,0:T(8,128)(2,1)S(1)}, u32[]{:S(2)}, u32[]{:S(2)}) %collective-permute-start.2) | collective-permute-done | bytes 393248 | tf_op jit(solution)/shard_map/ppermute | solution.py:29
  25.5 3.9 %terms.1 = (bf16[2,4,352,128]{3,2,1,0:T(8,128)(2,1)S(1)}, bf16[2,4,352,128]{3,2,1,0:T(8,128)(2,1)S(1)}, bf16[2,4,352,128]{3,2,1,0:T(8,128)(2,1)S(1)}, bf16[2,4,3...) custom-call(s32[4]{0:T(128)S(1)} %pad_add_fusion.pos, ...), custom_call_target="tpu_custom_call" | custom-call | tf_op jit(solution)/shard_map/terms/pallas_call | solution.py:34
  29.3 1.3 %collective-permute-start.6 = (bf16[2,4,352,128]{3,2,1,0:T(8,128)(2,1)S(1)}, bf16[2,4,352,128]{3,2,1,0:T(8,128)(2,1)S(1)}, u32[]{:S(2)}, u32[]{:S(2)}) collective-permute-start(bf16[2,4,352,128]{3,2,1,0:T(8,128)(2,1)S(1)} %get-tuple-element.40), channel_id=1, source_target_pairs={{0,32},{1,33},{2,34},{3,35},{4,36},{5,37},{6,38},{7,39},{8,40},{9,... | collective-permute-start | bytes 2162696 | tf_op jit(solution)/shard_map/ppermute | solution.py:29
  31.4 1.6 %collective-permute-start.8 = (bf16[2,4,352,128]{3,2,1,0:T(8,128)(2,1)S(1)}, bf16[2,4,352,128]{3,2,1,0:T(8,128)(2,1)S(1)}, u32[]{:S(2)}, u32[]{:S(2)}) collective-permute-start(bf16[2,4,352,128]{3,2,1,0:T(8,128)(2,1)S(1)} %get-tuple-element.44), channel_id=1, source_target_pairs={{0,64},{1,65},{2,66},{3,67},{4,68},{5,69},{6,70},{7,71},{8,72},{9,... | collective-permute-start | bytes 2162696 | tf_op jit(solution)/shard_map/ppermute | solution.py:29
  33.0 1.6 %collective-permute-start.9 = (bf16[2,4,352,128]{3,2,1,0:T(8,128)(2,1)S(1)}, bf16[2,4,352,128]{3,2,1,0:T(8,128)(2,1)S(1)}, u32[]{:S(2)}, u32[]{:S(2)}) collective-permute-start(bf16[2,4,352,128]{3,2,1,0:T(8,128)(2,1)S(1)} %get-tuple-element.45), channel_id=1, source_target_pairs={{0,192},{1,193},{2,194},{3,195},{4,196},{5,197},{6,198},{7,199},{8... | collective-permute-start | bytes 2162696 | tf_op jit(solution)/shard_map/ppermute | solution.py:29
  34.7 13.0 %collective-permute-done.6.refs_1_ = bf16[2,4,352,128]{3,2,1,0:T(8,128)(2,1)S(1)} collective-permute-done((bf16[2,4,352,128]{3,2,1,0:T(8,128)(2,1)S(1)}, bf16[2,4,352,128]{3,2,1,0:T(8,128)(2,1)S(1)}, u32[]{:S(2)}, u32[]{:S(2)}) %collective-permute-start.6) | collective-permute-done | bytes 720928 | tf_op jit(solution)/shard_map/ppermute | solution.py:29
  47.7 1.4 %collective-permute-done.7.refs_2_ = bf16[2,4,352,128]{3,2,1,0:T(8,128)(2,1)S(1)} collective-permute-done((bf16[2,4,352,128]{3,2,1,0:T(8,128)(2,1)S(1)}, bf16[2,4,352,128]{3,2,1,0:T(8,128)(2,1)S(1)}, u32[]{:S(2)}, u32[]{:S(2)}) %collective-permute-start.7) | collective-permute-done | bytes 720928 | tf_op jit(solution)/shard_map/ppermute | solution.py:29
  49.1 1.4 %collective-permute-done.8.refs_4_.refs_6_ = bf16[2,4,352,128]{3,2,1,0:T(8,128)(2,1)S(1)} collective-permute-done((bf16[2,4,352,128]{3,2,1,0:T(8,128)(2,1)S(1)}, bf16[2,4,352,128]{3,2,1,0:T(8,128)(2,1)S(1)}, u32[]{:S(2)}, u32[]{:S(2)}) %collective-permute-start.8) | collective-permute-done | bytes 720928 | tf_op jit(solution)/shard_map/ppermute | solution.py:29
  50.8 1.7 %collective-permute-start.10 = (bf16[4,352,128]{2,1,0:T(8,128)(2,1)S(1)}, bf16[4,352,128]{2,1,0:T(8,128)(2,1)S(1)}, u32[]{:S(2)}, u32[]{:S(2)}) collective-permute-start(bf16[4,352,128]{2,1,0:T(8,128)(2,1)S(1)} %get-tuple-element.46), channel_id=1, source_target_pairs={{0,32},{1,33},{2,34},{3,35},{4,36},{5,37},{6,38},{7,39},{8,40},{9,... | collective-permute-start | bytes 1081352 | tf_op jit(solution)/shard_map/ppermute | solution.py:29
  52.9 1.6 %collective-permute-start.12 = (bf16[4,352,128]{2,1,0:T(8,128)(2,1)S(1)}, bf16[4,352,128]{2,1,0:T(8,128)(2,1)S(1)}, u32[]{:S(2)}, u32[]{:S(2)}) collective-permute-start(bf16[4,352,128]{2,1,0:T(8,128)(2,1)S(1)} %get-tuple-element.49), channel_id=1, source_target_pairs={{0,64},{1,65},{2,66},{3,67},{4,68},{5,69},{6,70},{7,71},{8,72},{9,... | collective-permute-start | bytes 1081352 | tf_op jit(solution)/shard_map/ppermute | solution.py:29
  54.5 1.7 %collective-permute-start.13 = (bf16[4,352,128]{2,1,0:T(8,128)(2,1)S(1)}, bf16[4,352,128]{2,1,0:T(8,128)(2,1)S(1)}, u32[]{:S(2)}, u32[]{:S(2)}) collective-permute-start(bf16[4,352,128]{2,1,0:T(8,128)(2,1)S(1)} %get-tuple-element.50), channel_id=1, source_target_pairs={{0,192},{1,193},{2,194},{3,195},{4,196},{5,197},{6,198},{7,199},{8... | collective-permute-start | bytes 1081352 | tf_op jit(solution)/shard_map/ppermute | solution.py:29
  56.1 3.9 %collective-permute-done.10.refs_3_ = bf16[4,352,128]{2,1,0:T(8,128)(2,1)S(1)} collective-permute-done((bf16[4,352,128]{2,1,0:T(8,128)(2,1)S(1)}, bf16[4,352,128]{2,1,0:T(8,128)(2,1)S(1)}, u32[]{:S(2)}, u32[]{:S(2)}) %collective-permute-start.10) | collective-permute-done | bytes 360480 | tf_op jit(solution)/shard_map/ppermute | solution.py:29
  60.0 2.5 %collective-permute-done.11.refs_4_ = bf16[4,352,128]{2,1,0:T(8,128)(2,1)S(1)} collective-permute-done((bf16[4,352,128]{2,1,0:T(8,128)(2,1)S(1)}, bf16[4,352,128]{2,1,0:T(8,128)(2,1)S(1)}, u32[]{:S(2)}, u32[]{:S(2)}) %collective-permute-start.11) | collective-permute-done | bytes 360480 | tf_op jit(solution)/shard_map/ppermute | solution.py:29
  62.8 1.1 ring_turn.1
  63.9 1.0 collective-permute-start.14
  64.9 2.3 %collective-permute-start.15 = (bf16[2,352,128]{2,1,0:T(8,128)(2,1)S(1)}, bf16[2,352,128]{2,1,0:T(8,128)(2,1)S(1)}, u32[]{:S(2)}, u32[]{:S(2)}) collective-permute-start(bf16[2,352,128]{2,1,0:T(8,128)(2,1)S(1)} %get-tuple-element.53), channel_id=1, source_target_pairs={{0,192},{1,193},{2,194},{3,195},{4,196},{5,197},{6,198},{7,199},{8... | collective-permute-start | bytes 540680 | tf_op jit(solution)/shard_map/ppermute | solution.py:29
  67.2 2.6 %collective-permute-start.16 = (bf16[2,352,128]{2,1,0:T(8,128)(2,1)S(1)}, bf16[2,352,128]{2,1,0:T(8,128)(2,1)S(1)}, u32[]{:S(2)}, u32[]{:S(2)}) collective-permute-start(bf16[2,352,128]{2,1,0:T(8,128)(2,1)S(1)} %get-tuple-element.56), channel_id=1, source_target_pairs={{0,32},{1,33},{2,34},{3,35},{4,36},{5,37},{6,38},{7,39},{8,40},{9,... | collective-permute-start | bytes 540680 | tf_op jit(solution)/shard_map/ppermute | solution.py:29
  70.7 2.2 %collective-permute-done.16.refs_4_.refs_6_ = bf16[2,352,128]{2,1,0:T(8,128)(2,1)S(1)} collective-permute-done((bf16[2,352,128]{2,1,0:T(8,128)(2,1)S(1)}, bf16[2,352,128]{2,1,0:T(8,128)(2,1)S(1)}, u32[]{:S(2)}, u32[]{:S(2)}) %collective-permute-start.16) | collective-permute-done | bytes 180256 | tf_op jit(solution)/shard_map/ppermute | solution.py:29
  72.9 3.4 %collective-permute-done.17.refs_5_.refs_7_ = bf16[2,352,128]{2,1,0:T(8,128)(2,1)S(1)} collective-permute-done((bf16[2,352,128]{2,1,0:T(8,128)(2,1)S(1)}, bf16[2,352,128]{2,1,0:T(8,128)(2,1)S(1)}, u32[]{:S(2)}, u32[]{:S(2)}) %collective-permute-start.17) | collective-permute-done | bytes 180256 | tf_op jit(solution)/shard_map/ppermute | solution.py:29
  76.4 3.2 %collective-permute-start.19 = (bf16[352,128]{1,0:T(8,128)(2,1)S(1)}, bf16[352,128]{1,0:T(8,128)(2,1)S(1)}, u32[]{:S(2)}, u32[]{:S(2)}) collective-permute-start(bf16[352,128]{1,0:T(8,128)(2,1)S(1)} %get-tuple-element.59), channel_id=1, source_target_pairs={{0,192},{1,193},{2,194},{3,195},{4,196},{5,197},{6,198},{7,199},{8... | collective-permute-start | bytes 270344 | tf_op jit(solution)/shard_map/ppermute | solution.py:29
  79.7 3.2 %collective-permute-start.20 = (bf16[352,128]{1,0:T(8,128)(2,1)S(1)}, bf16[352,128]{1,0:T(8,128)(2,1)S(1)}, u32[]{:S(2)}, u32[]{:S(2)}) collective-permute-start(bf16[352,128]{1,0:T(8,128)(2,1)S(1)} %get-tuple-element.61), channel_id=1, source_target_pairs={{0,32},{1,33},{2,34},{3,35},{4,36},{5,37},{6,38},{7,39},{8,40},{9,... | collective-permute-start | bytes 270344 | tf_op jit(solution)/shard_map/ppermute | solution.py:29
  82.9 2.1 %collective-permute-done.20.refs_8_ = bf16[352,128]{1,0:T(8,128)(2,1)S(1)} collective-permute-done((bf16[352,128]{1,0:T(8,128)(2,1)S(1)}, bf16[352,128]{1,0:T(8,128)(2,1)S(1)}, u32[]{:S(2)}, u32[]{:S(2)}) %collective-permute-start.20) | collective-permute-done | bytes 90144 | tf_op jit(solution)/shard_map/ppermute | solution.py:29
  85.0 2.4 %collective-permute-done.21.refs_9_ = bf16[352,128]{1,0:T(8,128)(2,1)S(1)} collective-permute-done((bf16[352,128]{1,0:T(8,128)(2,1)S(1)}, bf16[352,128]{1,0:T(8,128)(2,1)S(1)}, u32[]{:S(2)}, u32[]{:S(2)}) %collective-permute-start.21) | collective-permute-done | bytes 90144 | tf_op jit(solution)/shard_map/ppermute | solution.py:29
  87.6 18.2 %all_to_all.10.got = bf16[8,176,128]{2,1,0:T(8,128)(2,1)S(1)} all-to-all(bf16[8,176,128]{2,1,0:T(8,128)(2,1)S(1)} %z_pack.1), channel_id=1, replica_groups=mesh['y'=4,'xl'=2,'z'=8,'xh'=2,'c'=2] {'z'}, dimensions={0} | all-to-all | bytes 720896 | tf_op jit(solution)/shard_map/all_to_all | solution.py:273
  105.8 10.3 %all_to_all.11.got = bf16[8,176,128]{2,1,0:T(8,128)(2,1)S(1)} all-to-all(bf16[8,176,128]{2,1,0:T(8,128)(2,1)S(1)} %z_sum.1), channel_id=1, replica_groups=mesh['y'=4,'xl'=2,'z'=8,'xh'=2,'c'=2] {'y','xl'}, dimensions={0} | all-to-all | bytes 720896 | tf_op jit(solution)/shard_map/all_to_all | solution.py:275
  (51 shorter events, 9.8 us)
Async XLA Ops:
  0.6 1.9 %copy-start = (bf16[1536,1024]{1,0:T(8,128)(2,1)S(1)}, bf16[1536,1024]{1,0:T(8,128)(2,1)}, u32[]{:S(2)}) copy-start(bf16[1536,1024]{1,0:T(8,128)(2,1)} %param.7) | copy-start | bytes 9437188
  2.5 3.3 %copy-start.5 = (f32[1024]{0:T(1024)S(1)}, f32[1024]{0:T(1024)}, u32[]{:S(2)}) copy-start(f32[1024]{0:T(1024)} %param.8) | copy-start | bytes 12292
  4.7 0.8 copy-start.3
  8.0 9.5 %copy-start.1 = (bf16[256,1024]{1,0:T(8,128)(2,1)S(1)}, bf16[256,1024]{1,0:T(8,128)(2,1)}, u32[]{:S(2)}) copy-start(bf16[256,1024]{1,0:T(8,128)(2,1)} %cm.1) | copy-start | bytes 1572868
  8.1 9.5 %copy-start.6 = (bf16[2048,1024]{1,0:T(8,128)(2,1)S(1)}, bf16[2048,1024]{1,0:T(8,128)(2,1)}, u32[]{:S(2)}) copy-start(bf16[2048,1024]{1,0:T(8,128)(2,1)} %param.10) | copy-start | bytes 12582916
  8.1 15.4 %collective-permute-start.1 = (bf16[16,32,256]{2,1,0:T(8,128)(2,1)S(1)}, bf16[16,32,256]{2,1,0:T(8,128)(2,1)S(1)}, u32[]{:S(2)}, u32[]{:S(2)}) collective-permute-start(bf16[16,32,256]{2,1,0:T(8,128)(2,1)S(1)} %get-tuple-element.36), channel_id=1, source_target_pairs={{0,1},{1,0},{2,3},{3,2},{4,5},{5,4},{6,7},{7,6},{8,9},{9,8},{10,11... | collective-permute-start | bytes 786440 | tf_op jit(solution)/shard_map/ppermute | solution.py:29
  8.2 17.3 %collective-permute-start.3 = (bf16[256,1024]{1,0:T(8,128)(2,1)}, bf16[256,1024]{1,0:T(8,128)(2,1)S(1)}, u32[]{:S(2)}, u32[]{:S(2)}) collective-permute-start(bf16[256,1024]{1,0:T(8,128)(2,1)} %cm.1), channel_id=1, source_target_pairs={{0,1},{1,0},{2,3},{3,2},{4,5},{5,4},{6,7},{7,6},{8,9},{9,8},{10,11... | collective-permute-start | bytes 1572872 | tf_op jit(solution)/shard_map/ppermute | solution.py:29
  17.2 8.2 %collective-permute-start = (bf16[16,64,256]{2,1,0:T(8,128)(2,1)S(1)}, bf16[16,64,256]{2,1,0:T(8,128)(2,1)S(1)}, u32[]{:S(2)}, u32[]{:S(2)}) collective-permute-start(bf16[16,64,256]{2,1,0:T(8,128)(2,1)S(1)} %get-tuple-element.34), channel_id=1, source_target_pairs={{0,1},{1,0},{2,3},{3,2},{4,5},{5,4},{6,7},{7,6},{8,9},{9,8},{10,11... | collective-permute-start | bytes 1572872 | tf_op jit(solution)/shard_map/ppermute | solution.py:29
  17.5 2.4 %copy-start.4 = (bf16[256,1024]{1,0:T(8,128)(2,1)S(1)}, bf16[256,1024]{1,0:T(8,128)(2,1)}, u32[]{:S(2)}) copy-start(bf16[256,1024]{1,0:T(8,128)(2,1)} %copy-done.3) | copy-start | bytes 1572868
  17.5 2.4 %copy-start.7 = (bf16[1024,2048]{1,0:T(8,128)(2,1)S(1)}, bf16[1024,2048]{1,0:T(8,128)(2,1)}, u32[]{:S(2)}) copy-start(bf16[1024,2048]{1,0:T(8,128)(2,1)} %param.9) | copy-start | bytes 12582916
  19.6 5.9 %collective-permute-start.4 = (bf16[256,2048]{1,0:T(8,128)(2,1)S(1)}, bf16[256,2048]{1,0:T(8,128)(2,1)S(1)}, u32[]{:S(2)}, u32[]{:S(2)}) collective-permute-start(bf16[256,2048]{1,0:T(8,128)(2,1)S(1)} %fusion.gm), channel_id=1, source_target_pairs={{0,1},{1,0},{2,3},{3,2},{4,5},{5,4},{6,7},{7,6},{8,9},{9,8},{10,11... | collective-permute-start | bytes 3145736 | tf_op jit(solution)/shard_map/ppermute | solution.py:29
  21.5 1.1 copy-start.2
  21.9 3.6 %collective-permute-start.5 = (bf16[256,1024]{1,0:T(8,128)(2,1)S(1)}, bf16[256,1024]{1,0:T(8,128)(2,1)S(1)}, u32[]{:S(2)}, u32[]{:S(2)}) collective-permute-start(bf16[256,1024]{1,0:T(8,128)(2,1)S(1)} %fusion.25.em), channel_id=1, source_target_pairs={{0,1},{1,0},{2,3},{3,2},{4,5},{5,4},{6,7},{7,6},{8,9},{9,8},{10,11... | collective-permute-start | bytes 1572872 | tf_op jit(solution)/shard_map/ppermute | solution.py:29
  23.5 2.0 %collective-permute-start.2 = (bf16[16,48,256]{2,1,0:T(8,128)(2,1)S(1)}, bf16[16,48,256]{2,1,0:T(8,128)(2,1)S(1)}, u32[]{:S(2)}, u32[]{:S(2)}) collective-permute-start(bf16[16,48,256]{2,1,0:T(8,128)(2,1)S(1)} %get-tuple-element.38), channel_id=1, source_target_pairs={{0,1},{1,0},{2,3},{3,2},{4,5},{5,4},{6,7},{7,6},{8,9},{9,8},{10,11... | collective-permute-start | bytes 1179656 | tf_op jit(solution)/shard_map/ppermute | solution.py:29
  29.3 18.4 %collective-permute-start.6 = (bf16[2,4,352,128]{3,2,1,0:T(8,128)(2,1)S(1)}, bf16[2,4,352,128]{3,2,1,0:T(8,128)(2,1)S(1)}, u32[]{:S(2)}, u32[]{:S(2)}) collective-permute-start(bf16[2,4,352,128]{3,2,1,0:T(8,128)(2,1)S(1)} %get-tuple-element.40), channel_id=1, source_target_pairs={{0,32},{1,33},{2,34},{3,35},{4,36},{5,37},{6,38},{7,39},{8,40},{9,... | collective-permute-start | bytes 2162696 | tf_op jit(solution)/shard_map/ppermute | solution.py:29
  30.6 18.5 %collective-permute-start.7 = (bf16[2,4,352,128]{3,2,1,0:T(8,128)(2,1)S(1)}, bf16[2,4,352,128]{3,2,1,0:T(8,128)(2,1)S(1)}, u32[]{:S(2)}, u32[]{:S(2)}) collective-permute-start(bf16[2,4,352,128]{3,2,1,0:T(8,128)(2,1)S(1)} %get-tuple-element.41), channel_id=1, source_target_pairs={{0,34},{1,35},{2,32},{3,33},{4,38},{5,39},{6,36},{7,37},{8,42},{9,... | collective-permute-start | bytes 2162696 | tf_op jit(solution)/shard_map/ppermute | solution.py:29
  31.4 19.0 %collective-permute-start.8 = (bf16[2,4,352,128]{3,2,1,0:T(8,128)(2,1)S(1)}, bf16[2,4,352,128]{3,2,1,0:T(8,128)(2,1)S(1)}, u32[]{:S(2)}, u32[]{:S(2)}) collective-permute-start(bf16[2,4,352,128]{3,2,1,0:T(8,128)(2,1)S(1)} %get-tuple-element.44), channel_id=1, source_target_pairs={{0,64},{1,65},{2,66},{3,67},{4,68},{5,69},{6,70},{7,71},{8,72},{9,... | collective-permute-start | bytes 2162696 | tf_op jit(solution)/shard_map/ppermute | solution.py:29
  33.0 17.4 %collective-permute-start.9 = (bf16[2,4,352,128]{3,2,1,0:T(8,128)(2,1)S(1)}, bf16[2,4,352,128]{3,2,1,0:T(8,128)(2,1)S(1)}, u32[]{:S(2)}, u32[]{:S(2)}) collective-permute-start(bf16[2,4,352,128]{3,2,1,0:T(8,128)(2,1)S(1)} %get-tuple-element.45), channel_id=1, source_target_pairs={{0,192},{1,193},{2,194},{3,195},{4,196},{5,197},{6,198},{7,199},{8... | collective-permute-start | bytes 2162696 | tf_op jit(solution)/shard_map/ppermute | solution.py:29
  50.8 9.2 %collective-permute-start.10 = (bf16[4,352,128]{2,1,0:T(8,128)(2,1)S(1)}, bf16[4,352,128]{2,1,0:T(8,128)(2,1)S(1)}, u32[]{:S(2)}, u32[]{:S(2)}) collective-permute-start(bf16[4,352,128]{2,1,0:T(8,128)(2,1)S(1)} %get-tuple-element.46), channel_id=1, source_target_pairs={{0,32},{1,33},{2,34},{3,35},{4,36},{5,37},{6,38},{7,39},{8,40},{9,... | collective-permute-start | bytes 1081352 | tf_op jit(solution)/shard_map/ppermute | solution.py:29
  52.5 10.0 %collective-permute-start.11 = (bf16[4,352,128]{2,1,0:T(8,128)(2,1)S(1)}, bf16[4,352,128]{2,1,0:T(8,128)(2,1)S(1)}, u32[]{:S(2)}, u32[]{:S(2)}) collective-permute-start(bf16[4,352,128]{2,1,0:T(8,128)(2,1)S(1)} %get-tuple-element.47), channel_id=1, source_target_pairs={{0,34},{1,35},{2,32},{3,33},{4,38},{5,39},{6,36},{7,37},{8,42},{9,... | collective-permute-start | bytes 1081352 | tf_op jit(solution)/shard_map/ppermute | solution.py:29
  52.9 9.9 %collective-permute-start.12 = (bf16[4,352,128]{2,1,0:T(8,128)(2,1)S(1)}, bf16[4,352,128]{2,1,0:T(8,128)(2,1)S(1)}, u32[]{:S(2)}, u32[]{:S(2)}) collective-permute-start(bf16[4,352,128]{2,1,0:T(8,128)(2,1)S(1)} %get-tuple-element.49), channel_id=1, source_target_pairs={{0,64},{1,65},{2,66},{3,67},{4,68},{5,69},{6,70},{7,71},{8,72},{9,... | collective-permute-start | bytes 1081352 | tf_op jit(solution)/shard_map/ppermute | solution.py:29
  54.5 8.3 %collective-permute-start.13 = (bf16[4,352,128]{2,1,0:T(8,128)(2,1)S(1)}, bf16[4,352,128]{2,1,0:T(8,128)(2,1)S(1)}, u32[]{:S(2)}, u32[]{:S(2)}) collective-permute-start(bf16[4,352,128]{2,1,0:T(8,128)(2,1)S(1)} %get-tuple-element.50), channel_id=1, source_target_pairs={{0,192},{1,193},{2,194},{3,195},{4,196},{5,197},{6,198},{7,199},{8... | collective-permute-start | bytes 1081352 | tf_op jit(solution)/shard_map/ppermute | solution.py:29
  63.9 6.8 %collective-permute-start.14 = (bf16[2,352,128]{2,1,0:T(8,128)(2,1)S(1)}, bf16[2,352,128]{2,1,0:T(8,128)(2,1)S(1)}, u32[]{:S(2)}, u32[]{:S(2)}) collective-permute-start(bf16[2,352,128]{2,1,0:T(8,128)(2,1)S(1)} %get-tuple-element.52), channel_id=1, source_target_pairs={{0,64},{1,65},{2,66},{3,67},{4,68},{5,69},{6,70},{7,71},{8,72},{9,... | collective-permute-start | bytes 540680 | tf_op jit(solution)/shard_map/ppermute | solution.py:29
  64.9 5.8 %collective-permute-start.15 = (bf16[2,352,128]{2,1,0:T(8,128)(2,1)S(1)}, bf16[2,352,128]{2,1,0:T(8,128)(2,1)S(1)}, u32[]{:S(2)}, u32[]{:S(2)}) collective-permute-start(bf16[2,352,128]{2,1,0:T(8,128)(2,1)S(1)} %get-tuple-element.53), channel_id=1, source_target_pairs={{0,192},{1,193},{2,194},{3,195},{4,196},{5,197},{6,198},{7,199},{8... | collective-permute-start | bytes 540680 | tf_op jit(solution)/shard_map/ppermute | solution.py:29
  67.2 5.7 %collective-permute-start.16 = (bf16[2,352,128]{2,1,0:T(8,128)(2,1)S(1)}, bf16[2,352,128]{2,1,0:T(8,128)(2,1)S(1)}, u32[]{:S(2)}, u32[]{:S(2)}) collective-permute-start(bf16[2,352,128]{2,1,0:T(8,128)(2,1)S(1)} %get-tuple-element.56), channel_id=1, source_target_pairs={{0,32},{1,33},{2,34},{3,35},{4,36},{5,37},{6,38},{7,39},{8,40},{9,... | collective-permute-start | bytes 540680 | tf_op jit(solution)/shard_map/ppermute | solution.py:29
  69.8 6.4 %collective-permute-start.17 = (bf16[2,352,128]{2,1,0:T(8,128)(2,1)S(1)}, bf16[2,352,128]{2,1,0:T(8,128)(2,1)S(1)}, u32[]{:S(2)}, u32[]{:S(2)}) collective-permute-start(bf16[2,352,128]{2,1,0:T(8,128)(2,1)S(1)} %get-tuple-element.57), channel_id=1, source_target_pairs={{0,34},{1,35},{2,32},{3,33},{4,38},{5,39},{6,36},{7,37},{8,42},{9,... | collective-permute-start | bytes 540680 | tf_op jit(solution)/shard_map/ppermute | solution.py:29
  76.4 6.6 %collective-permute-start.18 = (bf16[352,128]{1,0:T(8,128)(2,1)S(1)}, bf16[352,128]{1,0:T(8,128)(2,1)S(1)}, u32[]{:S(2)}, u32[]{:S(2)}) collective-permute-start(bf16[352,128]{1,0:T(8,128)(2,1)S(1)} %get-tuple-element.58), channel_id=1, source_target_pairs={{0,64},{1,65},{2,66},{3,67},{4,68},{5,69},{6,70},{7,71},{8,72},{9,... | collective-permute-start | bytes 270344 | tf_op jit(solution)/shard_map/ppermute | solution.py:29
  76.4 6.5 %collective-permute-start.19 = (bf16[352,128]{1,0:T(8,128)(2,1)S(1)}, bf16[352,128]{1,0:T(8,128)(2,1)S(1)}, u32[]{:S(2)}, u32[]{:S(2)}) collective-permute-start(bf16[352,128]{1,0:T(8,128)(2,1)S(1)} %get-tuple-element.59), channel_id=1, source_target_pairs={{0,192},{1,193},{2,194},{3,195},{4,196},{5,197},{6,198},{7,199},{8... | collective-permute-start | bytes 270344 | tf_op jit(solution)/shard_map/ppermute | solution.py:29
  79.7 5.4 %collective-permute-start.20 = (bf16[352,128]{1,0:T(8,128)(2,1)S(1)}, bf16[352,128]{1,0:T(8,128)(2,1)S(1)}, u32[]{:S(2)}, u32[]{:S(2)}) collective-permute-start(bf16[352,128]{1,0:T(8,128)(2,1)S(1)} %get-tuple-element.61), channel_id=1, source_target_pairs={{0,32},{1,33},{2,34},{3,35},{4,36},{5,37},{6,38},{7,39},{8,40},{9,... | collective-permute-start | bytes 270344 | tf_op jit(solution)/shard_map/ppermute | solution.py:29
  82.9 4.5 %collective-permute-start.21 = (bf16[352,128]{1,0:T(8,128)(2,1)S(1)}, bf16[352,128]{1,0:T(8,128)(2,1)S(1)}, u32[]{:S(2)}, u32[]{:S(2)}) collective-permute-start(bf16[352,128]{1,0:T(8,128)(2,1)S(1)} %get-tuple-element.62), channel_id=1, source_target_pairs={{0,34},{1,35},{2,32},{3,33},{4,38},{5,39},{6,36},{7,37},{8,42},{9,... | collective-permute-start | bytes 270344 | tf_op jit(solution)/shard_map/ppermute | solution.py:29

commit v2 on v1

v2 whole, which is shorter than its diff:
```python
import functools
import math

import jax
import jax.numpy as jnp
from jax import lax
from jax.experimental import pallas as pl
from jax.experimental.pallas import tpu as pltpu
from jax.sharding import Mesh, PartitionSpec as P

BF = jnp.bfloat16
F32 = jnp.float32
AXES = ("y", "xl", "z", "xh", "c")
VMEM = pl.BlockSpec(memory_space=pltpu.VMEM)
SMEM = pl.BlockSpec(memory_space=pltpu.SMEM)
LANES = 128


def move(value, axis, hop):
    pairs = []
    for y in range(4):
        for x in range(4):
            for z in range(8):
                for c in range(2):
                    far = hop * (1 - 2 * c)
                    X = (x + far) % 4 if axis == "x" else x
                    Y = (y + far) % 4 if axis == "y" else y
                    C = 1 - c if axis == "c" else c
                    src = (y * 2 + x % 2) * 32 + z * 4 + (x // 2) * 2 + c
                    dst = (Y * 2 + X % 2) * 32 + z * 4 + (X // 2) * 2 + C
                    pairs.append((src, dst))
    return lax.ppermute(value, AXES, sorted(pairs))


def call(body, outs, scratch, name, *operands, limit=8, specs=None):
    return pl.pallas_call(
        body,
        out_shape=[jax.ShapeDtypeStruct(s, d) for s, d in outs],
        in_specs=specs or [SMEM] + [VMEM] * (len(operands) - 1),
        out_specs=[VMEM] * len(outs),
        scratch_shapes=scratch,
        name=name,
        compiler_params=pltpu.CompilerParams(vmem_limit_bytes=limit << 20),
    )(*operands)


SHARE = 144


def forward_pass_body(
    pos, gain, patches_any, stem_any, up_any, deriv, normal, inverse, mine, send, p, w, u, t, sem
):
    copies = [pltpu.make_async_copy(patches_any, p, sem.at[0])]
    for k in range(3):
        rows = pl.ds(k * 512, 512)
        copies.append(pltpu.make_async_copy(stem_any.at[rows], w.at[rows], sem.at[1 + k]))
    for k in range(2):
        cols = pl.ds(k * 1024, 1024)
        copies.append(pltpu.make_async_copy(up_any.at[:, cols], u.at[:, cols], sem.at[4 + k]))
    for copy in copies:
        copy.start()

    copies[0].wait()
    acc = None
    for k in range(3):
        copies[1 + k].wait()
        part = jnp.dot(
            p[:, k * 512 : k * 512 + 512], w[k * 512 : k * 512 + 512], preferred_element_type=F32
        )
        acc = part if acc is None else acc + part
    embed = acc.astype(BF).astype(F32)
    center = jnp.mean(embed, axis=1, keepdims=True)
    shifted = embed - center
    scale = lax.rsqrt(jnp.mean(shifted * shifted, axis=1, keepdims=True) + 1e-06)
    norm = shifted * scale
    normal[...] = norm
    inverse[...] = scale
    normed = (norm * gain[...]).astype(BF)
    pt = p[...].T
    nt = normed.T
    for b in range(16):
        for half in range(2):
            at = b * 2 + half
            t[b, half, 64:96] = nt[at * 32 : at * 32 + 32]
            t[b, half, 96:144] = pt[at * 48 : at * 48 + 48]
    for j in range(8):
        if j % 4 == 0:
            copies[4 + j // 4].wait()
        cols = slice(j * 256, j * 256 + 256)
        pre = jnp.dot(normed, u[:, cols], preferred_element_type=F32)
        cdf = 0.5 * (1.0 + lax.erf(pre * math.sqrt(0.5)))
        deriv[:, cols] = cdf + pre * jnp.exp(-0.5 * pre * pre) * (1.0 / math.sqrt(2.0 * math.pi))
        ht = (pre * cdf).astype(BF).T
        for q in range(4):
            t[j * 2 + q // 2, q % 2, 0:64] = ht[q * 64 : q * 64 + 64]
    c = pos[3]
    mine[...] = t[:, c]
    send[...] = t[:, 1 - c]


def forward_pass(pos, gain, patches, stem_weight, up_weight):
    anywhere = pl.BlockSpec(memory_space=pl.ANY)
    return call(
        forward_pass_body,
        [((256, 2048), F32), ((256, 1024), F32), ((256, 1), F32)] + [((16, SHARE, 256), BF)] * 2,
        [
            pltpu.VMEM((256, 1536), BF),
            pltpu.VMEM((1536, 1024), BF),
            pltpu.VMEM((1024, 2048), BF),
            pltpu.VMEM((16, 2, SHARE, 256), BF),
            pltpu.SemaphoreType.DMA((6,)),
        ],
        "forward_pass",
        pos,
        gain.reshape(1, 1024),
        patches,
        stem_weight,
        up_weight,
        limit=50,
        specs=[SMEM, VMEM, anywhere, anywhere, anywhere],
    )


ROWS = 176
CHUNK = 704


def chunk_of(me, pos, rel):
    return lax.rem(me + rel * (1 + 2 * pos[3]), 4)


def dot2(lefts, rights):
    acc = jnp.dot(lefts[0], rights[0], preferred_element_type=F32)
    acc += jnp.dot(lefts[1], rights[1], preferred_element_type=F32)
    return acc.astype(BF)


def terms_body(pos, lm, lr, cm, cr, gm, gr, em, er, *outs):
    def columns(ref, start, width):
        return ref[:, pl.ds(pl.multiple_of(start, LANES), width)]

    left = (lm, lr)
    for rel in range(4):
        to = chunk_of(pos[0], pos, rel)
        xh, xl = to // 2, lax.rem(to, 2)
        dst = outs[rel]
        acc = dot2(
            [ref[:, xh, 0:64].reshape(512, 256) for ref in left],
            [columns(ref, xl * 512, 512) for ref in (cm, cr)],
        )
        for yy in range(4):
            dst[yy, 0:512] = acc[:, yy * 128 : yy * 128 + 128]
        acc = dot2(
            [ref[0:4, xh, 96:144].reshape(192, 256) for ref in left],
            [columns(ref, xl * 512, 512) for ref in (em, er)],
        )
        for yy in range(4):
            dst[yy, 512:704] = acc[:, yy * 128 : yy * 128 + 128]
    for rel in range(4):
        to = chunk_of(pos[1], pos, rel)
        dst = outs[4 + rel]
        acc = dot2(
            [ref[:, :, 64:96].reshape(512, 256) for ref in left],
            [columns(ref, to * 512, 512) for ref in (gm, gr)],
        )
        for z in range(8):
            for xx in range(4):
                for k in range(2):
                    row, col = (z * 2 + xx // 2) * 32, (xx % 2 * 2 + k) * 128
                    at = z * 64 + k * 32
                    dst[xx, at : at + 32] = acc[row : row + 32, col : col + 128]
        acc = dot2(
            [ref[4:8, :, 96:144].reshape(384, 256) for ref in left],
            [
                jnp.concatenate(
                    [columns(ref, to * 128, 128), columns(ref, 512 + to * 128, 128)], axis=1
                )
                for ref in (em, er)
            ],
        )
        for z in range(4):
            for xx in range(4):
                row, col = (z * 2 + xx // 2) * 48, xx % 2 * 128
                at = 512 + z * 48
                dst[xx, at : at + 48] = acc[row : row + 48, col : col + 128]


def terms(pos, left, cotangent, preact_grad, embed_grad):
    outs = call(
        terms_body,
        [((4, CHUNK, LANES), BF)] * 8,
        [],
        "terms",
        pos,
        *[v.reshape(8, 2, SHARE, 256) for v in left],
        *cotangent,
        *preact_grad,
        *embed_grad,
        limit=24,
    )
    return outs[:4], outs[4:]


def pass_on_body(keep, got, out):
    out[...] = (keep[...].astype(F32) + got[...].astype(F32)).astype(BF)


def rings(axes, parts):
    result = []
    for axis, (own, keep, ahead, behind) in zip(axes, parts):
        got = move(ahead, axis, 1)
        near = move(behind, axis, -1)
        (total,) = call(
            pass_on_body, [(keep.shape, BF)], [], "pass_on", keep, got, specs=[VMEM, VMEM]
        )
        result += [own, near, move(total, axis, 1)]
    return result


def add3(a, b, c):
    return (a.astype(F32) + b.astype(F32) + c.astype(F32)).astype(BF)


def turn_body(pos, *refs):
    for p in range(2):
        a, b, c = refs[3 * p : 3 * p + 3]
        for rel in range(4):
            to = chunk_of(pos[1 - p], pos, rel)
            refs[6 + 4 * p + rel][...] = add3(a[to], b[to], c[to])


def reduce_xy(pos, parts):
    outs = call(
        turn_body, [((CHUNK, LANES), BF)] * 8, [], "ring_turn", pos, *rings("xy", parts)
    )
    return rings("yx", (outs[:4], outs[4:]))


def pack_body(*refs):
    out = refs[6]
    for p in range(2):
        a, b, c = refs[3 * p : 3 * p + 3]
        total = add3(a[...], b[...], c[...])
        for z in range(8):
            out[z, 64 * p : 64 * p + 64] = total[z * 64 : z * 64 + 64]
        for z in range(4):
            out[4 * p + z, 128:176] = total[512 + z * 48 : 560 + z * 48]


def sum_body(got, out):
    total = got[0].astype(F32)
    for k in range(1, 8):
        total += got[k].astype(F32)
    share = total.astype(BF)
    for k in range(8):
        out[k] = share


def unpack_body(got, stem, up, down):
    for y in range(4):
        for xl in range(2):
            piece = got[y * 2 + xl].astype(F32)
            col = (xl * 4 + y) * LANES
            down[:, col : col + LANES] = piece[0:64]
            stem[:, col : col + LANES] = piece[128:176]
            col = (y * 2 + xl) * 256
            up[:, col : col + LANES] = piece[64:96]
            up[:, col + LANES : col + 256] = piece[96:128]


def finish(pieces):
    share = [((8, ROWS, LANES), BF)]
    (packed,) = call(pack_body, share, [], "z_pack", *pieces, specs=[VMEM] * 6)
    got = lax.all_to_all(packed, "z", 0, 0, tiled=True)
    (copies,) = call(sum_body, share, [], "z_sum", got, specs=[VMEM])
    every = lax.all_to_all(copies, ("y", "xl"), 0, 0, tiled=True)
    outs = [((48, 1024), F32), ((32, 2048), F32), ((64, 1024), F32)]
    return call(unpack_body, outs, [], "unpack", every, specs=[VMEM])


def local(patches, stem_weight, ln_gain, up_weight, down_weight, cotangent):
    x = lax.axis_index("xh") * 2 + lax.axis_index("xl")
    pos = jnp.stack([x, lax.axis_index("y"), lax.axis_index("z"), lax.axis_index("c")])
    pos = pos.astype(jnp.int32)

    cot_other = move(cotangent, "c", 0)
    deriv, normal, inverse, mine, send = forward_pass(
        pos, ln_gain, patches, stem_weight, up_weight
    )
    other = move(send, "c", 0)

    over_cols = (((1,), (1,)), ((), ()))
    hidden_grad = lax.dot_general(cotangent, down_weight, over_cols, preferred_element_type=F32)
    preact_grad = (hidden_grad * deriv).astype(BF)
    preact_other = move(preact_grad, "c", 0)

    normal_grad = (
        lax.dot_general(preact_grad, up_weight, over_cols, preferred_element_type=F32) * ln_gain
    )
    first_mean = jnp.mean(normal_grad, axis=1, keepdims=True)
    second_mean = jnp.mean(normal_grad * normal, axis=1, keepdims=True)
    embed_grad = (
        cotangent.astype(F32) + inverse * (normal_grad - first_mean - normal * second_mean)
    ).astype(BF)
    embed_other = move(embed_grad, "c", 0)

    parts = terms(
        pos, (mine, other), (cotangent, cot_other), (preact_grad, preact_other), (embed_grad, embed_other)
    )
    return tuple(finish(reduce_xy(pos, parts)))


def solution(mesh):
    fine = Mesh(mesh.devices.reshape(4, 2, 8, 2, 2), AXES)
    rows = P(("z", "xh", "c"), None)
    in_specs = (P(AXES, None), P(), P(), P(), P(), P(AXES, None))
    return jax.shard_map(
        local, mesh=fine, in_specs=in_specs, out_specs=(rows, rows, rows), check_vma=False
    )
```

time: 117 us -> 107 us (0.915)
  matrix products: 13.3 us -> 5.78 us
  starting transfers between devices: 25.3 us -> 18.1 us
  Pallas kernels: 8.98 us -> 15.2 us
  waiting for transfers between devices: 34.9 us -> 30.8 us
  blocking collectives: 28.5 us -> 31.9 us
  local copies, waits for them, and re-layouts: 3.09 us -> 1.85 us
    dot_general x2 -> x0, matrix products: 9.81 us -> none  [the longest x1 7.61 us: local(): preact = jnp.dot(normed, up_weight, preferred_element_type=F32)]
    pallas_call x5 -> x10, Pallas kernels: 7.49 us -> 15.2 us  [call(): pl.pallas_call(body, out_shape=[jax.ShapeDtypeStruct(s, d) for s, d in ou...]
    ppermute x22 -> x16, starting transfers between devices: 25.3 us -> 18.1 us  [move(): return lax.ppermute(value, AXES, sorted(pairs))]
    ppermute x22 -> x16, waiting for transfers between devices: 34.9 us -> 30.8 us  [move(): return lax.ppermute(value, AXES, sorted(pairs))]
    all_to_all x1, blocking collectives: 18.2 us -> 20.7 us  [finish(): got = lax.all_to_all(packed, 'z', 0, 0, tiled=True)]
    pallas_call x5 -> x0, Pallas kernels: 1.5 us -> none  [the longest x3 1.09 us: plain(): pl.pallas_call(body, out_shape=[jax.ShapeDtypeStruct(s, d) for s, d in ou...]
    convert_element_type x1, other arithmetic: 0.41 us -> 1.84 us  [local(): embed_grad = (cotangent.astype(F32) + inverse * (normal_grad - first_mean...]
    convert_element_type x1 -> x0, other arithmetic: 1.33 us -> none  [local(): normed = (normal * ln_gain).astype(BF)]
  transfers between devices with their start and end apart: 22 -> 16, of which waited for: 12 -> 9; matrix products, arithmetic and copies ran while one was open for 10% -> 7% of each run, Pallas kernels for 2% -> 8%
where the time goes in v2:
time: 107 us; the launch traced here: 106 us
  blocking collectives  31.9 us (30%)
  waiting for transfers between devices  30.8 us (29%)
  starting transfers between devices  18.1 us (17%)
  Pallas kernels  15.2 us (14%)
  matrix products  5.78 us (5%)
  other arithmetic  2.02 us (2%)
  local copies, waits for them, and re-layouts  1.85 us (2%)
    ppermute x16, waiting for transfers between devices, move(): return lax.ppermute(value, AXES, sorted(pairs))  30.8 us
    all_to_all x1, blocking collectives, finish(): got = lax.all_to_all(packed, 'z', 0, 0, tiled=True)  20.7 us
    ppermute x16, starting transfers between devices, move(): return lax.ppermute(value, AXES, sorted(pairs))  18.1 us
    pallas_call x10, Pallas kernels, call(): pl.pallas_call(body, out_shape=[jax.ShapeDtypeStruct(s, d) for s, d in ou...  15.2 us
    all_to_all x1, blocking collectives, finish(): every = lax.all_to_all(copies, ('y', 'xl'), 0, 0, tiled=True)  11.2 us
    dot_general x1, matrix products, local(): lax.dot_general(cotangent, down_weight, over_cols, preferred_element_type...  3.31 us
    dot_general x1, matrix products, local(): lax.dot_general(preact_grad, up_weight, over_cols, preferred_element_type...  2.47 us
  transfers between devices with their start and end apart: 16, of which 9 were waited for; matrix products, arithmetic and copies ran while one was open for 7% of the time, Pallas kernels for 8%

profile of v2, /device:TPU:4, one launch (start us, length us, event | category | flops | bytes accessed | tf_op | source)
XLA Modules:
  0.0 106.4 jit_solution(2277690676474320810)
XLA Ops:
  0.8 1.1 %copy-done.2 = bf16[256,1536]{1,0:T(8,128)(2,1)S(1)} copy-done((bf16[256,1536]{1,0:T(8,128)(2,1)S(1)}, bf16[256,1536]{1,0:T(8,128)(2,1)}, u32[]{:S(2)}) %copy-start.2) | copy-done | bytes 786456
  2.0 0.7 copy-done.3
  2.7 7.7 %forward_pass.1 = (f32[256,2048]{1,0:T(8,128)}, f32[256,1024]{1,0:T(8,128)S(1)}, f32[256,1]{1,0:T(8,128)S(1)}, bf16[16,144,256]{2,1,0:T(8,128)(2,1)S(1)}, bf16[16,144,256]{2,1,0:T(8,128)(2,1)}) custom-call(s32[4]{0:T(128)S(1)} %pad_add_fusion.pos, f32[1,1024]{1,0:T(1,128)S(1)} %bitcast.12, bf16[256,1536]{1,0:T(8,128)(2,1)S(1)} %copy-done.2, ...), custom_call_target="tpu_custom_call" | custom-call | tf_op jit(solution)/shard_map/forward_pass/pallas_call | solution.py:36
  10.5 3.3 %fusion.gm = bf16[256,2048]{1,0:T(8,128)(2,1)S(1)} fusion(f32[256,2048]{1,0:T(8,128)} %get-tuple-element.26, bf16[256,1024]{1,0:T(8,128)(2,1)S(1)} %copy-done, bf16[2048,1024]{1,0:T(8,128)(2,1)S(1)} %copy-done.5), kind=kOutput, calls=%fused_computation.1 | convolution fusion | flops 1074790400 | bytes 7864320 | tf_op jit(solution)/shard_map/dot_general | solution.py:293
  13.8 0.6 collective-permute-start.2
  14.4 2.5 %fusion.1 = (f32[256]{0:T(256)S(1)}, f32[256]{0:T(256)S(1)}, f32[256,1024]{1,0:T(8,128)}) fusion(f32[256,1024]{1,0:T(8,128)S(1)} %get-tuple-element.28, f32[1024]{0:T(1024)S(1)} %copy-done.4, bf16[256,2048]{1,0:T(8,128)(2,1)S(1)} %fusion.gm, bf16[1024,2048]{1,0:T(8,128)(2,1)S(1)} %copy-done.6), kind=kOutput, calls=%fused_computation.8 | convolution fusion | flops 1074789888 | bytes 7346176 | tf_op jit(solution)/shard_map/dot_general | solution.py:298
  17.0 1.8 %add_convert_fusion.em = bf16[256,1024]{1,0:T(8,128)(2,1)S(1)} fusion(f32[256,1024]{1,0:T(8,128)} %copy-done.1, f32[256,1024]{1,0:T(8,128)} %get-tuple-element.47, bf16[256,1024]{1,0:T(8,128)(2,1)S(1)} %copy-done, f32[256]{0:T(256)S(1)} %get-tuple-element.48, f32[256]{0:T(256)S(1)} %get-tuple-element.49, f32[256]{0:T(256)S(1)} %reduce), kind=kLoop, calls=%fused_computation.3 | loop fusion | flops 1835008 | bytes 3148800 | tf_op jit(solution)/shard_map/convert_element_type | solution.py:304
  18.9 0.5 collective-permute-start.3
  19.4 1.5 %collective-permute-done.3.er = bf16[256,1024]{1,0:T(8,128)(2,1)S(1)} collective-permute-done((bf16[256,1024]{1,0:T(8,128)(2,1)S(1)}, bf16[256,1024]{1,0:T(8,128)(2,1)S(1)}, u32[]{:S(2)}, u32[]{:S(2)}) %collective-permute-start.3) | collective-permute-done | bytes 524320 | tf_op jit(solution)/shard_map/ppermute | solution.py:32
  20.9 4.9 %terms.1 = (bf16[4,704,128]{2,1,0:T(8,128)(2,1)S(1)}, bf16[4,704,128]{2,1,0:T(8,128)(2,1)S(1)}, bf16[4,704,128]{2,1,0:T(8,128)(2,1)S(1)}, bf16[4,704,128]{2,1,0:...) custom-call(s32[4]{0:T(128)S(1)} %pad_add_fusion.pos, ...), custom_call_target="tpu_custom_call" | custom-call | tf_op jit(solution)/shard_map/terms/pallas_call | solution.py:36
  25.8 1.5 %collective-permute-start.5 = (bf16[4,704,128]{2,1,0:T(8,128)(2,1)S(1)}, bf16[4,704,128]{2,1,0:T(8,128)(2,1)S(1)}, u32[]{:S(2)}, u32[]{:S(2)}) collective-permute-start(bf16[4,704,128]{2,1,0:T(8,128)(2,1)S(1)} %get-tuple-element.32), channel_id=1, source_target_pairs={{0,32},{1,35},{2,34},{3,33},{4,36},{5,39},{6,38},{7,37},{8,40},{9,... | collective-permute-start | bytes 2162696 | tf_op jit(solution)/shard_map/ppermute | solution.py:32
  27.3 1.6 %collective-permute-start.8 = (bf16[4,704,128]{2,1,0:T(8,128)(2,1)S(1)}, bf16[4,704,128]{2,1,0:T(8,128)(2,1)S(1)}, u32[]{:S(2)}, u32[]{:S(2)}) collective-permute-start(bf16[4,704,128]{2,1,0:T(8,128)(2,1)S(1)} %get-tuple-element.36), channel_id=1, source_target_pairs={{0,64},{1,193},{2,66},{3,195},{4,68},{5,197},{6,70},{7,199},{8,72}... | collective-permute-start | bytes 2162696 | tf_op jit(solution)/shard_map/ppermute | solution.py:32
  28.9 0.8 collective-permute-start.4
  29.7 1.7 %collective-permute-start.7 = (bf16[4,704,128]{2,1,0:T(8,128)(2,1)S(1)}, bf16[4,704,128]{2,1,0:T(8,128)(2,1)S(1)}, u32[]{:S(2)}, u32[]{:S(2)}) collective-permute-start(bf16[4,704,128]{2,1,0:T(8,128)(2,1)S(1)} %get-tuple-element.34), channel_id=1, source_target_pairs={{0,192},{1,65},{2,194},{3,67},{4,196},{5,69},{6,198},{7,71},{8,200... | collective-permute-start | bytes 2162696 | tf_op jit(solution)/shard_map/ppermute | solution.py:32
  31.4 11.3 %collective-permute-done.5.got = bf16[4,704,128]{2,1,0:T(8,128)(2,1)S(1)} collective-permute-done((bf16[4,704,128]{2,1,0:T(8,128)(2,1)S(1)}, bf16[4,704,128]{2,1,0:T(8,128)(2,1)S(1)}, u32[]{:S(2)}, u32[]{:S(2)}) %collective-permute-start.5) | collective-permute-done | bytes 720928 | tf_op jit(solution)/shard_map/ppermute | solution.py:32
  42.8 1.0 collective-permute-start.6
  43.9 1.2 %collective-permute-done.8.got = bf16[4,704,128]{2,1,0:T(8,128)(2,1)S(1)} collective-permute-done((bf16[4,704,128]{2,1,0:T(8,128)(2,1)S(1)}, bf16[4,704,128]{2,1,0:T(8,128)(2,1)S(1)}, u32[]{:S(2)}, u32[]{:S(2)}) %collective-permute-start.8) | collective-permute-done | bytes 720928 | tf_op jit(solution)/shard_map/ppermute | solution.py:32
  45.3 3.0 %collective-permute-start.9 = (bf16[4,704,128]{2,1,0:T(8,128)(2,1)S(1)}, bf16[4,704,128]{2,1,0:T(8,128)(2,1)S(1)}, u32[]{:S(2)}, u32[]{:S(2)}) collective-permute-start(bf16[4,704,128]{2,1,0:T(8,128)(2,1)S(1)} %pass_on.5), channel_id=1, source_target_pairs={{0,64},{1,193},{2,66},{3,195},{4,68},{5,197},{6,70},{7,199},{8,72}... | collective-permute-start | bytes 2162696 | tf_op jit(solution)/shard_map/ppermute | solution.py:32
  48.3 5.9 %collective-permute-done.6.refs_2_ = bf16[4,704,128]{2,1,0:T(8,128)(2,1)S(1)} collective-permute-done((bf16[4,704,128]{2,1,0:T(8,128)(2,1)S(1)}, bf16[4,704,128]{2,1,0:T(8,128)(2,1)S(1)}, u32[]{:S(2)}, u32[]{:S(2)}) %collective-permute-start.6) | collective-permute-done | bytes 720928 | tf_op jit(solution)/shard_map/ppermute | solution.py:32
  54.2 4.5 %collective-permute-done.9.refs_5_ = bf16[4,704,128]{2,1,0:T(8,128)(2,1)S(1)} collective-permute-done((bf16[4,704,128]{2,1,0:T(8,128)(2,1)S(1)}, bf16[4,704,128]{2,1,0:T(8,128)(2,1)S(1)}, u32[]{:S(2)}, u32[]{:S(2)}) %collective-permute-start.9) | collective-permute-done | bytes 720928 | tf_op jit(solution)/shard_map/ppermute | solution.py:32
  58.7 1.1 ring_turn.1
  59.8 0.9 collective-permute-start.11
  60.7 0.4 collective-permute-start.14
  61.1 3.1 %collective-permute-start.10 = (bf16[704,128]{1,0:T(8,128)(2,1)S(1)}, bf16[704,128]{1,0:T(8,128)(2,1)S(1)}, u32[]{:S(2)}, u32[]{:S(2)}) collective-permute-start(bf16[704,128]{1,0:T(8,128)(2,1)S(1)} %get-tuple-element.38), channel_id=1, source_target_pairs={{0,192},{1,65},{2,194},{3,67},{4,196},{5,69},{6,198},{7,71},{8,200... | collective-permute-start | bytes 540680 | tf_op jit(solution)/shard_map/ppermute | solution.py:32
  64.2 0.9 collective-permute-start.13
  65.1 1.4 %collective-permute-done.11.got = bf16[704,128]{1,0:T(8,128)(2,1)S(1)} collective-permute-done((bf16[704,128]{1,0:T(8,128)(2,1)S(1)}, bf16[704,128]{1,0:T(8,128)(2,1)S(1)}, u32[]{:S(2)}, u32[]{:S(2)}) %collective-permute-start.11) | collective-permute-done | bytes 180256 | tf_op jit(solution)/shard_map/ppermute | solution.py:32
  66.8 1.8 %collective-permute-start.15 = (bf16[704,128]{1,0:T(8,128)(2,1)S(1)}, bf16[704,128]{1,0:T(8,128)(2,1)S(1)}, u32[]{:S(2)}, u32[]{:S(2)}) collective-permute-start(bf16[704,128]{1,0:T(8,128)(2,1)S(1)} %pass_on.7), channel_id=1, source_target_pairs={{0,32},{1,35},{2,34},{3,33},{4,36},{5,39},{6,38},{7,37},{8,40},{9,... | collective-permute-start | bytes 540680 | tf_op jit(solution)/shard_map/ppermute | solution.py:32
  68.8 2.3 %collective-permute-done.13.refs_4_ = bf16[704,128]{1,0:T(8,128)(2,1)S(1)} collective-permute-done((bf16[704,128]{1,0:T(8,128)(2,1)S(1)}, bf16[704,128]{1,0:T(8,128)(2,1)S(1)}, u32[]{:S(2)}, u32[]{:S(2)}) %collective-permute-start.13) | collective-permute-done | bytes 180256 | tf_op jit(solution)/shard_map/ppermute | solution.py:32
  71.2 2.2 %collective-permute-done.12.refs_2_ = bf16[704,128]{1,0:T(8,128)(2,1)S(1)} collective-permute-done((bf16[704,128]{1,0:T(8,128)(2,1)S(1)}, bf16[704,128]{1,0:T(8,128)(2,1)S(1)}, u32[]{:S(2)}, u32[]{:S(2)}) %collective-permute-start.12) | collective-permute-done | bytes 180256 | tf_op jit(solution)/shard_map/ppermute | solution.py:32
  73.5 20.7 %all_to_all.10.got = bf16[8,176,128]{2,1,0:T(8,128)(2,1)S(1)} all-to-all(bf16[8,176,128]{2,1,0:T(8,128)(2,1)S(1)} %z_pack.1), channel_id=1, replica_groups=mesh['y'=4,'xl'=2,'z'=8,'xh'=2,'c'=2] {'z'}, dimensions={0} | all-to-all | bytes 720896 | tf_op jit(solution)/shard_map/all_to_all | solution.py:274
  94.3 11.2 %all_to_all.11.got = bf16[8,176,128]{2,1,0:T(8,128)(2,1)S(1)} all-to-all(bf16[8,176,128]{2,1,0:T(8,128)(2,1)S(1)} %z_sum.1), channel_id=1, replica_groups=mesh['y'=4,'xl'=2,'z'=8,'xh'=2,'c'=2] {'y','xl'}, dimensions={0} | all-to-all | bytes 720896 | tf_op jit(solution)/shard_map/all_to_all | solution.py:276
  105.5 0.9 unpack.1
  (32 shorter events, 1.4 us)
Async XLA Ops:
  0.6 9.8 %copy-start = (bf16[256,1024]{1,0:T(8,128)(2,1)S(1)}, bf16[256,1024]{1,0:T(8,128)(2,1)}, u32[]{:S(2)}) copy-start(bf16[256,1024]{1,0:T(8,128)(2,1)} %cm.1) | copy-start | bytes 1572868
  0.6 18.7 %collective-permute-start.1 = (bf16[256,1024]{1,0:T(8,128)(2,1)}, bf16[256,1024]{1,0:T(8,128)(2,1)S(1)}, u32[]{:S(2)}, u32[]{:S(2)}) collective-permute-start(bf16[256,1024]{1,0:T(8,128)(2,1)} %cm.1), channel_id=1, source_target_pairs={{0,1},{1,0},{2,3},{3,2},{4,5},{5,4},{6,7},{7,6},{8,9},{9,8},{10,11... | collective-permute-start | bytes 1572872 | tf_op jit(solution)/shard_map/ppermute | solution.py:32
  0.8 1.1 %copy-start.2 = (bf16[256,1536]{1,0:T(8,128)(2,1)S(1)}, bf16[256,1536]{1,0:T(8,128)(2,1)}, u32[]{:S(2)}) copy-start(bf16[256,1536]{1,0:T(8,128)(2,1)} %patches_any.1) | copy-start | bytes 2359300
  2.0 0.7 copy-start.3
  2.6 7.8 %copy-start.5 = (bf16[2048,1024]{1,0:T(8,128)(2,1)S(1)}, bf16[2048,1024]{1,0:T(8,128)(2,1)}, u32[]{:S(2)}) copy-start(bf16[2048,1024]{1,0:T(8,128)(2,1)} %param.10) | copy-start | bytes 12582916
  10.4 6.5 %copy-start.1 = (f32[256,1024]{1,0:T(8,128)}, f32[256,1024]{1,0:T(8,128)S(1)}, u32[]{:S(2)}) copy-start(f32[256,1024]{1,0:T(8,128)S(1)} %get-tuple-element.28) | copy-start | bytes 3145732
  10.4 4.0 %copy-start.4 = (f32[1024]{0:T(1024)S(1)}, f32[1024]{0:T(1024)}, u32[]{:S(2)}) copy-start(f32[1024]{0:T(1024)} %param.8) | copy-start | bytes 12292
  10.4 4.0 %copy-start.6 = (bf16[1024,2048]{1,0:T(8,128)(2,1)S(1)}, bf16[1024,2048]{1,0:T(8,128)(2,1)}, u32[]{:S(2)}) copy-start(bf16[1024,2048]{1,0:T(8,128)(2,1)} %up_any.1) | copy-start | bytes 12582916
  13.8 7.2 %collective-permute-start.2 = (bf16[256,2048]{1,0:T(8,128)(2,1)S(1)}, bf16[256,2048]{1,0:T(8,128)(2,1)}, u32[]{:S(2)}, u32[]{:S(2)}) collective-permute-start(bf16[256,2048]{1,0:T(8,128)(2,1)S(1)} %fusion.gm), channel_id=1, source_target_pairs={{0,1},{1,0},{2,3},{3,2},{4,5},{5,4},{6,7},{7,6},{8,9},{9,8},{10,11... | collective-permute-start | bytes 3145736 | tf_op jit(solution)/shard_map/ppermute | solution.py:32
  14.3 6.6 %collective-permute-start = (bf16[16,144,256]{2,1,0:T(8,128)(2,1)}, bf16[16,144,256]{2,1,0:T(8,128)(2,1)}, u32[]{:S(2)}, u32[]{:S(2)}) collective-permute-start(bf16[16,144,256]{2,1,0:T(8,128)(2,1)} %get-tuple-element.25), channel_id=1, source_target_pairs={{0,1},{1,0},{2,3},{3,2},{4,5},{5,4},{6,7},{7,6},{8,9},{9,8},{10,11... | collective-permute-start | bytes 3538952 | tf_op jit(solution)/shard_map/ppermute | solution.py:32
  18.9 2.0 %collective-permute-start.3 = (bf16[256,1024]{1,0:T(8,128)(2,1)S(1)}, bf16[256,1024]{1,0:T(8,128)(2,1)S(1)}, u32[]{:S(2)}, u32[]{:S(2)}) collective-permute-start(bf16[256,1024]{1,0:T(8,128)(2,1)S(1)} %add_convert_fusion.em), channel_id=1, source_target_pairs={{0,1},{1,0},{2,3},{3,2},{4,5},{5,4},{6,7},{7,6},{8,9},{9,8},{10,11... | collective-permute-start | bytes 1572872 | tf_op jit(solution)/shard_map/ppermute | solution.py:32
  25.8 16.8 %collective-permute-start.5 = (bf16[4,704,128]{2,1,0:T(8,128)(2,1)S(1)}, bf16[4,704,128]{2,1,0:T(8,128)(2,1)S(1)}, u32[]{:S(2)}, u32[]{:S(2)}) collective-permute-start(bf16[4,704,128]{2,1,0:T(8,128)(2,1)S(1)} %get-tuple-element.32), channel_id=1, source_target_pairs={{0,32},{1,35},{2,34},{3,33},{4,36},{5,39},{6,38},{7,37},{8,40},{9,... | collective-permute-start | bytes 2162696 | tf_op jit(solution)/shard_map/ppermute | solution.py:32
  27.3 17.8 %collective-permute-start.8 = (bf16[4,704,128]{2,1,0:T(8,128)(2,1)S(1)}, bf16[4,704,128]{2,1,0:T(8,128)(2,1)S(1)}, u32[]{:S(2)}, u32[]{:S(2)}) collective-permute-start(bf16[4,704,128]{2,1,0:T(8,128)(2,1)S(1)} %get-tuple-element.36), channel_id=1, source_target_pairs={{0,64},{1,193},{2,66},{3,195},{4,68},{5,197},{6,70},{7,199},{8,72}... | collective-permute-start | bytes 2162696 | tf_op jit(solution)/shard_map/ppermute | solution.py:32
  28.9 19.4 %collective-permute-start.4 = (bf16[4,704,128]{2,1,0:T(8,128)(2,1)S(1)}, bf16[4,704,128]{2,1,0:T(8,128)(2,1)S(1)}, u32[]{:S(2)}, u32[]{:S(2)}) collective-permute-start(bf16[4,704,128]{2,1,0:T(8,128)(2,1)S(1)} %get-tuple-element.30), channel_id=1, source_target_pairs={{0,34},{1,33},{2,32},{3,35},{4,38},{5,37},{6,36},{7,39},{8,42},{9,... | collective-permute-start | bytes 2162696 | tf_op jit(solution)/shard_map/ppermute | solution.py:32
  29.7 18.6 %collective-permute-start.7 = (bf16[4,704,128]{2,1,0:T(8,128)(2,1)S(1)}, bf16[4,704,128]{2,1,0:T(8,128)(2,1)S(1)}, u32[]{:S(2)}, u32[]{:S(2)}) collective-permute-start(bf16[4,704,128]{2,1,0:T(8,128)(2,1)S(1)} %get-tuple-element.34), channel_id=1, source_target_pairs={{0,192},{1,65},{2,194},{3,67},{4,196},{5,69},{6,198},{7,71},{8,200... | collective-permute-start | bytes 2162696 | tf_op jit(solution)/shard_map/ppermute | solution.py:32
  42.8 11.4 %collective-permute-start.6 = (bf16[4,704,128]{2,1,0:T(8,128)(2,1)S(1)}, bf16[4,704,128]{2,1,0:T(8,128)(2,1)S(1)}, u32[]{:S(2)}, u32[]{:S(2)}) collective-permute-start(bf16[4,704,128]{2,1,0:T(8,128)(2,1)S(1)} %pass_on.4), channel_id=1, source_target_pairs={{0,32},{1,35},{2,34},{3,33},{4,36},{5,39},{6,38},{7,37},{8,40},{9,... | collective-permute-start | bytes 2162696 | tf_op jit(solution)/shard_map/ppermute | solution.py:32
  45.3 13.5 %collective-permute-start.9 = (bf16[4,704,128]{2,1,0:T(8,128)(2,1)S(1)}, bf16[4,704,128]{2,1,0:T(8,128)(2,1)S(1)}, u32[]{:S(2)}, u32[]{:S(2)}) collective-permute-start(bf16[4,704,128]{2,1,0:T(8,128)(2,1)S(1)} %pass_on.5), channel_id=1, source_target_pairs={{0,64},{1,193},{2,66},{3,195},{4,68},{5,197},{6,70},{7,199},{8,72}... | collective-permute-start | bytes 2162696 | tf_op jit(solution)/shard_map/ppermute | solution.py:32
  59.8 6.8 %collective-permute-start.11 = (bf16[704,128]{1,0:T(8,128)(2,1)S(1)}, bf16[704,128]{1,0:T(8,128)(2,1)S(1)}, u32[]{:S(2)}, u32[]{:S(2)}) collective-permute-start(bf16[704,128]{1,0:T(8,128)(2,1)S(1)} %get-tuple-element.40), channel_id=1, source_target_pairs={{0,64},{1,193},{2,66},{3,195},{4,68},{5,197},{6,70},{7,199},{8,72}... | collective-permute-start | bytes 540680 | tf_op jit(solution)/shard_map/ppermute | solution.py:32
  60.7 6.0 %collective-permute-start.14 = (bf16[704,128]{1,0:T(8,128)(2,1)S(1)}, bf16[704,128]{1,0:T(8,128)(2,1)S(1)}, u32[]{:S(2)}, u32[]{:S(2)}) collective-permute-start(bf16[704,128]{1,0:T(8,128)(2,1)S(1)} %get-tuple-element.44), channel_id=1, source_target_pairs={{0,32},{1,35},{2,34},{3,33},{4,36},{5,39},{6,38},{7,37},{8,40},{9,... | collective-permute-start | bytes 540680 | tf_op jit(solution)/shard_map/ppermute | solution.py:32
  61.1 7.7 %collective-permute-start.10 = (bf16[704,128]{1,0:T(8,128)(2,1)S(1)}, bf16[704,128]{1,0:T(8,128)(2,1)S(1)}, u32[]{:S(2)}, u32[]{:S(2)}) collective-permute-start(bf16[704,128]{1,0:T(8,128)(2,1)S(1)} %get-tuple-element.38), channel_id=1, source_target_pairs={{0,192},{1,65},{2,194},{3,67},{4,196},{5,69},{6,198},{7,71},{8,200... | collective-permute-start | bytes 540680 | tf_op jit(solution)/shard_map/ppermute | solution.py:32
  64.2 6.9 %collective-permute-start.13 = (bf16[704,128]{1,0:T(8,128)(2,1)S(1)}, bf16[704,128]{1,0:T(8,128)(2,1)S(1)}, u32[]{:S(2)}, u32[]{:S(2)}) collective-permute-start(bf16[704,128]{1,0:T(8,128)(2,1)S(1)} %get-tuple-element.42), channel_id=1, source_target_pairs={{0,34},{1,33},{2,32},{3,35},{4,38},{5,37},{6,36},{7,39},{8,42},{9,... | collective-permute-start | bytes 540680 | tf_op jit(solution)/shard_map/ppermute | solution.py:32
  66.6 6.8 %collective-permute-start.12 = (bf16[704,128]{1,0:T(8,128)(2,1)S(1)}, bf16[704,128]{1,0:T(8,128)(2,1)S(1)}, u32[]{:S(2)}, u32[]{:S(2)}) collective-permute-start(bf16[704,128]{1,0:T(8,128)(2,1)S(1)} %pass_on.6), channel_id=1, source_target_pairs={{0,64},{1,193},{2,66},{3,195},{4,68},{5,197},{6,70},{7,199},{8,72}... | collective-permute-start | bytes 540680 | tf_op jit(solution)/shard_map/ppermute | solution.py:32
  66.8 6.6 %collective-permute-start.15 = (bf16[704,128]{1,0:T(8,128)(2,1)S(1)}, bf16[704,128]{1,0:T(8,128)(2,1)S(1)}, u32[]{:S(2)}, u32[]{:S(2)}) collective-permute-start(bf16[704,128]{1,0:T(8,128)(2,1)S(1)} %pass_on.7), channel_id=1, source_target_pairs={{0,32},{1,35},{2,34},{3,33},{4,36},{5,39},{6,38},{7,37},{8,40},{9,... | collective-permute-start | bytes 540680 | tf_op jit(solution)/shard_map/ppermute | solution.py:32

commit v3 on v2

v3 whole, which is shorter than its diff:
```python
import functools
import math

import jax
import jax.numpy as jnp
from jax import lax
from jax.experimental import pallas as pl
from jax.experimental.pallas import tpu as pltpu
from jax.sharding import Mesh, PartitionSpec as P

BF = jnp.bfloat16
F32 = jnp.float32
AXES = ("y", "xl", "z", "xh", "c")
VMEM = pl.BlockSpec(memory_space=pltpu.VMEM)
SMEM = pl.BlockSpec(memory_space=pltpu.SMEM)
LANES = 128
OVER_COLUMNS = (((1,), (1,)), ((), ()))


def move(value, axis, hop):
    pairs = []
    for y in range(4):
        for x in range(4):
            for z in range(8):
                for c in range(2):
                    far = hop * (1 - 2 * c)
                    X = (x + far) % 4 if axis == "x" else x
                    Y = (y + far) % 4 if axis == "y" else y
                    C = 1 - c if axis == "c" else c
                    src = (y * 2 + x % 2) * 32 + z * 4 + (x // 2) * 2 + c
                    dst = (Y * 2 + X % 2) * 32 + z * 4 + (X // 2) * 2 + C
                    pairs.append((src, dst))
    return lax.ppermute(value, AXES, sorted(pairs))


def call(body, outs, scratch, name, *operands, limit=8, specs=None, gflop=0.02):
    return pl.pallas_call(
        body,
        out_shape=[jax.ShapeDtypeStruct(s, d) for s, d in outs],
        in_specs=specs or [SMEM] + [VMEM] * (len(operands) - 1),
        out_specs=[VMEM] * len(outs),
        scratch_shapes=scratch,
        name=name,
        cost_estimate=pl.CostEstimate(
            flops=int(gflop * 1e9), bytes_accessed=1 << 20, transcendentals=0
        ),
        compiler_params=pltpu.CompilerParams(vmem_limit_bytes=limit << 20),
    )(*operands)


SHARE = 144


def gelu_pass_body(
    pos, gain_any, patches_any, cot_any, stem_any, up_any, down_any,
    preact_grad, normal, inverse, mine, send,
    p, g, w, u, d, gain, t, sem,
):
    plan = [(patches_any, p), (cot_any, g)]
    for k in range(3):
        rows = pl.ds(k * 512, 512)
        plan.append((stem_any.at[rows], w.at[rows]))
    for k in range(2):
        cols = pl.ds(k * 1024, 1024)
        plan.append((up_any.at[:, cols], u.at[:, cols]))
        plan.append((down_any.at[cols], d.at[cols]))
    plan.append((gain_any, gain))
    order = [0, 2, 3, 4, 9, 5, 1, 6, 7, 8]
    copies = [pltpu.make_async_copy(src, dst, sem.at[k]) for k, (src, dst) in enumerate(plan)]
    for k in order:
        copies[k].start()

    copies[0].wait()
    acc = None
    for k in range(3):
        copies[2 + k].wait()
        part = jnp.dot(
            p[:, k * 512 : k * 512 + 512], w[k * 512 : k * 512 + 512], preferred_element_type=F32
        )
        acc = part if acc is None else acc + part
    copies[9].wait()
    embed = acc.astype(BF).astype(F32)
    center = jnp.mean(embed, axis=1, keepdims=True)
    shifted = embed - center
    scale = lax.rsqrt(jnp.mean(shifted * shifted, axis=1, keepdims=True) + 1e-06)
    norm = shifted * scale
    normal[...] = norm
    inverse[...] = scale
    normed = (norm * gain[...]).astype(BF)
    pt = p[...].T
    nt = normed.T
    for b in range(16):
        for half in range(2):
            at = b * 2 + half
            t[b, half, 64:96] = nt[at * 32 : at * 32 + 32]
            t[b, half, 96:144] = pt[at * 48 : at * 48 + 48]
    copies[1].wait()
    for j in range(8):
        if j % 4 == 0:
            copies[5 + j // 2].wait()
            copies[6 + j // 2].wait()
        cols = slice(j * 256, j * 256 + 256)
        pre = jnp.dot(normed, u[:, cols], preferred_element_type=F32)
        grad = lax.dot_general(g[...], d[cols], OVER_COLUMNS, preferred_element_type=F32)
        cdf = 0.5 * (1.0 + lax.erf(pre * math.sqrt(0.5)))
        slope = cdf + pre * jnp.exp(-0.5 * pre * pre) * (1.0 / math.sqrt(2.0 * math.pi))
        preact_grad[:, cols] = (grad * slope).astype(BF)
        ht = (pre * cdf).astype(BF).T
        for q in range(4):
            t[j * 2 + q // 2, q % 2, 0:64] = ht[q * 64 : q * 64 + 64]
    c = pos[3]
    mine[...] = t[:, c]
    send[...] = t[:, 1 - c]


def gelu_pass(pos, gain, patches, cotangent, stem_weight, up_weight, down_weight):
    outs = [((256, 2048), BF), ((256, 1024), F32), ((256, 1), F32)]
    return call(
        gelu_pass_body,
        outs + [((16, SHARE, 256), BF)] * 2,
        [
            pltpu.VMEM((256, 1536), BF),
            pltpu.VMEM((256, 1024), BF),
            pltpu.VMEM((1536, 1024), BF),
            pltpu.VMEM((1024, 2048), BF),
            pltpu.VMEM((2048, 1024), BF),
            pltpu.VMEM((1, 1024), F32),
            pltpu.VMEM((16, 2, SHARE, 256), BF),
            pltpu.SemaphoreType.DMA((10,)),
        ],
        "gelu_pass",
        pos,
        gain,
        patches,
        cotangent,
        stem_weight,
        up_weight,
        down_weight,
        limit=48,
        specs=[SMEM] + [pl.BlockSpec(memory_space=pl.ANY)] * 6,
        gflop=8,
    )


def norm_back_body(gain, preact_grad, up, cot, normal, inverse, embed_grad):
    grad = lax.dot_general(preact_grad[...], up[...], OVER_COLUMNS, preferred_element_type=F32)
    grad = grad * gain[...]
    norm = normal[...]
    first = jnp.mean(grad, axis=1, keepdims=True)
    second = jnp.mean(grad * norm, axis=1, keepdims=True)
    embed_grad[...] = (
        cot[...].astype(F32) + inverse[...] * (grad - first - norm * second)
    ).astype(BF)


ROWS = 176
CHUNK = 704


def chunk_of(me, pos, rel):
    return lax.rem(me + rel * (1 + 2 * pos[3]), 4)


def dot2(lefts, rights):
    acc = jnp.dot(lefts[0], rights[0], preferred_element_type=F32)
    acc += jnp.dot(lefts[1], rights[1], preferred_element_type=F32)
    return acc.astype(BF)


def columns(ref, starts, width):
    parts = [ref[:, pl.ds(pl.multiple_of(start, LANES), width)] for start in starts]
    return parts[0] if len(parts) == 1 else jnp.concatenate(parts, axis=1)


def terms_x_body(pos, lm, lr, cm, cr, gm, gr, *outs):
    for rel in range(4):
        to = chunk_of(pos[0], pos, rel)
        xh, xl = to // 2, lax.rem(to, 2)
        dst = outs[rel]
        acc = dot2(
            [ref[:, xh, 0:64].reshape(512, 256) for ref in (lm, lr)],
            [columns(ref, [xl * 512], 512) for ref in (cm, cr)],
        )
        for yy in range(4):
            dst[yy, 0:512] = acc[:, yy * 128 : yy * 128 + 128]
        acc = dot2(
            [ref[0:3, xh, 64:96].reshape(96, 256) for ref in (lm, lr)],
            [columns(ref, [(yy * 2 + xl) * 256 for yy in range(4)], 256) for ref in (gm, gr)],
        )
        for z in range(3):
            for yy in range(4):
                for k in range(2):
                    at, col = 512 + z * 64 + k * 32, (yy * 2 + k) * 128
                    dst[yy, at : at + 32] = acc[z * 32 : z * 32 + 32, col : col + 128]


def terms_y_body(pos, lm, lr, gm, gr, em, er, *outs):
    for rel in range(4):
        to = chunk_of(pos[1], pos, rel)
        dst = outs[rel]
        acc = dot2(
            [ref[3:8, :, 64:96].reshape(320, 256) for ref in (lm, lr)],
            [columns(ref, [to * 512], 512) for ref in (gm, gr)],
        )
        for z in range(5):
            for xx in range(4):
                for k in range(2):
                    row, col = (z * 2 + xx // 2) * 32, (xx % 2 * 2 + k) * 128
                    at = z * 64 + k * 32
                    dst[xx, at : at + 32] = acc[row : row + 32, col : col + 128]
        acc = dot2(
            [ref[:, :, 96:144].reshape(768, 256) for ref in (lm, lr)],
            [columns(ref, [to * 128, 512 + to * 128], 128) for ref in (em, er)],
        )
        for z in range(8):
            for xx in range(4):
                row, col = (z * 2 + xx // 2) * 48, xx % 2 * 128
                at = 320 + z * 48
                dst[xx, at : at + 48] = acc[row : row + 48, col : col + 128]


def pass_on_body(keep, got, out):
    out[...] = (keep[...].astype(F32) + got[...].astype(F32)).astype(BF)


def rings(axes, parts):
    result = []
    for axis, (own, keep, ahead, behind) in zip(axes, parts):
        got = move(ahead, axis, 1)
        near = move(behind, axis, -1)
        (total,) = call(
            pass_on_body, [(keep.shape, BF)], [], "pass_on", keep, got, specs=[VMEM, VMEM]
        )
        result += [own, near, move(total, axis, 1)]
    return result


def add3(a, b, c):
    return (a.astype(F32) + b.astype(F32) + c.astype(F32)).astype(BF)


def turn_body(pos, *refs):
    for p in range(2):
        a, b, c = refs[3 * p : 3 * p + 3]
        for rel in range(4):
            to = chunk_of(pos[1 - p], pos, rel)
            refs[6 + 4 * p + rel][...] = add3(a[to], b[to], c[to])


def reduce_xy(pos, parts):
    outs = call(
        turn_body, [((CHUNK, LANES), BF)] * 8, [], "ring_turn", pos, *rings("xy", parts)
    )
    return rings("yx", (outs[:4], outs[4:]))


def pack_body(*refs):
    out = refs[6]
    x, y = (add3(*(ref[...] for ref in refs[3 * p : 3 * p + 3])) for p in range(2))
    for z in range(8):
        out[z, 0:64] = x[z * 64 : z * 64 + 64]
        out[z, 64:128] = x[512 + z * 64 : 576 + z * 64] if z < 3 else y[z * 64 - 192 : z * 64 - 128]
        out[z, 128:176] = y[320 + z * 48 : 368 + z * 48]


def sum_body(got, out):
    total = got[0].astype(F32)
    for k in range(1, 8):
        total += got[k].astype(F32)
    share = total.astype(BF)
    for k in range(8):
        out[k] = share


def unpack_body(got, stem, up, down):
    for y in range(4):
        for xl in range(2):
            piece = got[y * 2 + xl].astype(F32)
            col = (xl * 4 + y) * LANES
            down[:, col : col + LANES] = piece[0:64]
            stem[:, col : col + LANES] = piece[128:176]
            col = (y * 2 + xl) * 256
            up[:, col : col + LANES] = piece[64:96]
            up[:, col + LANES : col + 256] = piece[96:128]


def finish(pieces):
    share = [((8, ROWS, LANES), BF)]
    (packed,) = call(pack_body, share, [], "z_pack", *pieces, specs=[VMEM] * 6)
    got = lax.all_to_all(packed, "z", 0, 0, tiled=True)
    (copies,) = call(sum_body, share, [], "z_sum", got, specs=[VMEM])
    every = lax.all_to_all(copies, ("y", "xl"), 0, 0, tiled=True)
    outs = [((48, 1024), F32), ((32, 2048), F32), ((64, 1024), F32)]
    return call(unpack_body, outs, [], "unpack", every, specs=[VMEM])


def local(patches, stem_weight, ln_gain, up_weight, down_weight, cotangent):
    x = lax.axis_index("xh") * 2 + lax.axis_index("xl")
    pos = jnp.stack([x, lax.axis_index("y"), lax.axis_index("z"), lax.axis_index("c")])
    pos = pos.astype(jnp.int32)

    gain = ln_gain.reshape(1, 1024)
    cot_other = move(cotangent, "c", 0)
    preact_grad, normal, inverse, mine, send = gelu_pass(
        pos, gain, patches, cotangent, stem_weight, up_weight, down_weight
    )
    other = move(send, "c", 0)
    preact_other = move(preact_grad, "c", 0)
    (embed_grad,) = call(
        norm_back_body,
        [((256, 1024), BF)],
        [],
        "norm_back",
        gain,
        preact_grad,
        up_weight,
        cotangent,
        normal,
        inverse,
        specs=[VMEM] * 6,
        limit=16,
        gflop=2,
    )
    embed_other = move(embed_grad, "c", 0)

    left = [v.reshape(8, 2, SHARE, 256) for v in (mine, other)]
    outs = [((4, CHUNK, LANES), BF)] * 4
    grads = (preact_grad, preact_other)
    part_x = call(
        terms_x_body, outs, [], "terms_x", pos, *left, cotangent, cot_other, *grads, limit=16, gflop=2
    )
    embed_other, *part_x = lax.optimization_barrier((embed_other, *part_x))
    part_y = call(
        terms_y_body, outs, [], "terms_y", pos, *left, *grads, embed_grad, embed_other, limit=16, gflop=2
    )
    return tuple(finish(reduce_xy(pos, (part_x, part_y))))


def solution(mesh):
    fine = Mesh(mesh.devices.reshape(4, 2, 8, 2, 2), AXES)
    rows = P(("z", "xh", "c"), None)
    in_specs = (P(AXES, None), P(), P(), P(), P(), P(AXES, None))
    return jax.shard_map(
        local, mesh=fine, in_specs=in_specs, out_specs=(rows, rows, rows), check_vma=False
    )
```

time: 107 us -> 102 us (0.953)
  matrix products: 5.78 us -> 0 us
  waiting for transfers between devices: 30.8 us -> 33.3 us
  other arithmetic: 2.02 us -> 0.08 us
  starting transfers between devices: 18.1 us -> 16.4 us
    dot_general x2 -> x0, matrix products: 5.78 us -> none  [the longest x1 3.31 us: local(): lax.dot_general(cotangent, down_weight, over_cols, preferred_element_type...]
    ppermute x16, waiting for transfers between devices: 30.8 us -> 33.3 us  [move(): return lax.ppermute(value, AXES, sorted(pairs))]
    convert_element_type x1 -> x0, other arithmetic: 1.84 us -> none  [local(): embed_grad = (cotangent.astype(F32) + inverse * (normal_grad - first_mean...]
    ppermute x16, starting transfers between devices: 18.1 us -> 16.4 us  [move(): return lax.ppermute(value, AXES, sorted(pairs))]
    unnamed x14 -> x8, local copies, waits for them, and re-layouts: 1.85 us -> 2.87 us
    pallas_call x10 -> x12, Pallas kernels: 15.2 us -> 16.2 us  [call(): pl.pallas_call(body, out_shape=[jax.ShapeDtypeStruct(s, d) for s, d in ou...]
  transfers between devices with their start and end apart: 16 -> 16, of which waited for: 9 -> 9; matrix products, arithmetic and copies ran while one was open for 7% -> 0% of each run, Pallas kernels for 8% -> 7%
where the time goes in v3:
time: 102 us; the launch traced here: 101 us
  waiting for transfers between devices  33.3 us (33%)
  blocking collectives  31.5 us (31%)
  starting transfers between devices  16.4 us (16%)
  Pallas kernels  16.2 us (16%)
  local copies, waits for them, and re-layouts  2.87 us (3%)
    ppermute x16, waiting for transfers between devices, move(): return lax.ppermute(value, AXES, sorted(pairs))  33.3 us
    all_to_all x1, blocking collectives, finish(): got = lax.all_to_all(packed, 'z', 0, 0, tiled=True)  19.8 us
    ppermute x16, starting transfers between devices, move(): return lax.ppermute(value, AXES, sorted(pairs))  16.4 us
    pallas_call x12, Pallas kernels, call(): pl.pallas_call(body, out_shape=[jax.ShapeDtypeStruct(s, d) for s, d in ou...  16.2 us
    all_to_all x1, blocking collectives, finish(): every = lax.all_to_all(copies, ('y', 'xl'), 0, 0, tiled=True)  11.7 us
    unnamed x8, local copies, waits for them, and re-layouts  2.87 us
  transfers between devices with their start and end apart: 16, of which 9 were waited for; matrix products, arithmetic and copies ran while one was open for 0% of the time, Pallas kernels for 7%

profile of v3, /device:TPU:4, one launch (start us, length us, event | category | flops | bytes accessed | tf_op | source)
XLA Modules:
  0.0 101.1 jit_solution(14671448821781972879)
XLA Ops:
  0.7 1.0 %copy-done.1 = bf16[256,1024]{1,0:T(8,128)(2,1)S(1)} copy-done((bf16[256,1024]{1,0:T(8,128)(2,1)S(1)}, bf16[256,1024]{1,0:T(8,128)(2,1)}, u32[]{:S(2)}) %copy-start.1) | copy-done | bytes 524312
  1.8 0.7 copy-done.2
  2.4 1.1 %copy-done.3 = bf16[256,1536]{1,0:T(8,128)(2,1)S(1)} copy-done((bf16[256,1536]{1,0:T(8,128)(2,1)S(1)}, bf16[256,1536]{1,0:T(8,128)(2,1)}, u32[]{:S(2)}) %copy-start.3) | copy-done | bytes 786456
  3.6 7.3 %gelu_pass.1 = (bf16[256,2048]{1,0:T(8,128)(2,1)S(1)}, f32[256,1024]{1,0:T(8,128)S(1)}, f32[256,1]{1,0:T(8,128)S(1)}, bf16[16,144,256]{2,1,0:T(8,128)(2,1)S(1)}, bf16[16,144,256]{2,1,0:T(8,128)(2,1)S(1)}) custom-call(s32[4]{0:T(128)S(1)} %pad_add_fusion.pos, f32[1,1024]{1,0:T(1,128)S(1)} %bitcast.7, bf16[256,1536]{1,0:T(8,128)(2,1)S(1)} %copy-done.3, ...), custom_call_target="tpu_custom_call" | custom-call | flops 8000000000 | bytes 1048576 | tf_op jit(solution)/shard_map/gelu_pass/pallas_call | solution.py:37
  11.0 0.5 collective-permute-start.3
  11.6 1.6 %norm_back.1.em = bf16[256,1024]{1,0:T(8,128)(2,1)S(1)} custom-call(f32[1,1024]{1,0:T(1,128)S(1)} %bitcast.8, bf16[256,2048]{1,0:T(8,128)(2,1)S(1)} %get-tuple-element.29.preact_grad.gm, bf16[1024,2048]{1,0:T(8,128)(2,1)S(1)} %copy-done, bf16[256,1024]{1,0:T(8,128)(2,1)S(1)} %copy-done.1, f32[256,1024]{1,0:T(8,128)S(1)} %get-tuple-element.30.normal, ...), custom_call_target="tpu_custom_call" | custom-call | flops 2000000000 | bytes 1048576 | tf_op jit(solution)/shard_map/norm_back/pallas_call | solution.py:37
  13.2 0.5 collective-permute-start
  13.7 2.4 %collective-permute-done.2.cr = bf16[256,1024]{1,0:T(8,128)(2,1)S(1)} collective-permute-done((bf16[256,1024]{1,0:T(8,128)(2,1)S(1)}, bf16[256,1024]{1,0:T(8,128)(2,1)S(1)}, u32[]{:S(2)}, u32[]{:S(2)}) %collective-permute-start.2) | collective-permute-done | bytes 524320 | tf_op jit(solution)/shard_map/ppermute | solution.py:33
  16.1 2.5 %terms_x.1 = (bf16[4,704,128]{2,1,0:T(8,128)(2,1)S(1)}, bf16[4,704,128]{2,1,0:T(8,128)(2,1)S(1)}, bf16[4,704,128]{2,1,0:T(8,128)(2,1)S(1)}, bf16[4,704,128]{2,1,0:T(8,128)(2,1)S(1)}) custom-call(s32[4]{0:T(128)S(1)} %pad_add_fusion.pos, bf16[8,2,144,256]{3,2,1,0:T(8,128)(2,1)S(1)} %bitcast.11, bf16[8,2,144,256]{3,2,1,0:T(8,128)(2,1)S(1)} %bitcast.9, ...), custom_call_target="tpu_custom_call" | custom-call | flops 2000000000 | bytes 1048576 | tf_op jit(solution)/shard_map/terms_x/pallas_call | solution.py:37
  18.6 1.3 %collective-permute-start.5 = (bf16[4,704,128]{2,1,0:T(8,128)(2,1)S(1)}, bf16[4,704,128]{2,1,0:T(8,128)(2,1)S(1)}, u32[]{:S(2)}, u32[]{:S(2)}) collective-permute-start(bf16[4,704,128]{2,1,0:T(8,128)(2,1)S(1)} %get-tuple-element.41), channel_id=1, source_target_pairs={{0,32},{1,35},{2,34},{3,33},{4,36},{5,39},{6,38},{7,37},{8,40},{9,... | collective-permute-start | bytes 2162696 | tf_op jit(solution)/shard_map/ppermute | solution.py:33
  19.9 2.2 %terms_y.1 = (bf16[4,704,128]{2,1,0:T(8,128)(2,1)S(1)}, bf16[4,704,128]{2,1,0:T(8,128)(2,1)S(1)}, bf16[4,704,128]{2,1,0:T(8,128)(2,1)S(1)}, bf16[4,704,128]{2,1,0:T(8,128)(2,1)S(1)}) custom-call(s32[4]{0:T(128)S(1)} %pad_add_fusion.pos, bf16[8,2,144,256]{3,2,1,0:T(8,128)(2,1)S(1)} %bitcast.12, bf16[8,2,144,256]{3,2,1,0:T(8,128)(2,1)S(1)} %bitcast.10, ...), custom_call_target="tpu_custom_call" | custom-call | flops 2000000000 | bytes 1048576 | tf_op jit(solution)/shard_map/terms_y/pallas_call | solution.py:37
  22.2 1.8 %collective-permute-start.8 = (bf16[4,704,128]{2,1,0:T(8,128)(2,1)S(1)}, bf16[4,704,128]{2,1,0:T(8,128)(2,1)S(1)}, u32[]{:S(2)}, u32[]{:S(2)}) collective-permute-start(bf16[4,704,128]{2,1,0:T(8,128)(2,1)S(1)} %get-tuple-element.46), channel_id=1, source_target_pairs={{0,64},{1,193},{2,66},{3,195},{4,68},{5,197},{6,70},{7,199},{8,72}... | collective-permute-start | bytes 2162696 | tf_op jit(solution)/shard_map/ppermute | solution.py:33
  24.0 0.8 collective-permute-start.4
  24.8 1.7 %collective-permute-start.7 = (bf16[4,704,128]{2,1,0:T(8,128)(2,1)S(1)}, bf16[4,704,128]{2,1,0:T(8,128)(2,1)S(1)}, u32[]{:S(2)}, u32[]{:S(2)}) collective-permute-start(bf16[4,704,128]{2,1,0:T(8,128)(2,1)S(1)} %get-tuple-element.44), channel_id=1, source_target_pairs={{0,192},{1,65},{2,194},{3,67},{4,196},{5,69},{6,198},{7,71},{8,200... | collective-permute-start | bytes 2162696 | tf_op jit(solution)/shard_map/ppermute | solution.py:33
  26.5 6.5 %collective-permute-done.5.got = bf16[4,704,128]{2,1,0:T(8,128)(2,1)S(1)} collective-permute-done((bf16[4,704,128]{2,1,0:T(8,128)(2,1)S(1)}, bf16[4,704,128]{2,1,0:T(8,128)(2,1)S(1)}, u32[]{:S(2)}, u32[]{:S(2)}) %collective-permute-start.5) | collective-permute-done | bytes 720928 | tf_op jit(solution)/shard_map/ppermute | solution.py:33
  33.2 1.0 collective-permute-start.6
  34.1 6.2 %collective-permute-done.8.got = bf16[4,704,128]{2,1,0:T(8,128)(2,1)S(1)} collective-permute-done((bf16[4,704,128]{2,1,0:T(8,128)(2,1)S(1)}, bf16[4,704,128]{2,1,0:T(8,128)(2,1)S(1)}, u32[]{:S(2)}, u32[]{:S(2)}) %collective-permute-start.8) | collective-permute-done | bytes 720928 | tf_op jit(solution)/shard_map/ppermute | solution.py:33
  40.6 1.8 %collective-permute-start.9 = (bf16[4,704,128]{2,1,0:T(8,128)(2,1)S(1)}, bf16[4,704,128]{2,1,0:T(8,128)(2,1)S(1)}, u32[]{:S(2)}, u32[]{:S(2)}) collective-permute-start(bf16[4,704,128]{2,1,0:T(8,128)(2,1)S(1)} %pass_on.5), channel_id=1, source_target_pairs={{0,64},{1,193},{2,66},{3,195},{4,68},{5,197},{6,70},{7,199},{8,72}... | collective-permute-start | bytes 2162696 | tf_op jit(solution)/shard_map/ppermute | solution.py:33
  42.4 3.0 %collective-permute-done.6.refs_2_ = bf16[4,704,128]{2,1,0:T(8,128)(2,1)S(1)} collective-permute-done((bf16[4,704,128]{2,1,0:T(8,128)(2,1)S(1)}, bf16[4,704,128]{2,1,0:T(8,128)(2,1)S(1)}, u32[]{:S(2)}, u32[]{:S(2)}) %collective-permute-start.6) | collective-permute-done | bytes 720928 | tf_op jit(solution)/shard_map/ppermute | solution.py:33
  45.4 8.4 %collective-permute-done.9.refs_5_ = bf16[4,704,128]{2,1,0:T(8,128)(2,1)S(1)} collective-permute-done((bf16[4,704,128]{2,1,0:T(8,128)(2,1)S(1)}, bf16[4,704,128]{2,1,0:T(8,128)(2,1)S(1)}, u32[]{:S(2)}, u32[]{:S(2)}) %collective-permute-start.9) | collective-permute-done | bytes 720928 | tf_op jit(solution)/shard_map/ppermute | solution.py:33
  53.9 1.1 %ring_turn.1 = (bf16[704,128]{1,0:T(8,128)(2,1)S(1)}, bf16[704,128]{1,0:T(8,128)(2,1)S(1)}, bf16[704,128]{1,0:T(8,128)(2,1)S(1)}, bf16[704,128]{1,0:T(8,128)(2,1...) custom-call(s32[4]{0:T(128)S(1)} %pad_add_fusion.pos, ...), custom_call_target="tpu_custom_call" | custom-call | flops 20000000 | bytes 1048576 | tf_op jit(solution)/shard_map/ring_turn/pallas_call | solution.py:37
  55.0 1.4 %collective-permute-start.14 = (bf16[704,128]{1,0:T(8,128)(2,1)S(1)}, bf16[704,128]{1,0:T(8,128)(2,1)S(1)}, u32[]{:S(2)}, u32[]{:S(2)}) collective-permute-start(bf16[704,128]{1,0:T(8,128)(2,1)S(1)} %get-tuple-element.54), channel_id=1, source_target_pairs={{0,32},{1,35},{2,34},{3,33},{4,36},{5,39},{6,38},{7,37},{8,40},{9,... | collective-permute-start | bytes 540680 | tf_op jit(solution)/shard_map/ppermute | solution.py:33
  56.4 3.1 %collective-permute-start.10 = (bf16[704,128]{1,0:T(8,128)(2,1)S(1)}, bf16[704,128]{1,0:T(8,128)(2,1)S(1)}, u32[]{:S(2)}, u32[]{:S(2)}) collective-permute-start(bf16[704,128]{1,0:T(8,128)(2,1)S(1)} %get-tuple-element.48), channel_id=1, source_target_pairs={{0,192},{1,65},{2,194},{3,67},{4,196},{5,69},{6,198},{7,71},{8,200... | collective-permute-start | bytes 540680 | tf_op jit(solution)/shard_map/ppermute | solution.py:33
  59.5 0.7 collective-permute-start.13
  60.3 1.4 %collective-permute-done.11.got = bf16[704,128]{1,0:T(8,128)(2,1)S(1)} collective-permute-done((bf16[704,128]{1,0:T(8,128)(2,1)S(1)}, bf16[704,128]{1,0:T(8,128)(2,1)S(1)}, u32[]{:S(2)}, u32[]{:S(2)}) %collective-permute-start.11) | collective-permute-done | bytes 180256 | tf_op jit(solution)/shard_map/ppermute | solution.py:33
  61.9 1.4 %collective-permute-start.15 = (bf16[704,128]{1,0:T(8,128)(2,1)S(1)}, bf16[704,128]{1,0:T(8,128)(2,1)S(1)}, u32[]{:S(2)}, u32[]{:S(2)}) collective-permute-start(bf16[704,128]{1,0:T(8,128)(2,1)S(1)} %pass_on.7), channel_id=1, source_target_pairs={{0,32},{1,35},{2,34},{3,33},{4,36},{5,39},{6,38},{7,37},{8,40},{9,... | collective-permute-start | bytes 540680 | tf_op jit(solution)/shard_map/ppermute | solution.py:33
  63.3 0.2 collective-permute-done.10.refs_1_
  63.5 2.3 %collective-permute-done.13.refs_4_ = bf16[704,128]{1,0:T(8,128)(2,1)S(1)} collective-permute-done((bf16[704,128]{1,0:T(8,128)(2,1)S(1)}, bf16[704,128]{1,0:T(8,128)(2,1)S(1)}, u32[]{:S(2)}, u32[]{:S(2)}) %collective-permute-start.13) | collective-permute-done | bytes 180256 | tf_op jit(solution)/shard_map/ppermute | solution.py:33
  65.8 2.7 %collective-permute-done.12.refs_2_ = bf16[704,128]{1,0:T(8,128)(2,1)S(1)} collective-permute-done((bf16[704,128]{1,0:T(8,128)(2,1)S(1)}, bf16[704,128]{1,0:T(8,128)(2,1)S(1)}, u32[]{:S(2)}, u32[]{:S(2)}) %collective-permute-start.12) | collective-permute-done | bytes 180256 | tf_op jit(solution)/shard_map/ppermute | solution.py:33
  68.7 19.8 %all_to_all.10.got = bf16[8,176,128]{2,1,0:T(8,128)(2,1)S(1)} all-to-all(bf16[8,176,128]{2,1,0:T(8,128)(2,1)S(1)} %z_pack.1), channel_id=1, replica_groups=mesh['y'=4,'xl'=2,'z'=8,'xh'=2,'c'=2] {'z'}, dimensions={0} | all-to-all | bytes 720896 | tf_op jit(solution)/shard_map/all_to_all | solution.py:290
  88.5 11.7 %all_to_all.11.got = bf16[8,176,128]{2,1,0:T(8,128)(2,1)S(1)} all-to-all(bf16[8,176,128]{2,1,0:T(8,128)(2,1)S(1)} %z_sum.1), channel_id=1, replica_groups=mesh['y'=4,'xl'=2,'z'=8,'xh'=2,'c'=2] {'y','xl'}, dimensions={0} | all-to-all | bytes 720896 | tf_op jit(solution)/shard_map/all_to_all | solution.py:292
  100.2 0.9 unpack.1
  (23 shorter events, 1.1 us)
Async XLA Ops:
  0.7 1.0 %copy-start.1 = (bf16[256,1024]{1,0:T(8,128)(2,1)S(1)}, bf16[256,1024]{1,0:T(8,128)(2,1)}, u32[]{:S(2)}) copy-start(bf16[256,1024]{1,0:T(8,128)(2,1)} %cm.1) | copy-start | bytes 1572868
  1.8 0.7 copy-start.2
  2.4 1.1 %copy-start.3 = (bf16[256,1536]{1,0:T(8,128)(2,1)S(1)}, bf16[256,1536]{1,0:T(8,128)(2,1)}, u32[]{:S(2)}) copy-start(bf16[256,1536]{1,0:T(8,128)(2,1)} %patches_any.1) | copy-start | bytes 2359300
  3.6 8.1 %copy-start = (bf16[1024,2048]{1,0:T(8,128)(2,1)S(1)}, bf16[1024,2048]{1,0:T(8,128)(2,1)}, u32[]{:S(2)}) copy-start(bf16[1024,2048]{1,0:T(8,128)(2,1)} %up.1) | copy-start | bytes 12582916
  10.9 5.2 %collective-permute-start.1 = (bf16[16,144,256]{2,1,0:T(8,128)(2,1)S(1)}, bf16[16,144,256]{2,1,0:T(8,128)(2,1)S(1)}, u32[]{:S(2)}, u32[]{:S(2)}) collective-permute-start(bf16[16,144,256]{2,1,0:T(8,128)(2,1)S(1)} %get-tuple-element.33), channel_id=1, source_target_pairs={{0,1},{1,0},{2,3},{3,2},{4,5},{5,4},{6,7},{7,6},{8,9},{9,8},{10,11... | collective-permute-start | bytes 3538952 | tf_op jit(solution)/shard_map/ppermute | solution.py:33
  11.0 5.1 %collective-permute-start.3 = (bf16[256,2048]{1,0:T(8,128)(2,1)S(1)}, bf16[256,2048]{1,0:T(8,128)(2,1)S(1)}, u32[]{:S(2)}, u32[]{:S(2)}) collective-permute-start(bf16[256,2048]{1,0:T(8,128)(2,1)S(1)} %get-tuple-element.29.preact_grad.gm), channel_id=1, source_target_pairs={{0,1},{1,0},{2,3},{3,2},{4,5},{5,4},{6,7},{7,6},{8,9},{9,8},{10,11... | collective-permute-start | bytes 3145736 | tf_op jit(solution)/shard_map/ppermute | solution.py:33
  11.5 4.6 %collective-permute-start.2 = (bf16[256,1024]{1,0:T(8,128)(2,1)S(1)}, bf16[256,1024]{1,0:T(8,128)(2,1)S(1)}, u32[]{:S(2)}, u32[]{:S(2)}) collective-permute-start(bf16[256,1024]{1,0:T(8,128)(2,1)S(1)} %copy-done.1), channel_id=1, source_target_pairs={{0,1},{1,0},{2,3},{3,2},{4,5},{5,4},{6,7},{7,6},{8,9},{9,8},{10,11... | collective-permute-start | bytes 1572872 | tf_op jit(solution)/shard_map/ppermute | solution.py:33
  13.2 5.4 %collective-permute-start = (bf16[256,1024]{1,0:T(8,128)(2,1)S(1)}, bf16[256,1024]{1,0:T(8,128)(2,1)S(1)}, u32[]{:S(2)}, u32[]{:S(2)}) collective-permute-start(bf16[256,1024]{1,0:T(8,128)(2,1)S(1)} %norm_back.1.em), channel_id=1, source_target_pairs={{0,1},{1,0},{2,3},{3,2},{4,5},{5,4},{6,7},{7,6},{8,9},{9,8},{10,11... | collective-permute-start | bytes 1572872 | tf_op jit(solution)/shard_map/ppermute | solution.py:33
  18.6 14.4 %collective-permute-start.5 = (bf16[4,704,128]{2,1,0:T(8,128)(2,1)S(1)}, bf16[4,704,128]{2,1,0:T(8,128)(2,1)S(1)}, u32[]{:S(2)}, u32[]{:S(2)}) collective-permute-start(bf16[4,704,128]{2,1,0:T(8,128)(2,1)S(1)} %get-tuple-element.41), channel_id=1, source_target_pairs={{0,32},{1,35},{2,34},{3,33},{4,36},{5,39},{6,38},{7,37},{8,40},{9,... | collective-permute-start | bytes 2162696 | tf_op jit(solution)/shard_map/ppermute | solution.py:33
  22.2 18.2 %collective-permute-start.8 = (bf16[4,704,128]{2,1,0:T(8,128)(2,1)S(1)}, bf16[4,704,128]{2,1,0:T(8,128)(2,1)S(1)}, u32[]{:S(2)}, u32[]{:S(2)}) collective-permute-start(bf16[4,704,128]{2,1,0:T(8,128)(2,1)S(1)} %get-tuple-element.46), channel_id=1, source_target_pairs={{0,64},{1,193},{2,66},{3,195},{4,68},{5,197},{6,70},{7,199},{8,72}... | collective-permute-start | bytes 2162696 | tf_op jit(solution)/shard_map/ppermute | solution.py:33
  24.0 18.4 %collective-permute-start.4 = (bf16[4,704,128]{2,1,0:T(8,128)(2,1)S(1)}, bf16[4,704,128]{2,1,0:T(8,128)(2,1)S(1)}, u32[]{:S(2)}, u32[]{:S(2)}) collective-permute-start(bf16[4,704,128]{2,1,0:T(8,128)(2,1)S(1)} %get-tuple-element.39), channel_id=1, source_target_pairs={{0,34},{1,33},{2,32},{3,35},{4,38},{5,37},{6,36},{7,39},{8,42},{9,... | collective-permute-start | bytes 2162696 | tf_op jit(solution)/shard_map/ppermute | solution.py:33
  24.8 17.6 %collective-permute-start.7 = (bf16[4,704,128]{2,1,0:T(8,128)(2,1)S(1)}, bf16[4,704,128]{2,1,0:T(8,128)(2,1)S(1)}, u32[]{:S(2)}, u32[]{:S(2)}) collective-permute-start(bf16[4,704,128]{2,1,0:T(8,128)(2,1)S(1)} %get-tuple-element.44), channel_id=1, source_target_pairs={{0,192},{1,65},{2,194},{3,67},{4,196},{5,69},{6,198},{7,71},{8,200... | collective-permute-start | bytes 2162696 | tf_op jit(solution)/shard_map/ppermute | solution.py:33
  33.2 12.3 %collective-permute-start.6 = (bf16[4,704,128]{2,1,0:T(8,128)(2,1)S(1)}, bf16[4,704,128]{2,1,0:T(8,128)(2,1)S(1)}, u32[]{:S(2)}, u32[]{:S(2)}) collective-permute-start(bf16[4,704,128]{2,1,0:T(8,128)(2,1)S(1)} %pass_on.4), channel_id=1, source_target_pairs={{0,32},{1,35},{2,34},{3,33},{4,36},{5,39},{6,38},{7,37},{8,40},{9,... | collective-permute-start | bytes 2162696 | tf_op jit(solution)/shard_map/ppermute | solution.py:33
  40.6 13.3 %collective-permute-start.9 = (bf16[4,704,128]{2,1,0:T(8,128)(2,1)S(1)}, bf16[4,704,128]{2,1,0:T(8,128)(2,1)S(1)}, u32[]{:S(2)}, u32[]{:S(2)}) collective-permute-start(bf16[4,704,128]{2,1,0:T(8,128)(2,1)S(1)} %pass_on.5), channel_id=1, source_target_pairs={{0,64},{1,193},{2,66},{3,195},{4,68},{5,197},{6,70},{7,199},{8,72}... | collective-permute-start | bytes 2162696 | tf_op jit(solution)/shard_map/ppermute | solution.py:33
  54.9 6.8 %collective-permute-start.11 = (bf16[704,128]{1,0:T(8,128)(2,1)S(1)}, bf16[704,128]{1,0:T(8,128)(2,1)S(1)}, u32[]{:S(2)}, u32[]{:S(2)}) collective-permute-start(bf16[704,128]{1,0:T(8,128)(2,1)S(1)} %get-tuple-element.50), channel_id=1, source_target_pairs={{0,64},{1,193},{2,66},{3,195},{4,68},{5,197},{6,70},{7,199},{8,72}... | collective-permute-start | bytes 540680 | tf_op jit(solution)/shard_map/ppermute | solution.py:33
  55.0 6.8 %collective-permute-start.14 = (bf16[704,128]{1,0:T(8,128)(2,1)S(1)}, bf16[704,128]{1,0:T(8,128)(2,1)S(1)}, u32[]{:S(2)}, u32[]{:S(2)}) collective-permute-start(bf16[704,128]{1,0:T(8,128)(2,1)S(1)} %get-tuple-element.54), channel_id=1, source_target_pairs={{0,32},{1,35},{2,34},{3,33},{4,36},{5,39},{6,38},{7,37},{8,40},{9,... | collective-permute-start | bytes 540680 | tf_op jit(solution)/shard_map/ppermute | solution.py:33
  56.4 7.1 %collective-permute-start.10 = (bf16[704,128]{1,0:T(8,128)(2,1)S(1)}, bf16[704,128]{1,0:T(8,128)(2,1)S(1)}, u32[]{:S(2)}, u32[]{:S(2)}) collective-permute-start(bf16[704,128]{1,0:T(8,128)(2,1)S(1)} %get-tuple-element.48), channel_id=1, source_target_pairs={{0,192},{1,65},{2,194},{3,67},{4,196},{5,69},{6,198},{7,71},{8,200... | collective-permute-start | bytes 540680 | tf_op jit(solution)/shard_map/ppermute | solution.py:33
  59.5 6.3 %collective-permute-start.13 = (bf16[704,128]{1,0:T(8,128)(2,1)S(1)}, bf16[704,128]{1,0:T(8,128)(2,1)S(1)}, u32[]{:S(2)}, u32[]{:S(2)}) collective-permute-start(bf16[704,128]{1,0:T(8,128)(2,1)S(1)} %get-tuple-element.52), channel_id=1, source_target_pairs={{0,34},{1,33},{2,32},{3,35},{4,38},{5,37},{6,36},{7,39},{8,42},{9,... | collective-permute-start | bytes 540680 | tf_op jit(solution)/shard_map/ppermute | solution.py:33
  61.8 6.8 %collective-permute-start.12 = (bf16[704,128]{1,0:T(8,128)(2,1)S(1)}, bf16[704,128]{1,0:T(8,128)(2,1)S(1)}, u32[]{:S(2)}, u32[]{:S(2)}) collective-permute-start(bf16[704,128]{1,0:T(8,128)(2,1)S(1)} %pass_on.6), channel_id=1, source_target_pairs={{0,64},{1,193},{2,66},{3,195},{4,68},{5,197},{6,70},{7,199},{8,72}... | collective-permute-start | bytes 540680 | tf_op jit(solution)/shard_map/ppermute | solution.py:33
  61.9 6.6 %collective-permute-start.15 = (bf16[704,128]{1,0:T(8,128)(2,1)S(1)}, bf16[704,128]{1,0:T(8,128)(2,1)S(1)}, u32[]{:S(2)}, u32[]{:S(2)}) collective-permute-start(bf16[704,128]{1,0:T(8,128)(2,1)S(1)} %pass_on.7), channel_id=1, source_target_pairs={{0,32},{1,35},{2,34},{3,33},{4,36},{5,39},{6,38},{7,37},{8,40},{9,... | collective-permute-start | bytes 540680 | tf_op jit(solution)/shard_map/ppermute | solution.py:33

commit v4 on v3

--- a/solution.py
+++ b/solution.py
@@ -52,11 +52,11 @@
 
 
 def gelu_pass_body(
-    pos, gain_any, patches_any, cot_any, stem_any, up_any, down_any,
+    pos, gain, p, g, stem_any, up_any, down_any,
     preact_grad, normal, inverse, mine, send,
-    p, g, w, u, d, gain, t, sem,
+    w, u, d, t, sem,
 ):
-    plan = [(patches_any, p), (cot_any, g)]
+    plan = []
     for k in range(3):
         rows = pl.ds(k * 512, 512)
         plan.append((stem_any.at[rows], w.at[rows]))
@@ -64,21 +64,22 @@
         cols = pl.ds(k * 1024, 1024)
         plan.append((up_any.at[:, cols], u.at[:, cols]))
         plan.append((down_any.at[cols], d.at[cols]))
-    plan.append((gain_any, gain))
-    order = [0, 2, 3, 4, 9, 5, 1, 6, 7, 8]
     copies = [pltpu.make_async_copy(src, dst, sem.at[k]) for k, (src, dst) in enumerate(plan)]
-    for k in order:
-        copies[k].start()
-
-    copies[0].wait()
+    for copy in copies:
+        copy.start()
+
+    pt = p[...].T
+    for b in range(16):
+        for half in range(2):
+            at = (b * 2 + half) * 48
+            t[b, half, 96:144] = pt[at : at + 48]
     acc = None
     for k in range(3):
-        copies[2 + k].wait()
+        copies[k].wait()
         part = jnp.dot(
             p[:, k * 512 : k * 512 + 512], w[k * 512 : k * 512 + 512], preferred_element_type=F32
         )
         acc = part if acc is None else acc + part
-    copies[9].wait()
     embed = acc.astype(BF).astype(F32)
     center = jnp.mean(embed, axis=1, keepdims=True)
     shifted = embed - center
@@ -87,18 +88,15 @@
     normal[...] = norm
     inverse[...] = scale
     normed = (norm * gain[...]).astype(BF)
-    pt = p[...].T
     nt = normed.T
     for b in range(16):
         for half in range(2):
             at = b * 2 + half
             t[b, half, 64:96] = nt[at * 32 : at * 32 + 32]
-            t[b, half, 96:144] = pt[at * 48 : at * 48 + 48]
-    copies[1].wait()
     for j in range(8):
         if j % 4 == 0:
-            copies[5 + j // 2].wait()
-            copies[6 + j // 2].wait()
+            copies[3 + j // 2].wait()
+            copies[4 + j // 2].wait()
         cols = slice(j * 256, j * 256 + 256)
         pre = jnp.dot(normed, u[:, cols], preferred_element_type=F32)
         grad = lax.dot_general(g[...], d[cols], OVER_COLUMNS, preferred_element_type=F32)
@@ -119,14 +117,11 @@
         gelu_pass_body,
         outs + [((16, SHARE, 256), BF)] * 2,
         [
-            pltpu.VMEM((256, 1536), BF),
-            pltpu.VMEM((256, 1024), BF),
             pltpu.VMEM((1536, 1024), BF),
             pltpu.VMEM((1024, 2048), BF),
             pltpu.VMEM((2048, 1024), BF),
-            pltpu.VMEM((1, 1024), F32),
             pltpu.VMEM((16, 2, SHARE, 256), BF),
-            pltpu.SemaphoreType.DMA((10,)),
+            pltpu.SemaphoreType.DMA((7,)),
         ],
         "gelu_pass",
         pos,
@@ -137,7 +132,7 @@
         up_weight,
         down_weight,
         limit=48,
-        specs=[SMEM] + [pl.BlockSpec(memory_space=pl.ANY)] * 6,
+        specs=[SMEM] + [VMEM] * 3 + [pl.BlockSpec(memory_space=pl.ANY)] * 3,
         gflop=8,
     )
 
@@ -154,7 +149,9 @@
 
 
 ROWS = 176
-CHUNK = 704
+SPLIT = 4
+CHUNK_X = 512 + SPLIT * 64
+CHUNK_Y = (8 - SPLIT) * 64 + 384
 
 
 def chunk_of(me, pos, rel):
@@ -184,10 +181,10 @@
         for yy in range(4):
             dst[yy, 0:512] = acc[:, yy * 128 : yy * 128 + 128]
         acc = dot2(
-            [ref[0:3, xh, 64:96].reshape(96, 256) for ref in (lm, lr)],
+            [ref[0:SPLIT, xh, 64:96].reshape(SPLIT * 32, 256) for ref in (lm, lr)],
             [columns(ref, [(yy * 2 + xl) * 256 for yy in range(4)], 256) for ref in (gm, gr)],
         )
-        for z in range(3):
+        for z in range(SPLIT):
             for yy in range(4):
                 for k in range(2):
                     at, col = 512 + z * 64 + k * 32, (yy * 2 + k) * 128
@@ -199,10 +196,10 @@
         to = chunk_of(pos[1], pos, rel)
         dst = outs[rel]
         acc = dot2(
-            [ref[3:8, :, 64:96].reshape(320, 256) for ref in (lm, lr)],
+            [ref[SPLIT:8, :, 64:96].reshape((8 - SPLIT) * 64, 256) for ref in (lm, lr)],
             [columns(ref, [to * 512], 512) for ref in (gm, gr)],
         )
-        for z in range(5):
+        for z in range(8 - SPLIT):
             for xx in range(4):
                 for k in range(2):
                     row, col = (z * 2 + xx // 2) * 32, (xx % 2 * 2 + k) * 128
@@ -215,7 +212,7 @@
         for z in range(8):
             for xx in range(4):
                 row, col = (z * 2 + xx // 2) * 48, xx % 2 * 128
-                at = 320 + z * 48
+                at = CHUNK_Y - 384 + z * 48
                 dst[xx, at : at + 48] = acc[row : row + 48, col : col + 128]
 
 
@@ -248,9 +245,8 @@
 
 
 def reduce_xy(pos, parts):
-    outs = call(
-        turn_body, [((CHUNK, LANES), BF)] * 8, [], "ring_turn", pos, *rings("xy", parts)
-    )
+    outs = [((CHUNK_X, LANES), BF)] * 4 + [((CHUNK_Y, LANES), BF)] * 4
+    outs = call(turn_body, outs, [], "ring_turn", pos, *rings("xy", parts))
     return rings("yx", (outs[:4], outs[4:]))
 
 
@@ -259,8 +255,10 @@
     x, y = (add3(*(ref[...] for ref in refs[3 * p : 3 * p + 3])) for p in range(2))
     for z in range(8):
         out[z, 0:64] = x[z * 64 : z * 64 + 64]
-        out[z, 64:128] = x[512 + z * 64 : 576 + z * 64] if z < 3 else y[z * 64 - 192 : z * 64 - 128]
-        out[z, 128:176] = y[320 + z * 48 : 368 + z * 48]
+        up, at = (x, 512 + z * 64) if z < SPLIT else (y, (z - SPLIT) * 64)
+        out[z, 64:128] = up[at : at + 64]
+        at = CHUNK_Y - 384 + z * 48
+        out[z, 128:176] = y[at : at + 48]
 
 
 def sum_body(got, out):
@@ -324,14 +322,14 @@
     embed_other = move(embed_grad, "c", 0)
 
     left = [v.reshape(8, 2, SHARE, 256) for v in (mine, other)]
-    outs = [((4, CHUNK, LANES), BF)] * 4
+    outs_x, outs_y = ([((4, rows, LANES), BF)] * 4 for rows in (CHUNK_X, CHUNK_Y))
     grads = (preact_grad, preact_other)
     part_x = call(
-        terms_x_body, outs, [], "terms_x", pos, *left, cotangent, cot_other, *grads, limit=16, gflop=2
+        terms_x_body, outs_x, [], "terms_x", pos, *left, cotangent, cot_other, *grads, limit=16, gflop=2
     )
     embed_other, *part_x = lax.optimization_barrier((embed_other, *part_x))
     part_y = call(
-        terms_y_body, outs, [], "terms_y", pos, *left, *grads, embed_grad, embed_other, limit=16, gflop=2
+        terms_y_body, outs_y, [], "terms_y", pos, *left, *grads, embed_grad, embed_other, limit=16, gflop=2
     )
     return tuple(finish(reduce_xy(pos, (part_x, part_y))))
 

time: 102 us -> 108 us (1.059)
  blocking collectives: 31.5 us -> 37.3 us
  starting transfers between devices: 16.4 us -> 18.2 us
    all_to_all x1, blocking collectives: 11.7 us -> 16.1 us  [finish(): every = lax.all_to_all(copies, ('y', 'xl'), 0, 0, tiled=True)]
    ppermute x16, starting transfers between devices: 16.4 us -> 18.2 us  [move(): return lax.ppermute(value, AXES, sorted(pairs))]
    all_to_all x1, blocking collectives: 19.8 us -> 21.2 us  [finish(): got = lax.all_to_all(packed, 'z', 0, 0, tiled=True)]
  transfers between devices with their start and end apart: 16 -> 16, of which waited for: 9 -> 8; matrix products, arithmetic and copies ran while one was open for 0% -> 0% of each run, Pallas kernels for 7% -> 6%
where the time goes in v4:
time: 108 us
  blocking collectives  37.3 us (35%)
  waiting for transfers between devices  33.1 us (31%)
  starting transfers between devices  18.2 us (17%)
  Pallas kernels  15.8 us (15%)
  local copies, waits for them, and re-layouts  2.87 us (3%)
    ppermute x16, waiting for transfers between devices, move(): return lax.ppermute(value, AXES, sorted(pairs))  33.1 us
    all_to_all x1, blocking collectives, finish(): got = lax.all_to_all(packed, 'z', 0, 0, tiled=True)  21.2 us
    ppermute x16, starting transfers between devices, move(): return lax.ppermute(value, AXES, sorted(pairs))  18.2 us
    all_to_all x1, blocking collectives, finish(): every = lax.all_to_all(copies, ('y', 'xl'), 0, 0, tiled=True)  16.1 us
    pallas_call x12, Pallas kernels, call(): pl.pallas_call(body, out_shape=[jax.ShapeDtypeStruct(s, d) for s, d in ou...  15.8 us
    unnamed x8, local copies, waits for them, and re-layouts  2.87 us
  transfers between devices with their start and end apart: 16, of which 8 were waited for; matrix products, arithmetic and copies ran while one was open for 0% of the time, Pallas kernels for 6%

profile of v4, /device:TPU:4, one launch (start us, length us, event | category | flops | bytes accessed | tf_op | source)
XLA Modules:
  0.0 108.2 jit_solution(15408492815872334155)
XLA Ops:
  0.7 1.0 copy-done.1
  1.8 0.7 copy-done.2
  2.4 1.1 %copy-done.3 = bf16[256,1536]{1,0:T(8,128)(2,1)S(1)} copy-done((bf16[256,1536]{1,0:T(8,128)(2,1)S(1)}, bf16[256,1536]{1,0:T(8,128)(2,1)}, u32[]{:S(2)}) %copy-start.3) | copy-done | bytes 786456
  3.6 7.2 %gelu_pass.1 = (bf16[256,2048]{1,0:T(8,128)(2,1)S(1)}, f32[256,1024]{1,0:T(8,128)S(1)}, f32[256,1]{1,0:T(8,128)S(1)}, bf16[16,144,256]{2,1,0:T(8,128)(2,1)S(1)}, bf16[16,144,256]{2,1,0:T(8,128)(2,1)S(1)}) custom-call(s32[4]{0:T(128)S(1)} %pad_add_fusion.pos, f32[1,1024]{1,0:T(1,128)S(1)} %bitcast.7, bf16[256,1536]{1,0:T(8,128)(2,1)S(1)} %copy-done.3, ...), custom_call_target="tpu_custom_call" | custom-call | flops 8000000000 | bytes 1048576 | tf_op jit(solution)/shard_map/gelu_pass/pallas_call | solution.py:37
  10.9 0.5 collective-permute-start.3
  11.5 1.6 %norm_back.1.em = bf16[256,1024]{1,0:T(8,128)(2,1)S(1)} custom-call(f32[1,1024]{1,0:T(1,128)S(1)} %bitcast.8, bf16[256,2048]{1,0:T(8,128)(2,1)S(1)} %get-tuple-element.29.preact_grad.gm, bf16[1024,2048]{1,0:T(8,128)(2,1)S(1)} %copy-done, bf16[256,1024]{1,0:T(8,128)(2,1)S(1)} %copy-done.1, f32[256,1024]{1,0:T(8,128)S(1)} %get-tuple-element.30.normal, ...), custom_call_target="tpu_custom_call" | custom-call | flops 2000000000 | bytes 1048576 | tf_op jit(solution)/shard_map/norm_back/pallas_call | solution.py:37
  13.1 0.5 collective-permute-start
  13.6 2.4 %collective-permute-done.2.cr = bf16[256,1024]{1,0:T(8,128)(2,1)S(1)} collective-permute-done((bf16[256,1024]{1,0:T(8,128)(2,1)S(1)}, bf16[256,1024]{1,0:T(8,128)(2,1)S(1)}, u32[]{:S(2)}, u32[]{:S(2)}) %collective-permute-start.2) | collective-permute-done | bytes 524320 | tf_op jit(solution)/shard_map/ppermute | solution.py:33
  16.0 2.4 %terms_x.1 = (bf16[4,768,128]{2,1,0:T(8,128)(2,1)S(1)}, bf16[4,768,128]{2,1,0:T(8,128)(2,1)S(1)}, bf16[4,768,128]{2,1,0:T(8,128)(2,1)S(1)}, bf16[4,768,128]{2,1,0:T(8,128)(2,1)S(1)}) custom-call(s32[4]{0:T(128)S(1)} %pad_add_fusion.pos, bf16[8,2,144,256]{3,2,1,0:T(8,128)(2,1)S(1)} %bitcast.11, bf16[8,2,144,256]{3,2,1,0:T(8,128)(2,1)S(1)} %bitcast.9, ...), custom_call_target="tpu_custom_call" | custom-call | flops 2000000000 | bytes 1048576 | tf_op jit(solution)/shard_map/terms_x/pallas_call | solution.py:37
  18.4 1.3 %collective-permute-start.5 = (bf16[4,768,128]{2,1,0:T(8,128)(2,1)S(1)}, bf16[4,768,128]{2,1,0:T(8,128)(2,1)S(1)}, u32[]{:S(2)}, u32[]{:S(2)}) collective-permute-start(bf16[4,768,128]{2,1,0:T(8,128)(2,1)S(1)} %get-tuple-element.41), channel_id=1, source_target_pairs={{0,32},{1,35},{2,34},{3,33},{4,36},{5,39},{6,38},{7,37},{8,40},{9,... | collective-permute-start | bytes 2359304 | tf_op jit(solution)/shard_map/ppermute | solution.py:33
  19.7 2.1 %terms_y.1 = (bf16[4,640,128]{2,1,0:T(8,128)(2,1)S(1)}, bf16[4,640,128]{2,1,0:T(8,128)(2,1)S(1)}, bf16[4,640,128]{2,1,0:T(8,128)(2,1)S(1)}, bf16[4,640,128]{2,1,0:T(8,128)(2,1)S(1)}) custom-call(s32[4]{0:T(128)S(1)} %pad_add_fusion.pos, bf16[8,2,144,256]{3,2,1,0:T(8,128)(2,1)S(1)} %bitcast.12, bf16[8,2,144,256]{3,2,1,0:T(8,128)(2,1)S(1)} %bitcast.10, ...), custom_call_target="tpu_custom_call" | custom-call | flops 2000000000 | bytes 1048576 | tf_op jit(solution)/shard_map/terms_y/pallas_call | solution.py:37
  21.8 1.8 %collective-permute-start.8 = (bf16[4,640,128]{2,1,0:T(8,128)(2,1)S(1)}, bf16[4,640,128]{2,1,0:T(8,128)(2,1)S(1)}, u32[]{:S(2)}, u32[]{:S(2)}) collective-permute-start(bf16[4,640,128]{2,1,0:T(8,128)(2,1)S(1)} %get-tuple-element.46), channel_id=1, source_target_pairs={{0,64},{1,193},{2,66},{3,195},{4,68},{5,197},{6,70},{7,199},{8,72}... | collective-permute-start | bytes 1966088 | tf_op jit(solution)/shard_map/ppermute | solution.py:33
  23.6 0.8 collective-permute-start.4
  24.4 9.8 %collective-permute-done.5.got = bf16[4,768,128]{2,1,0:T(8,128)(2,1)S(1)} collective-permute-done((bf16[4,768,128]{2,1,0:T(8,128)(2,1)S(1)}, bf16[4,768,128]{2,1,0:T(8,128)(2,1)S(1)}, u32[]{:S(2)}, u32[]{:S(2)}) %collective-permute-start.5) | collective-permute-done | bytes 786464 | tf_op jit(solution)/shard_map/ppermute | solution.py:33
  34.3 0.2 pass_on.4
  34.5 1.0 collective-permute-start.6
  35.5 5.3 %collective-permute-start.7 = (bf16[4,640,128]{2,1,0:T(8,128)(2,1)S(1)}, bf16[4,640,128]{2,1,0:T(8,128)(2,1)S(1)}, u32[]{:S(2)}, u32[]{:S(2)}) collective-permute-start(bf16[4,640,128]{2,1,0:T(8,128)(2,1)S(1)} %get-tuple-element.44), channel_id=1, source_target_pairs={{0,192},{1,65},{2,194},{3,67},{4,196},{5,69},{6,198},{7,71},{8,200... | collective-permute-start | bytes 1966088 | tf_op jit(solution)/shard_map/ppermute | solution.py:33
  41.0 10.2 %collective-permute-done.7.refs_4_ = bf16[4,640,128]{2,1,0:T(8,128)(2,1)S(1)} collective-permute-done((bf16[4,640,128]{2,1,0:T(8,128)(2,1)S(1)}, bf16[4,640,128]{2,1,0:T(8,128)(2,1)S(1)}, u32[]{:S(2)}, u32[]{:S(2)}) %collective-permute-start.7) | collective-permute-done | bytes 655392 | tf_op jit(solution)/shard_map/ppermute | solution.py:33
  51.2 1.6 %collective-permute-done.9.refs_5_ = bf16[4,640,128]{2,1,0:T(8,128)(2,1)S(1)} collective-permute-done((bf16[4,640,128]{2,1,0:T(8,128)(2,1)S(1)}, bf16[4,640,128]{2,1,0:T(8,128)(2,1)S(1)}, u32[]{:S(2)}, u32[]{:S(2)}) %collective-permute-start.9) | collective-permute-done | bytes 655392 | tf_op jit(solution)/shard_map/ppermute | solution.py:33
  52.8 1.1 ring_turn.1
  53.9 0.5 collective-permute-start.11
  54.4 2.5 %collective-permute-start.14 = (bf16[640,128]{1,0:T(8,128)(2,1)S(1)}, bf16[640,128]{1,0:T(8,128)(2,1)S(1)}, u32[]{:S(2)}, u32[]{:S(2)}) collective-permute-start(bf16[640,128]{1,0:T(8,128)(2,1)S(1)} %get-tuple-element.54), channel_id=1, source_target_pairs={{0,32},{1,35},{2,34},{3,33},{4,36},{5,39},{6,38},{7,37},{8,40},{9,... | collective-permute-start | bytes 491528 | tf_op jit(solution)/shard_map/ppermute | solution.py:33
  56.8 1.5 %collective-permute-start.10 = (bf16[768,128]{1,0:T(8,128)(2,1)S(1)}, bf16[768,128]{1,0:T(8,128)(2,1)S(1)}, u32[]{:S(2)}, u32[]{:S(2)}) collective-permute-start(bf16[768,128]{1,0:T(8,128)(2,1)S(1)} %get-tuple-element.48), channel_id=1, source_target_pairs={{0,192},{1,65},{2,194},{3,67},{4,196},{5,69},{6,198},{7,71},{8,200... | collective-permute-start | bytes 589832 | tf_op jit(solution)/shard_map/ppermute | solution.py:33
  58.3 4.5 %collective-permute-done.11.got = bf16[768,128]{1,0:T(8,128)(2,1)S(1)} collective-permute-done((bf16[768,128]{1,0:T(8,128)(2,1)S(1)}, bf16[768,128]{1,0:T(8,128)(2,1)S(1)}, u32[]{:S(2)}, u32[]{:S(2)}) %collective-permute-start.11) | collective-permute-done | bytes 196640 | tf_op jit(solution)/shard_map/ppermute | solution.py:33
  62.9 0.2 collective-permute-start.13
  63.2 2.0 %collective-permute-start.15 = (bf16[640,128]{1,0:T(8,128)(2,1)S(1)}, bf16[640,128]{1,0:T(8,128)(2,1)S(1)}, u32[]{:S(2)}, u32[]{:S(2)}) collective-permute-start(bf16[640,128]{1,0:T(8,128)(2,1)S(1)} %pass_on.7), channel_id=1, source_target_pairs={{0,32},{1,35},{2,34},{3,33},{4,36},{5,39},{6,38},{7,37},{8,40},{9,... | collective-permute-start | bytes 491528 | tf_op jit(solution)/shard_map/ppermute | solution.py:33
  65.1 3.5 %collective-permute-done.13.refs_4_ = bf16[640,128]{1,0:T(8,128)(2,1)S(1)} collective-permute-done((bf16[640,128]{1,0:T(8,128)(2,1)S(1)}, bf16[640,128]{1,0:T(8,128)(2,1)S(1)}, u32[]{:S(2)}, u32[]{:S(2)}) %collective-permute-start.13) | collective-permute-done | bytes 163872 | tf_op jit(solution)/shard_map/ppermute | solution.py:33
  68.7 0.3 collective-permute-done.15.refs_5_
  69.0 0.8 collective-permute-done.12.refs_2_
  69.9 21.2 %all_to_all.10.got = bf16[8,176,128]{2,1,0:T(8,128)(2,1)S(1)} all-to-all(bf16[8,176,128]{2,1,0:T(8,128)(2,1)S(1)} %z_pack.1), channel_id=1, replica_groups=mesh['y'=4,'xl'=2,'z'=8,'xh'=2,'c'=2] {'z'}, dimensions={0} | all-to-all | bytes 720896 | tf_op jit(solution)/shard_map/all_to_all | solution.py:288
  91.1 16.1 %all_to_all.11.got = bf16[8,176,128]{2,1,0:T(8,128)(2,1)S(1)} all-to-all(bf16[8,176,128]{2,1,0:T(8,128)(2,1)S(1)} %z_sum.1), channel_id=1, replica_groups=mesh['y'=4,'xl'=2,'z'=8,'xh'=2,'c'=2] {'y','xl'}, dimensions={0} | all-to-all | bytes 720896 | tf_op jit(solution)/shard_map/all_to_all | solution.py:290
  107.3 0.9 unpack.1
  (23 shorter events, 0.9 us)
Async XLA Ops:
  0.7 1.0 copy-start.1
  1.8 0.7 copy-start.2
  2.4 1.1 %copy-start.3 = (bf16[256,1536]{1,0:T(8,128)(2,1)S(1)}, bf16[256,1536]{1,0:T(8,128)(2,1)}, u32[]{:S(2)}) copy-start(bf16[256,1536]{1,0:T(8,128)(2,1)} %p.1) | copy-start | bytes 2359300
  3.6 7.9 %copy-start = (bf16[1024,2048]{1,0:T(8,128)(2,1)S(1)}, bf16[1024,2048]{1,0:T(8,128)(2,1)}, u32[]{:S(2)}) copy-start(bf16[1024,2048]{1,0:T(8,128)(2,1)} %up.1) | copy-start | bytes 12582916
  10.8 5.2 %collective-permute-start.1 = (bf16[16,144,256]{2,1,0:T(8,128)(2,1)S(1)}, bf16[16,144,256]{2,1,0:T(8,128)(2,1)S(1)}, u32[]{:S(2)}, u32[]{:S(2)}) collective-permute-start(bf16[16,144,256]{2,1,0:T(8,128)(2,1)S(1)} %get-tuple-element.33), channel_id=1, source_target_pairs={{0,1},{1,0},{2,3},{3,2},{4,5},{5,4},{6,7},{7,6},{8,9},{9,8},{10,11... | collective-permute-start | bytes 3538952 | tf_op jit(solution)/shard_map/ppermute | solution.py:33
  10.9 5.1 %collective-permute-start.3 = (bf16[256,2048]{1,0:T(8,128)(2,1)S(1)}, bf16[256,2048]{1,0:T(8,128)(2,1)S(1)}, u32[]{:S(2)}, u32[]{:S(2)}) collective-permute-start(bf16[256,2048]{1,0:T(8,128)(2,1)S(1)} %get-tuple-element.29.preact_grad.gm), channel_id=1, source_target_pairs={{0,1},{1,0},{2,3},{3,2},{4,5},{5,4},{6,7},{7,6},{8,9},{9,8},{10,11... | collective-permute-start | bytes 3145736 | tf_op jit(solution)/shard_map/ppermute | solution.py:33
  11.4 4.6 %collective-permute-start.2 = (bf16[256,1024]{1,0:T(8,128)(2,1)S(1)}, bf16[256,1024]{1,0:T(8,128)(2,1)S(1)}, u32[]{:S(2)}, u32[]{:S(2)}) collective-permute-start(bf16[256,1024]{1,0:T(8,128)(2,1)S(1)} %copy-done.1), channel_id=1, source_target_pairs={{0,1},{1,0},{2,3},{3,2},{4,5},{5,4},{6,7},{7,6},{8,9},{9,8},{10,11... | collective-permute-start | bytes 1572872 | tf_op jit(solution)/shard_map/ppermute | solution.py:33
  13.1 5.3 %collective-permute-start = (bf16[256,1024]{1,0:T(8,128)(2,1)S(1)}, bf16[256,1024]{1,0:T(8,128)(2,1)S(1)}, u32[]{:S(2)}, u32[]{:S(2)}) collective-permute-start(bf16[256,1024]{1,0:T(8,128)(2,1)S(1)} %norm_back.1.em), channel_id=1, source_target_pairs={{0,1},{1,0},{2,3},{3,2},{4,5},{5,4},{6,7},{7,6},{8,9},{9,8},{10,11... | collective-permute-start | bytes 1572872 | tf_op jit(solution)/shard_map/ppermute | solution.py:33
  18.4 15.9 %collective-permute-start.5 = (bf16[4,768,128]{2,1,0:T(8,128)(2,1)S(1)}, bf16[4,768,128]{2,1,0:T(8,128)(2,1)S(1)}, u32[]{:S(2)}, u32[]{:S(2)}) collective-permute-start(bf16[4,768,128]{2,1,0:T(8,128)(2,1)S(1)} %get-tuple-element.41), channel_id=1, source_target_pairs={{0,32},{1,35},{2,34},{3,33},{4,36},{5,39},{6,38},{7,37},{8,40},{9,... | collective-permute-start | bytes 2359304 | tf_op jit(solution)/shard_map/ppermute | solution.py:33
  21.8 19.0 %collective-permute-start.8 = (bf16[4,640,128]{2,1,0:T(8,128)(2,1)S(1)}, bf16[4,640,128]{2,1,0:T(8,128)(2,1)S(1)}, u32[]{:S(2)}, u32[]{:S(2)}) collective-permute-start(bf16[4,640,128]{2,1,0:T(8,128)(2,1)S(1)} %get-tuple-element.46), channel_id=1, source_target_pairs={{0,64},{1,193},{2,66},{3,195},{4,68},{5,197},{6,70},{7,199},{8,72}... | collective-permute-start | bytes 1966088 | tf_op jit(solution)/shard_map/ppermute | solution.py:33
  23.6 27.6 %collective-permute-start.4 = (bf16[4,768,128]{2,1,0:T(8,128)(2,1)S(1)}, bf16[4,768,128]{2,1,0:T(8,128)(2,1)S(1)}, u32[]{:S(2)}, u32[]{:S(2)}) collective-permute-start(bf16[4,768,128]{2,1,0:T(8,128)(2,1)S(1)} %get-tuple-element.39), channel_id=1, source_target_pairs={{0,34},{1,33},{2,32},{3,35},{4,38},{5,37},{6,36},{7,39},{8,42},{9,... | collective-permute-start | bytes 2359304 | tf_op jit(solution)/shard_map/ppermute | solution.py:33
  34.5 18.3 %collective-permute-start.6 = (bf16[4,768,128]{2,1,0:T(8,128)(2,1)S(1)}, bf16[4,768,128]{2,1,0:T(8,128)(2,1)S(1)}, u32[]{:S(2)}, u32[]{:S(2)}) collective-permute-start(bf16[4,768,128]{2,1,0:T(8,128)(2,1)S(1)} %pass_on.4), channel_id=1, source_target_pairs={{0,32},{1,35},{2,34},{3,33},{4,36},{5,39},{6,38},{7,37},{8,40},{9,... | collective-permute-start | bytes 2359304 | tf_op jit(solution)/shard_map/ppermute | solution.py:33
  35.5 15.8 %collective-permute-start.7 = (bf16[4,640,128]{2,1,0:T(8,128)(2,1)S(1)}, bf16[4,640,128]{2,1,0:T(8,128)(2,1)S(1)}, u32[]{:S(2)}, u32[]{:S(2)}) collective-permute-start(bf16[4,640,128]{2,1,0:T(8,128)(2,1)S(1)} %get-tuple-element.44), channel_id=1, source_target_pairs={{0,192},{1,65},{2,194},{3,67},{4,196},{5,69},{6,198},{7,71},{8,200... | collective-permute-start | bytes 1966088 | tf_op jit(solution)/shard_map/ppermute | solution.py:33
  40.9 11.9 %collective-permute-start.9 = (bf16[4,640,128]{2,1,0:T(8,128)(2,1)S(1)}, bf16[4,640,128]{2,1,0:T(8,128)(2,1)S(1)}, u32[]{:S(2)}, u32[]{:S(2)}) collective-permute-start(bf16[4,640,128]{2,1,0:T(8,128)(2,1)S(1)} %pass_on.5), channel_id=1, source_target_pairs={{0,64},{1,193},{2,66},{3,195},{4,68},{5,197},{6,70},{7,199},{8,72}... | collective-permute-start | bytes 1966088 | tf_op jit(solution)/shard_map/ppermute | solution.py:33
  53.9 8.9 %collective-permute-start.11 = (bf16[768,128]{1,0:T(8,128)(2,1)S(1)}, bf16[768,128]{1,0:T(8,128)(2,1)S(1)}, u32[]{:S(2)}, u32[]{:S(2)}) collective-permute-start(bf16[768,128]{1,0:T(8,128)(2,1)S(1)} %get-tuple-element.50), channel_id=1, source_target_pairs={{0,64},{1,193},{2,66},{3,195},{4,68},{5,197},{6,70},{7,199},{8,72}... | collective-permute-start | bytes 589832 | tf_op jit(solution)/shard_map/ppermute | solution.py:33
  54.4 8.8 %collective-permute-start.14 = (bf16[640,128]{1,0:T(8,128)(2,1)S(1)}, bf16[640,128]{1,0:T(8,128)(2,1)S(1)}, u32[]{:S(2)}, u32[]{:S(2)}) collective-permute-start(bf16[640,128]{1,0:T(8,128)(2,1)S(1)} %get-tuple-element.54), channel_id=1, source_target_pairs={{0,32},{1,35},{2,34},{3,33},{4,36},{5,39},{6,38},{7,37},{8,40},{9,... | collective-permute-start | bytes 491528 | tf_op jit(solution)/shard_map/ppermute | solution.py:33
  56.8 11.9 %collective-permute-start.10 = (bf16[768,128]{1,0:T(8,128)(2,1)S(1)}, bf16[768,128]{1,0:T(8,128)(2,1)S(1)}, u32[]{:S(2)}, u32[]{:S(2)}) collective-permute-start(bf16[768,128]{1,0:T(8,128)(2,1)S(1)} %get-tuple-element.48), channel_id=1, source_target_pairs={{0,192},{1,65},{2,194},{3,67},{4,196},{5,69},{6,198},{7,71},{8,200... | collective-permute-start | bytes 589832 | tf_op jit(solution)/shard_map/ppermute | solution.py:33
  62.8 7.0 %collective-permute-start.12 = (bf16[768,128]{1,0:T(8,128)(2,1)S(1)}, bf16[768,128]{1,0:T(8,128)(2,1)S(1)}, u32[]{:S(2)}, u32[]{:S(2)}) collective-permute-start(bf16[768,128]{1,0:T(8,128)(2,1)S(1)} %pass_on.6), channel_id=1, source_target_pairs={{0,64},{1,193},{2,66},{3,195},{4,68},{5,197},{6,70},{7,199},{8,72}... | collective-permute-start | bytes 589832 | tf_op jit(solution)/shard_map/ppermute | solution.py:33
  62.9 5.8 %collective-permute-start.13 = (bf16[640,128]{1,0:T(8,128)(2,1)S(1)}, bf16[640,128]{1,0:T(8,128)(2,1)S(1)}, u32[]{:S(2)}, u32[]{:S(2)}) collective-permute-start(bf16[640,128]{1,0:T(8,128)(2,1)S(1)} %get-tuple-element.52), channel_id=1, source_target_pairs={{0,34},{1,33},{2,32},{3,35},{4,38},{5,37},{6,36},{7,39},{8,42},{9,... | collective-permute-start | bytes 491528 | tf_op jit(solution)/shard_map/ppermute | solution.py:33
  63.2 5.8 %collective-permute-start.15 = (bf16[640,128]{1,0:T(8,128)(2,1)S(1)}, bf16[640,128]{1,0:T(8,128)(2,1)S(1)}, u32[]{:S(2)}, u32[]{:S(2)}) collective-permute-start(bf16[640,128]{1,0:T(8,128)(2,1)S(1)} %pass_on.7), channel_id=1, source_target_pairs={{0,32},{1,35},{2,34},{3,33},{4,36},{5,39},{6,38},{7,37},{8,40},{9,... | collective-permute-start | bytes 491528 | tf_op jit(solution)/shard_map/ppermute | solution.py:33

commit v5 on v4

--- a/solution.py
+++ b/solution.py
@@ -222,9 +222,11 @@
 
 def rings(axes, parts):
     result = []
-    for axis, (own, keep, ahead, behind) in zip(axes, parts):
+    for p, (axis, (own, keep, ahead, behind)) in enumerate(zip(axes, parts)):
         got = move(ahead, axis, 1)
         near = move(behind, axis, -1)
+        if p == 1:
+            got, near = lax.optimization_barrier((got, near))
         (total,) = call(
             pass_on_body, [(keep.shape, BF)], [], "pass_on", keep, got, specs=[VMEM, VMEM]
         )
@@ -236,18 +238,26 @@
     return (a.astype(F32) + b.astype(F32) + c.astype(F32)).astype(BF)
 
 
-def turn_body(pos, *refs):
-    for p in range(2):
-        a, b, c = refs[3 * p : 3 * p + 3]
-        for rel in range(4):
-            to = chunk_of(pos[1 - p], pos, rel)
-            refs[6 + 4 * p + rel][...] = add3(a[to], b[to], c[to])
+def turn_body(second, pos, own, near, far, *outs):
+    for rel in range(4):
+        to = chunk_of(pos[second], pos, rel)
+        outs[rel][...] = add3(own[to], near[to], far[to])
 
 
 def reduce_xy(pos, parts):
-    outs = [((CHUNK_X, LANES), BF)] * 4 + [((CHUNK_Y, LANES), BF)] * 4
-    outs = call(turn_body, outs, [], "ring_turn", pos, *rings("xy", parts))
-    return rings("yx", (outs[:4], outs[4:]))
+    sums = rings("xy", parts)
+    turned = [
+        call(
+            functools.partial(turn_body, 1 - p),
+            [(sums[3 * p].shape[1:], BF)] * 4,
+            [],
+            "ring_turn_" + "xy"[p],
+            pos,
+            *sums[3 * p : 3 * p + 3],
+        )
+        for p in range(2)
+    ]
+    return rings("yx", turned)
 
 
 def pack_body(*refs):

time: 108 us -> 99.6 us (0.922)
  blocking collectives: 37.3 us -> 31.5 us
  waiting for transfers between devices: 33.1 us -> 30 us
    ppermute x16, waiting for transfers between devices: 33.1 us -> 30 us  [move(): return lax.ppermute(value, AXES, sorted(pairs))]
    all_to_all x1, blocking collectives: 16.1 us -> 13.1 us  [finish(): every = lax.all_to_all(copies, ('y', 'xl'), 0, 0, tiled=True)]
    all_to_all x1, blocking collectives: 21.2 us -> 18.5 us  [finish(): got = lax.all_to_all(packed, 'z', 0, 0, tiled=True)]
    pallas_call x12 -> x13, Pallas kernels: 15.8 us -> 16.4 us  [call(): pl.pallas_call(body, out_shape=[jax.ShapeDtypeStruct(s, d) for s, d in ou...]
  transfers between devices with their start and end apart: 16 -> 16, of which waited for: 8 -> 9; matrix products, arithmetic and copies ran while one was open for 0% -> 0% of each run, Pallas kernels for 6% -> 8%
where the time goes in v5:
time: 99.6 us; the launch traced here: 99.1 us
  blocking collectives  31.5 us (32%)
  waiting for transfers between devices  30 us (30%)
  starting transfers between devices  17.5 us (18%)
  Pallas kernels  16.4 us (16%)
  local copies, waits for them, and re-layouts  2.87 us (3%)
    ppermute x16, waiting for transfers between devices, move(): return lax.ppermute(value, AXES, sorted(pairs))  30 us
    all_to_all x1, blocking collectives, finish(): got = lax.all_to_all(packed, 'z', 0, 0, tiled=True)  18.5 us
    ppermute x16, starting transfers between devices, move(): return lax.ppermute(value, AXES, sorted(pairs))  17.5 us
    pallas_call x13, Pallas kernels, call(): pl.pallas_call(body, out_shape=[jax.ShapeDtypeStruct(s, d) for s, d in ou...  16.4 us
    all_to_all x1, blocking collectives, finish(): every = lax.all_to_all(copies, ('y', 'xl'), 0, 0, tiled=True)  13.1 us
    unnamed x8, local copies, waits for them, and re-layouts  2.87 us
  transfers between devices with their start and end apart: 16, of which 9 were waited for; matrix products, arithmetic and copies ran while one was open for 0% of the time, Pallas kernels for 8%

profile of v5, /device:TPU:4, one launch (start us, length us, event | category | flops | bytes accessed | tf_op | source)
XLA Modules:
  0.0 99.1 jit_solution(5679507599669830412)
XLA Ops:
  0.7 1.0 %copy-done.1 = bf16[256,1024]{1,0:T(8,128)(2,1)S(1)} copy-done((bf16[256,1024]{1,0:T(8,128)(2,1)S(1)}, bf16[256,1024]{1,0:T(8,128)(2,1)}, u32[]{:S(2)}) %copy-start.1) | copy-done | bytes 524312
  1.8 0.7 copy-done.2
  2.4 1.1 %copy-done.3 = bf16[256,1536]{1,0:T(8,128)(2,1)S(1)} copy-done((bf16[256,1536]{1,0:T(8,128)(2,1)S(1)}, bf16[256,1536]{1,0:T(8,128)(2,1)}, u32[]{:S(2)}) %copy-start.3) | copy-done | bytes 786456
  3.6 7.2 %gelu_pass.1 = (bf16[256,2048]{1,0:T(8,128)(2,1)S(1)}, f32[256,1024]{1,0:T(8,128)S(1)}, f32[256,1]{1,0:T(8,128)S(1)}, bf16[16,144,256]{2,1,0:T(8,128)(2,1)S(1)}, bf16[16,144,256]{2,1,0:T(8,128)(2,1)S(1)}) custom-call(s32[4]{0:T(128)S(1)} %pad_add_fusion.pos, f32[1,1024]{1,0:T(1,128)S(1)} %bitcast.7, bf16[256,1536]{1,0:T(8,128)(2,1)S(1)} %copy-done.3, ...), custom_call_target="tpu_custom_call" | custom-call | flops 8000000000 | bytes 1048576 | tf_op jit(solution)/shard_map/gelu_pass/pallas_call | solution.py:37
  10.9 0.5 collective-permute-start.3
  11.5 1.6 %norm_back.1.em = bf16[256,1024]{1,0:T(8,128)(2,1)S(1)} custom-call(f32[1,1024]{1,0:T(1,128)S(1)} %bitcast.8, bf16[256,2048]{1,0:T(8,128)(2,1)S(1)} %get-tuple-element.33.preact_grad.gm, bf16[1024,2048]{1,0:T(8,128)(2,1)S(1)} %copy-done, bf16[256,1024]{1,0:T(8,128)(2,1)S(1)} %copy-done.1, f32[256,1024]{1,0:T(8,128)S(1)} %get-tuple-element.34.normal, ...), custom_call_target="tpu_custom_call" | custom-call | flops 2000000000 | bytes 1048576 | tf_op jit(solution)/shard_map/norm_back/pallas_call | solution.py:37
  13.6 2.4 %collective-permute-done.2.cr = bf16[256,1024]{1,0:T(8,128)(2,1)S(1)} collective-permute-done((bf16[256,1024]{1,0:T(8,128)(2,1)S(1)}, bf16[256,1024]{1,0:T(8,128)(2,1)S(1)}, u32[]{:S(2)}, u32[]{:S(2)}) %collective-permute-start.2) | collective-permute-done | bytes 524320 | tf_op jit(solution)/shard_map/ppermute | solution.py:33
  16.0 2.4 %terms_x.1 = (bf16[4,768,128]{2,1,0:T(8,128)(2,1)S(1)}, bf16[4,768,128]{2,1,0:T(8,128)(2,1)S(1)}, bf16[4,768,128]{2,1,0:T(8,128)(2,1)S(1)}, bf16[4,768,128]{2,1,0:T(8,128)(2,1)S(1)}) custom-call(s32[4]{0:T(128)S(1)} %pad_add_fusion.pos, bf16[8,2,144,256]{3,2,1,0:T(8,128)(2,1)S(1)} %bitcast.11, bf16[8,2,144,256]{3,2,1,0:T(8,128)(2,1)S(1)} %bitcast.9, ...), custom_call_target="tpu_custom_call" | custom-call | flops 2000000000 | bytes 1048576 | tf_op jit(solution)/shard_map/terms_x/pallas_call | solution.py:37
  18.4 1.3 %collective-permute-start.5 = (bf16[4,768,128]{2,1,0:T(8,128)(2,1)S(1)}, bf16[4,768,128]{2,1,0:T(8,128)(2,1)S(1)}, u32[]{:S(2)}, u32[]{:S(2)}) collective-permute-start(bf16[4,768,128]{2,1,0:T(8,128)(2,1)S(1)} %get-tuple-element.45), channel_id=1, source_target_pairs={{0,32},{1,35},{2,34},{3,33},{4,36},{5,39},{6,38},{7,37},{8,40},{9,... | collective-permute-start | bytes 2359304 | tf_op jit(solution)/shard_map/ppermute | solution.py:33
  19.7 2.1 %terms_y.1 = (bf16[4,640,128]{2,1,0:T(8,128)(2,1)S(1)}, bf16[4,640,128]{2,1,0:T(8,128)(2,1)S(1)}, bf16[4,640,128]{2,1,0:T(8,128)(2,1)S(1)}, bf16[4,640,128]{2,1,0:T(8,128)(2,1)S(1)}) custom-call(s32[4]{0:T(128)S(1)} %pad_add_fusion.pos, bf16[8,2,144,256]{3,2,1,0:T(8,128)(2,1)S(1)} %bitcast.12, bf16[8,2,144,256]{3,2,1,0:T(8,128)(2,1)S(1)} %bitcast.10, ...), custom_call_target="tpu_custom_call" | custom-call | flops 2000000000 | bytes 1048576 | tf_op jit(solution)/shard_map/terms_y/pallas_call | solution.py:37
  21.8 1.8 %collective-permute-start.10 = (bf16[4,640,128]{2,1,0:T(8,128)(2,1)S(1)}, bf16[4,640,128]{2,1,0:T(8,128)(2,1)S(1)}, u32[]{:S(2)}, u32[]{:S(2)}) collective-permute-start(bf16[4,640,128]{2,1,0:T(8,128)(2,1)S(1)} %get-tuple-element.52), channel_id=1, source_target_pairs={{0,64},{1,193},{2,66},{3,195},{4,68},{5,197},{6,70},{7,199},{8,72}... | collective-permute-start | bytes 1966088 | tf_op jit(solution)/shard_map/ppermute | solution.py:33
  23.6 1.7 %collective-permute-start.11 = (bf16[4,640,128]{2,1,0:T(8,128)(2,1)S(1)}, bf16[4,640,128]{2,1,0:T(8,128)(2,1)S(1)}, u32[]{:S(2)}, u32[]{:S(2)}) collective-permute-start(bf16[4,640,128]{2,1,0:T(8,128)(2,1)S(1)} %get-tuple-element.53), channel_id=1, source_target_pairs={{0,192},{1,65},{2,194},{3,67},{4,196},{5,69},{6,198},{7,71},{8,200... | collective-permute-start | bytes 1966088 | tf_op jit(solution)/shard_map/ppermute | solution.py:33
  25.3 0.8 collective-permute-start.4
  26.1 8.2 %collective-permute-done.5.got = bf16[4,768,128]{2,1,0:T(8,128)(2,1)S(1)} collective-permute-done((bf16[4,768,128]{2,1,0:T(8,128)(2,1)S(1)}, bf16[4,768,128]{2,1,0:T(8,128)(2,1)S(1)}, u32[]{:S(2)}, u32[]{:S(2)}) %collective-permute-start.5) | collective-permute-done | bytes 786464 | tf_op jit(solution)/shard_map/ppermute | solution.py:33
  34.5 1.0 collective-permute-start.6
  35.5 4.4 %collective-permute-done.10.got = bf16[4,640,128]{2,1,0:T(8,128)(2,1)S(1)} collective-permute-done((bf16[4,640,128]{2,1,0:T(8,128)(2,1)S(1)}, bf16[4,640,128]{2,1,0:T(8,128)(2,1)S(1)}, u32[]{:S(2)}, u32[]{:S(2)}) %collective-permute-start.10) | collective-permute-done | bytes 655392 | tf_op jit(solution)/shard_map/ppermute | solution.py:33
  40.1 1.1 %collective-permute-start.12 = (bf16[4,640,128]{2,1,0:T(8,128)(2,1)S(1)}, bf16[4,640,128]{2,1,0:T(8,128)(2,1)S(1)}, u32[]{:S(2)}, u32[]{:S(2)}) collective-permute-start(bf16[4,640,128]{2,1,0:T(8,128)(2,1)S(1)} %pass_on.6), channel_id=1, source_target_pairs={{0,64},{1,193},{2,66},{3,195},{4,68},{5,197},{6,70},{7,199},{8,72}... | collective-permute-start | bytes 1966088 | tf_op jit(solution)/shard_map/ppermute | solution.py:33
  41.1 1.6 %collective-permute-done.4.near = bf16[4,768,128]{2,1,0:T(8,128)(2,1)S(1)} collective-permute-done((bf16[4,768,128]{2,1,0:T(8,128)(2,1)S(1)}, bf16[4,768,128]{2,1,0:T(8,128)(2,1)S(1)}, u32[]{:S(2)}, u32[]{:S(2)}) %collective-permute-start.4) | collective-permute-done | bytes 786464 | tf_op jit(solution)/shard_map/ppermute | solution.py:33
  42.8 4.6 %collective-permute-done.6.far = bf16[4,768,128]{2,1,0:T(8,128)(2,1)S(1)} collective-permute-done((bf16[4,768,128]{2,1,0:T(8,128)(2,1)S(1)}, bf16[4,768,128]{2,1,0:T(8,128)(2,1)S(1)}, u32[]{:S(2)}, u32[]{:S(2)}) %collective-permute-start.6) | collective-permute-done | bytes 786464 | tf_op jit(solution)/shard_map/ppermute | solution.py:33
  47.3 0.8 ring_turn_x.1
  48.2 2.2 %collective-permute-start.8 = (bf16[768,128]{1,0:T(8,128)(2,1)S(1)}, bf16[768,128]{1,0:T(8,128)(2,1)S(1)}, u32[]{:S(2)}, u32[]{:S(2)}) collective-permute-start(bf16[768,128]{1,0:T(8,128)(2,1)S(1)} %get-tuple-element.49), channel_id=1, source_target_pairs={{0,64},{1,193},{2,66},{3,195},{4,68},{5,197},{6,70},{7,199},{8,72}... | collective-permute-start | bytes 589832 | tf_op jit(solution)/shard_map/ppermute | solution.py:33
  50.3 1.6 %collective-permute-done.12.far = bf16[4,640,128]{2,1,0:T(8,128)(2,1)S(1)} collective-permute-done((bf16[4,640,128]{2,1,0:T(8,128)(2,1)S(1)}, bf16[4,640,128]{2,1,0:T(8,128)(2,1)S(1)}, u32[]{:S(2)}, u32[]{:S(2)}) %collective-permute-start.12) | collective-permute-done | bytes 655392 | tf_op jit(solution)/shard_map/ppermute | solution.py:33
  51.9 0.8 ring_turn_y.1
  52.7 3.0 %collective-permute-start.13 = (bf16[640,128]{1,0:T(8,128)(2,1)S(1)}, bf16[640,128]{1,0:T(8,128)(2,1)S(1)}, u32[]{:S(2)}, u32[]{:S(2)}) collective-permute-start(bf16[640,128]{1,0:T(8,128)(2,1)S(1)} %get-tuple-element.58), channel_id=1, source_target_pairs={{0,32},{1,35},{2,34},{3,33},{4,36},{5,39},{6,38},{7,37},{8,40},{9,... | collective-permute-start | bytes 491528 | tf_op jit(solution)/shard_map/ppermute | solution.py:33
  55.9 2.0 %collective-permute-start.9 = (bf16[768,128]{1,0:T(8,128)(2,1)S(1)}, bf16[768,128]{1,0:T(8,128)(2,1)S(1)}, u32[]{:S(2)}, u32[]{:S(2)}) collective-permute-start(bf16[768,128]{1,0:T(8,128)(2,1)S(1)} %pass_on.5), channel_id=1, source_target_pairs={{0,64},{1,193},{2,66},{3,195},{4,68},{5,197},{6,70},{7,199},{8,72}... | collective-permute-start | bytes 589832 | tf_op jit(solution)/shard_map/ppermute | solution.py:33
  57.9 0.7 collective-permute-done.13.got
  58.6 2.5 %collective-permute-done.14.refs_4_ = bf16[640,128]{1,0:T(8,128)(2,1)S(1)} collective-permute-done((bf16[640,128]{1,0:T(8,128)(2,1)S(1)}, bf16[640,128]{1,0:T(8,128)(2,1)S(1)}, u32[]{:S(2)}, u32[]{:S(2)}) %collective-permute-start.14) | collective-permute-done | bytes 163872 | tf_op jit(solution)/shard_map/ppermute | solution.py:33
  61.1 1.4 %collective-permute-start.15 = (bf16[640,128]{1,0:T(8,128)(2,1)S(1)}, bf16[640,128]{1,0:T(8,128)(2,1)S(1)}, u32[]{:S(2)}, u32[]{:S(2)}) collective-permute-start(bf16[640,128]{1,0:T(8,128)(2,1)S(1)} %pass_on.7), channel_id=1, source_target_pairs={{0,32},{1,35},{2,34},{3,33},{4,36},{5,39},{6,38},{7,37},{8,40},{9,... | collective-permute-start | bytes 491528 | tf_op jit(solution)/shard_map/ppermute | solution.py:33
  62.5 4.0 %collective-permute-done.15.refs_5_ = bf16[640,128]{1,0:T(8,128)(2,1)S(1)} collective-permute-done((bf16[640,128]{1,0:T(8,128)(2,1)S(1)}, bf16[640,128]{1,0:T(8,128)(2,1)S(1)}, u32[]{:S(2)}, u32[]{:S(2)}) %collective-permute-start.15) | collective-permute-done | bytes 163872 | tf_op jit(solution)/shard_map/ppermute | solution.py:33
  66.6 18.5 %all_to_all.10.got = bf16[8,176,128]{2,1,0:T(8,128)(2,1)S(1)} all-to-all(bf16[8,176,128]{2,1,0:T(8,128)(2,1)S(1)} %z_pack.1), channel_id=1, replica_groups=mesh['y'=4,'xl'=2,'z'=8,'xh'=2,'c'=2] {'z'}, dimensions={0} | all-to-all | bytes 720896 | tf_op jit(solution)/shard_map/all_to_all | solution.py:298
  85.2 13.1 %all_to_all.11.got = bf16[8,176,128]{2,1,0:T(8,128)(2,1)S(1)} all-to-all(bf16[8,176,128]{2,1,0:T(8,128)(2,1)S(1)} %z_sum.1), channel_id=1, replica_groups=mesh['y'=4,'xl'=2,'z'=8,'xh'=2,'c'=2] {'y','xl'}, dimensions={0} | all-to-all | bytes 720896 | tf_op jit(solution)/shard_map/all_to_all | solution.py:300
  98.2 0.9 unpack.1
  (24 shorter events, 1.5 us)
Async XLA Ops:
  0.7 1.0 %copy-start.1 = (bf16[256,1024]{1,0:T(8,128)(2,1)S(1)}, bf16[256,1024]{1,0:T(8,128)(2,1)}, u32[]{:S(2)}) copy-start(bf16[256,1024]{1,0:T(8,128)(2,1)} %cm.1) | copy-start | bytes 1572868
  1.8 0.7 copy-start.2
  2.4 1.1 %copy-start.3 = (bf16[256,1536]{1,0:T(8,128)(2,1)S(1)}, bf16[256,1536]{1,0:T(8,128)(2,1)}, u32[]{:S(2)}) copy-start(bf16[256,1536]{1,0:T(8,128)(2,1)} %p.1) | copy-start | bytes 2359300
  3.6 7.9 %copy-start = (bf16[1024,2048]{1,0:T(8,128)(2,1)S(1)}, bf16[1024,2048]{1,0:T(8,128)(2,1)}, u32[]{:S(2)}) copy-start(bf16[1024,2048]{1,0:T(8,128)(2,1)} %up.1) | copy-start | bytes 12582916
  10.8 5.2 %collective-permute-start.1 = (bf16[16,144,256]{2,1,0:T(8,128)(2,1)S(1)}, bf16[16,144,256]{2,1,0:T(8,128)(2,1)S(1)}, u32[]{:S(2)}, u32[]{:S(2)}) collective-permute-start(bf16[16,144,256]{2,1,0:T(8,128)(2,1)S(1)} %get-tuple-element.37), channel_id=1, source_target_pairs={{0,1},{1,0},{2,3},{3,2},{4,5},{5,4},{6,7},{7,6},{8,9},{9,8},{10,11... | collective-permute-start | bytes 3538952 | tf_op jit(solution)/shard_map/ppermute | solution.py:33
  10.9 5.1 %collective-permute-start.3 = (bf16[256,2048]{1,0:T(8,128)(2,1)S(1)}, bf16[256,2048]{1,0:T(8,128)(2,1)S(1)}, u32[]{:S(2)}, u32[]{:S(2)}) collective-permute-start(bf16[256,2048]{1,0:T(8,128)(2,1)S(1)} %get-tuple-element.33.preact_grad.gm), channel_id=1, source_target_pairs={{0,1},{1,0},{2,3},{3,2},{4,5},{5,4},{6,7},{7,6},{8,9},{9,8},{10,11... | collective-permute-start | bytes 3145736 | tf_op jit(solution)/shard_map/ppermute | solution.py:33
  11.4 4.6 %collective-permute-start.2 = (bf16[256,1024]{1,0:T(8,128)(2,1)S(1)}, bf16[256,1024]{1,0:T(8,128)(2,1)S(1)}, u32[]{:S(2)}, u32[]{:S(2)}) collective-permute-start(bf16[256,1024]{1,0:T(8,128)(2,1)S(1)} %copy-done.1), channel_id=1, source_target_pairs={{0,1},{1,0},{2,3},{3,2},{4,5},{5,4},{6,7},{7,6},{8,9},{9,8},{10,11... | collective-permute-start | bytes 1572872 | tf_op jit(solution)/shard_map/ppermute | solution.py:33
  13.1 5.3 %collective-permute-start = (bf16[256,1024]{1,0:T(8,128)(2,1)S(1)}, bf16[256,1024]{1,0:T(8,128)(2,1)S(1)}, u32[]{:S(2)}, u32[]{:S(2)}) collective-permute-start(bf16[256,1024]{1,0:T(8,128)(2,1)S(1)} %norm_back.1.em), channel_id=1, source_target_pairs={{0,1},{1,0},{2,3},{3,2},{4,5},{5,4},{6,7},{7,6},{8,9},{9,8},{10,11... | collective-permute-start | bytes 1572872 | tf_op jit(solution)/shard_map/ppermute | solution.py:33
  18.4 15.9 %collective-permute-start.5 = (bf16[4,768,128]{2,1,0:T(8,128)(2,1)S(1)}, bf16[4,768,128]{2,1,0:T(8,128)(2,1)S(1)}, u32[]{:S(2)}, u32[]{:S(2)}) collective-permute-start(bf16[4,768,128]{2,1,0:T(8,128)(2,1)S(1)} %get-tuple-element.45), channel_id=1, source_target_pairs={{0,32},{1,35},{2,34},{3,33},{4,36},{5,39},{6,38},{7,37},{8,40},{9,... | collective-permute-start | bytes 2359304 | tf_op jit(solution)/shard_map/ppermute | solution.py:33
  21.8 18.1 %collective-permute-start.10 = (bf16[4,640,128]{2,1,0:T(8,128)(2,1)S(1)}, bf16[4,640,128]{2,1,0:T(8,128)(2,1)S(1)}, u32[]{:S(2)}, u32[]{:S(2)}) collective-permute-start(bf16[4,640,128]{2,1,0:T(8,128)(2,1)S(1)} %get-tuple-element.52), channel_id=1, source_target_pairs={{0,64},{1,193},{2,66},{3,195},{4,68},{5,197},{6,70},{7,199},{8,72}... | collective-permute-start | bytes 1966088 | tf_op jit(solution)/shard_map/ppermute | solution.py:33
  23.6 16.3 %collective-permute-start.11 = (bf16[4,640,128]{2,1,0:T(8,128)(2,1)S(1)}, bf16[4,640,128]{2,1,0:T(8,128)(2,1)S(1)}, u32[]{:S(2)}, u32[]{:S(2)}) collective-permute-start(bf16[4,640,128]{2,1,0:T(8,128)(2,1)S(1)} %get-tuple-element.53), channel_id=1, source_target_pairs={{0,192},{1,65},{2,194},{3,67},{4,196},{5,69},{6,198},{7,71},{8,200... | collective-permute-start | bytes 1966088 | tf_op jit(solution)/shard_map/ppermute | solution.py:33
  25.3 17.5 %collective-permute-start.4 = (bf16[4,768,128]{2,1,0:T(8,128)(2,1)S(1)}, bf16[4,768,128]{2,1,0:T(8,128)(2,1)S(1)}, u32[]{:S(2)}, u32[]{:S(2)}) collective-permute-start(bf16[4,768,128]{2,1,0:T(8,128)(2,1)S(1)} %get-tuple-element.43), channel_id=1, source_target_pairs={{0,34},{1,33},{2,32},{3,35},{4,38},{5,37},{6,36},{7,39},{8,42},{9,... | collective-permute-start | bytes 2359304 | tf_op jit(solution)/shard_map/ppermute | solution.py:33
  34.5 12.8 %collective-permute-start.6 = (bf16[4,768,128]{2,1,0:T(8,128)(2,1)S(1)}, bf16[4,768,128]{2,1,0:T(8,128)(2,1)S(1)}, u32[]{:S(2)}, u32[]{:S(2)}) collective-permute-start(bf16[4,768,128]{2,1,0:T(8,128)(2,1)S(1)} %pass_on.4), channel_id=1, source_target_pairs={{0,32},{1,35},{2,34},{3,33},{4,36},{5,39},{6,38},{7,37},{8,40},{9,... | collective-permute-start | bytes 2359304 | tf_op jit(solution)/shard_map/ppermute | solution.py:33
  40.1 11.9 %collective-permute-start.12 = (bf16[4,640,128]{2,1,0:T(8,128)(2,1)S(1)}, bf16[4,640,128]{2,1,0:T(8,128)(2,1)S(1)}, u32[]{:S(2)}, u32[]{:S(2)}) collective-permute-start(bf16[4,640,128]{2,1,0:T(8,128)(2,1)S(1)} %pass_on.6), channel_id=1, source_target_pairs={{0,64},{1,193},{2,66},{3,195},{4,68},{5,197},{6,70},{7,199},{8,72}... | collective-permute-start | bytes 1966088 | tf_op jit(solution)/shard_map/ppermute | solution.py:33
  48.2 7.7 %collective-permute-start.8 = (bf16[768,128]{1,0:T(8,128)(2,1)S(1)}, bf16[768,128]{1,0:T(8,128)(2,1)S(1)}, u32[]{:S(2)}, u32[]{:S(2)}) collective-permute-start(bf16[768,128]{1,0:T(8,128)(2,1)S(1)} %get-tuple-element.49), channel_id=1, source_target_pairs={{0,64},{1,193},{2,66},{3,195},{4,68},{5,197},{6,70},{7,199},{8,72}... | collective-permute-start | bytes 589832 | tf_op jit(solution)/shard_map/ppermute | solution.py:33
  52.7 5.8 %collective-permute-start.13 = (bf16[640,128]{1,0:T(8,128)(2,1)S(1)}, bf16[640,128]{1,0:T(8,128)(2,1)S(1)}, u32[]{:S(2)}, u32[]{:S(2)}) collective-permute-start(bf16[640,128]{1,0:T(8,128)(2,1)S(1)} %get-tuple-element.58), channel_id=1, source_target_pairs={{0,32},{1,35},{2,34},{3,33},{4,36},{5,39},{6,38},{7,37},{8,40},{9,... | collective-permute-start | bytes 491528 | tf_op jit(solution)/shard_map/ppermute | solution.py:33
  55.7 5.3 %collective-permute-start.14 = (bf16[640,128]{1,0:T(8,128)(2,1)S(1)}, bf16[640,128]{1,0:T(8,128)(2,1)S(1)}, u32[]{:S(2)}, u32[]{:S(2)}) collective-permute-start(bf16[640,128]{1,0:T(8,128)(2,1)S(1)} %get-tuple-element.59), channel_id=1, source_target_pairs={{0,34},{1,33},{2,32},{3,35},{4,38},{5,37},{6,36},{7,39},{8,42},{9,... | collective-permute-start | bytes 491528 | tf_op jit(solution)/shard_map/ppermute | solution.py:33
  55.7 10.8 %collective-permute-start.7 = (bf16[768,128]{1,0:T(8,128)(2,1)S(1)}, bf16[768,128]{1,0:T(8,128)(2,1)S(1)}, u32[]{:S(2)}, u32[]{:S(2)}) collective-permute-start(bf16[768,128]{1,0:T(8,128)(2,1)S(1)} %get-tuple-element.47), channel_id=1, source_target_pairs={{0,192},{1,65},{2,194},{3,67},{4,196},{5,69},{6,198},{7,71},{8,200... | collective-permute-start | bytes 589832 | tf_op jit(solution)/shard_map/ppermute | solution.py:33
  55.9 10.6 %collective-permute-start.9 = (bf16[768,128]{1,0:T(8,128)(2,1)S(1)}, bf16[768,128]{1,0:T(8,128)(2,1)S(1)}, u32[]{:S(2)}, u32[]{:S(2)}) collective-permute-start(bf16[768,128]{1,0:T(8,128)(2,1)S(1)} %pass_on.5), channel_id=1, source_target_pairs={{0,64},{1,193},{2,66},{3,195},{4,68},{5,197},{6,70},{7,199},{8,72}... | collective-permute-start | bytes 589832 | tf_op jit(solution)/shard_map/ppermute | solution.py:33
  61.1 5.4 %collective-permute-start.15 = (bf16[640,128]{1,0:T(8,128)(2,1)S(1)}, bf16[640,128]{1,0:T(8,128)(2,1)S(1)}, u32[]{:S(2)}, u32[]{:S(2)}) collective-permute-start(bf16[640,128]{1,0:T(8,128)(2,1)S(1)} %pass_on.7), channel_id=1, source_target_pairs={{0,32},{1,35},{2,34},{3,33},{4,36},{5,39},{6,38},{7,37},{8,40},{9,... | collective-permute-start | bytes 491528 | tf_op jit(solution)/shard_map/ppermute | solution.py:33

commit v6 on v5

--- a/solution.py
+++ b/solution.py
@@ -220,12 +220,12 @@
     out[...] = (keep[...].astype(F32) + got[...].astype(F32)).astype(BF)
 
 
-def rings(axes, parts):
+def rings(axes, parts, together):
     result = []
     for p, (axis, (own, keep, ahead, behind)) in enumerate(zip(axes, parts)):
         got = move(ahead, axis, 1)
         near = move(behind, axis, -1)
-        if p == 1:
+        if together[p]:
             got, near = lax.optimization_barrier((got, near))
         (total,) = call(
             pass_on_body, [(keep.shape, BF)], [], "pass_on", keep, got, specs=[VMEM, VMEM]
@@ -245,7 +245,7 @@
 
 
 def reduce_xy(pos, parts):
-    sums = rings("xy", parts)
+    sums = rings("xy", parts, (False, True))
     turned = [
         call(
             functools.partial(turn_body, 1 - p),
@@ -257,7 +257,7 @@
         )
         for p in range(2)
     ]
-    return rings("yx", turned)
+    return rings("yx", turned, (True, True))
 
 
 def pack_body(*refs):

time: 99.6 us -> 101 us (1.014)
  starting transfers between devices: 17.5 us -> 18.9 us
  waiting for transfers between devices: 30 us -> 28.8 us
  blocking collectives: 31.5 us -> 32.6 us
    ppermute x16, starting transfers between devices: 17.5 us -> 18.9 us  [move(): return lax.ppermute(value, AXES, sorted(pairs))]
    all_to_all x1, blocking collectives: 13.1 us -> 14.3 us  [finish(): every = lax.all_to_all(copies, ('y', 'xl'), 0, 0, tiled=True)]
    ppermute x16, waiting for transfers between devices: 30 us -> 28.8 us  [move(): return lax.ppermute(value, AXES, sorted(pairs))]
  transfers between devices with their start and end apart: 16 -> 16, of which waited for: 9 -> 10; matrix products, arithmetic and copies ran while one was open for 0% -> 0% of each run, Pallas kernels for 8% -> 8%
where the time goes in v6:
time: 101 us; the launch traced here: 100 us
  blocking collectives  32.6 us (32%)
  waiting for transfers between devices  28.8 us (29%)
  starting transfers between devices  18.9 us (19%)
  Pallas kernels  16.4 us (16%)
  local copies, waits for them, and re-layouts  2.87 us (3%)
    ppermute x16, waiting for transfers between devices, move(): return lax.ppermute(value, AXES, sorted(pairs))  28.8 us
    ppermute x16, starting transfers between devices, move(): return lax.ppermute(value, AXES, sorted(pairs))  18.9 us
    all_to_all x1, blocking collectives, finish(): got = lax.all_to_all(packed, 'z', 0, 0, tiled=True)  18.3 us
    pallas_call x13, Pallas kernels, call(): pl.pallas_call(body, out_shape=[jax.ShapeDtypeStruct(s, d) for s, d in ou...  16.4 us
    all_to_all x1, blocking collectives, finish(): every = lax.all_to_all(copies, ('y', 'xl'), 0, 0, tiled=True)  14.3 us
    unnamed x8, local copies, waits for them, and re-layouts  2.87 us
  transfers between devices with their start and end apart: 16, of which 10 were waited for; matrix products, arithmetic and copies ran while one was open for 0% of the time, Pallas kernels for 8%

profile of v6, /device:TPU:4, one launch (start us, length us, event | category | flops | bytes accessed | tf_op | source)
XLA Modules:
  0.0 100.4 jit_solution(4735052802358743030)
XLA Ops:
  0.7 1.0 %copy-done.1 = bf16[256,1024]{1,0:T(8,128)(2,1)S(1)} copy-done((bf16[256,1024]{1,0:T(8,128)(2,1)S(1)}, bf16[256,1024]{1,0:T(8,128)(2,1)}, u32[]{:S(2)}) %copy-start.1) | copy-done | bytes 524312
  1.8 0.7 copy-done.2
  2.4 1.1 %copy-done.3 = bf16[256,1536]{1,0:T(8,128)(2,1)S(1)} copy-done((bf16[256,1536]{1,0:T(8,128)(2,1)S(1)}, bf16[256,1536]{1,0:T(8,128)(2,1)}, u32[]{:S(2)}) %copy-start.3) | copy-done | bytes 786456
  3.6 7.2 %gelu_pass.1 = (bf16[256,2048]{1,0:T(8,128)(2,1)S(1)}, f32[256,1024]{1,0:T(8,128)S(1)}, f32[256,1]{1,0:T(8,128)S(1)}, bf16[16,144,256]{2,1,0:T(8,128)(2,1)S(1)}, bf16[16,144,256]{2,1,0:T(8,128)(2,1)S(1)}) custom-call(s32[4]{0:T(128)S(1)} %pad_add_fusion.pos, f32[1,1024]{1,0:T(1,128)S(1)} %bitcast.7, bf16[256,1536]{1,0:T(8,128)(2,1)S(1)} %copy-done.3, ...), custom_call_target="tpu_custom_call" | custom-call | flops 8000000000 | bytes 1048576 | tf_op jit(solution)/shard_map/gelu_pass/pallas_call | solution.py:37
  11.5 1.6 %norm_back.1.em = bf16[256,1024]{1,0:T(8,128)(2,1)S(1)} custom-call(f32[1,1024]{1,0:T(1,128)S(1)} %bitcast.8, bf16[256,2048]{1,0:T(8,128)(2,1)S(1)} %get-tuple-element.35.preact_grad.gm, bf16[1024,2048]{1,0:T(8,128)(2,1)S(1)} %copy-done, bf16[256,1024]{1,0:T(8,128)(2,1)S(1)} %copy-done.1, f32[256,1024]{1,0:T(8,128)S(1)} %get-tuple-element.36.normal, ...), custom_call_target="tpu_custom_call" | custom-call | flops 2000000000 | bytes 1048576 | tf_op jit(solution)/shard_map/norm_back/pallas_call | solution.py:37
  13.1 0.5 collective-permute-start
  13.6 2.4 %collective-permute-done.2.cr = bf16[256,1024]{1,0:T(8,128)(2,1)S(1)} collective-permute-done((bf16[256,1024]{1,0:T(8,128)(2,1)S(1)}, bf16[256,1024]{1,0:T(8,128)(2,1)S(1)}, u32[]{:S(2)}, u32[]{:S(2)}) %collective-permute-start.2) | collective-permute-done | bytes 524320 | tf_op jit(solution)/shard_map/ppermute | solution.py:33
  16.0 2.4 %terms_x.1 = (bf16[4,768,128]{2,1,0:T(8,128)(2,1)S(1)}, bf16[4,768,128]{2,1,0:T(8,128)(2,1)S(1)}, bf16[4,768,128]{2,1,0:T(8,128)(2,1)S(1)}, bf16[4,768,128]{2,1,0:T(8,128)(2,1)S(1)}) custom-call(s32[4]{0:T(128)S(1)} %pad_add_fusion.pos, bf16[8,2,144,256]{3,2,1,0:T(8,128)(2,1)S(1)} %bitcast.11, bf16[8,2,144,256]{3,2,1,0:T(8,128)(2,1)S(1)} %bitcast.9, ...), custom_call_target="tpu_custom_call" | custom-call | flops 2000000000 | bytes 1048576 | tf_op jit(solution)/shard_map/terms_x/pallas_call | solution.py:37
  18.4 1.3 %collective-permute-start.5 = (bf16[4,768,128]{2,1,0:T(8,128)(2,1)S(1)}, bf16[4,768,128]{2,1,0:T(8,128)(2,1)S(1)}, u32[]{:S(2)}, u32[]{:S(2)}) collective-permute-start(bf16[4,768,128]{2,1,0:T(8,128)(2,1)S(1)} %get-tuple-element.47), channel_id=1, source_target_pairs={{0,32},{1,35},{2,34},{3,33},{4,36},{5,39},{6,38},{7,37},{8,40},{9,... | collective-permute-start | bytes 2359304 | tf_op jit(solution)/shard_map/ppermute | solution.py:33
  19.7 2.1 %terms_y.1 = (bf16[4,640,128]{2,1,0:T(8,128)(2,1)S(1)}, bf16[4,640,128]{2,1,0:T(8,128)(2,1)S(1)}, bf16[4,640,128]{2,1,0:T(8,128)(2,1)S(1)}, bf16[4,640,128]{2,1,0:T(8,128)(2,1)S(1)}) custom-call(s32[4]{0:T(128)S(1)} %pad_add_fusion.pos, bf16[8,2,144,256]{3,2,1,0:T(8,128)(2,1)S(1)} %bitcast.12, bf16[8,2,144,256]{3,2,1,0:T(8,128)(2,1)S(1)} %bitcast.10, ...), custom_call_target="tpu_custom_call" | custom-call | flops 2000000000 | bytes 1048576 | tf_op jit(solution)/shard_map/terms_y/pallas_call | solution.py:37
  21.8 1.8 %collective-permute-start.10 = (bf16[4,640,128]{2,1,0:T(8,128)(2,1)S(1)}, bf16[4,640,128]{2,1,0:T(8,128)(2,1)S(1)}, u32[]{:S(2)}, u32[]{:S(2)}) collective-permute-start(bf16[4,640,128]{2,1,0:T(8,128)(2,1)S(1)} %get-tuple-element.56), channel_id=1, source_target_pairs={{0,64},{1,193},{2,66},{3,195},{4,68},{5,197},{6,70},{7,199},{8,72}... | collective-permute-start | bytes 1966088 | tf_op jit(solution)/shard_map/ppermute | solution.py:33
  23.6 1.7 %collective-permute-start.11 = (bf16[4,640,128]{2,1,0:T(8,128)(2,1)S(1)}, bf16[4,640,128]{2,1,0:T(8,128)(2,1)S(1)}, u32[]{:S(2)}, u32[]{:S(2)}) collective-permute-start(bf16[4,640,128]{2,1,0:T(8,128)(2,1)S(1)} %get-tuple-element.57), channel_id=1, source_target_pairs={{0,192},{1,65},{2,194},{3,67},{4,196},{5,69},{6,198},{7,71},{8,200... | collective-permute-start | bytes 1966088 | tf_op jit(solution)/shard_map/ppermute | solution.py:33
  25.3 0.8 collective-permute-start.4
  26.1 8.2 %collective-permute-done.5.got = bf16[4,768,128]{2,1,0:T(8,128)(2,1)S(1)} collective-permute-done((bf16[4,768,128]{2,1,0:T(8,128)(2,1)S(1)}, bf16[4,768,128]{2,1,0:T(8,128)(2,1)S(1)}, u32[]{:S(2)}, u32[]{:S(2)}) %collective-permute-start.5) | collective-permute-done | bytes 786464 | tf_op jit(solution)/shard_map/ppermute | solution.py:33
  34.5 1.0 collective-permute-start.6
  35.5 4.4 %collective-permute-done.10.got = bf16[4,640,128]{2,1,0:T(8,128)(2,1)S(1)} collective-permute-done((bf16[4,640,128]{2,1,0:T(8,128)(2,1)S(1)}, bf16[4,640,128]{2,1,0:T(8,128)(2,1)S(1)}, u32[]{:S(2)}, u32[]{:S(2)}) %collective-permute-start.10) | collective-permute-done | bytes 655392 | tf_op jit(solution)/shard_map/ppermute | solution.py:33
  40.1 1.1 %collective-permute-start.12 = (bf16[4,640,128]{2,1,0:T(8,128)(2,1)S(1)}, bf16[4,640,128]{2,1,0:T(8,128)(2,1)S(1)}, u32[]{:S(2)}, u32[]{:S(2)}) collective-permute-start(bf16[4,640,128]{2,1,0:T(8,128)(2,1)S(1)} %pass_on.6), channel_id=1, source_target_pairs={{0,64},{1,193},{2,66},{3,195},{4,68},{5,197},{6,70},{7,199},{8,72}... | collective-permute-start | bytes 1966088 | tf_op jit(solution)/shard_map/ppermute | solution.py:33
  41.1 1.6 %collective-permute-done.4.near = bf16[4,768,128]{2,1,0:T(8,128)(2,1)S(1)} collective-permute-done((bf16[4,768,128]{2,1,0:T(8,128)(2,1)S(1)}, bf16[4,768,128]{2,1,0:T(8,128)(2,1)S(1)}, u32[]{:S(2)}, u32[]{:S(2)}) %collective-permute-start.4) | collective-permute-done | bytes 786464 | tf_op jit(solution)/shard_map/ppermute | solution.py:33
  42.8 4.6 %collective-permute-done.6.far = bf16[4,768,128]{2,1,0:T(8,128)(2,1)S(1)} collective-permute-done((bf16[4,768,128]{2,1,0:T(8,128)(2,1)S(1)}, bf16[4,768,128]{2,1,0:T(8,128)(2,1)S(1)}, u32[]{:S(2)}, u32[]{:S(2)}) %collective-permute-start.6) | collective-permute-done | bytes 786464 | tf_op jit(solution)/shard_map/ppermute | solution.py:33
  47.3 0.8 ring_turn_x.1
  48.2 2.2 %collective-permute-start.7 = (bf16[768,128]{1,0:T(8,128)(2,1)S(1)}, bf16[768,128]{1,0:T(8,128)(2,1)S(1)}, u32[]{:S(2)}, u32[]{:S(2)}) collective-permute-start(bf16[768,128]{1,0:T(8,128)(2,1)S(1)} %get-tuple-element.49), channel_id=1, source_target_pairs={{0,64},{1,193},{2,66},{3,195},{4,68},{5,197},{6,70},{7,199},{8,72}... | collective-permute-start | bytes 589832 | tf_op jit(solution)/shard_map/ppermute | solution.py:33
  50.3 1.2 %collective-permute-start.8 = (bf16[768,128]{1,0:T(8,128)(2,1)S(1)}, bf16[768,128]{1,0:T(8,128)(2,1)S(1)}, u32[]{:S(2)}, u32[]{:S(2)}) collective-permute-start(bf16[768,128]{1,0:T(8,128)(2,1)S(1)} %get-tuple-element.50), channel_id=1, source_target_pairs={{0,192},{1,65},{2,194},{3,67},{4,196},{5,69},{6,198},{7,71},{8,200... | collective-permute-start | bytes 589832 | tf_op jit(solution)/shard_map/ppermute | solution.py:33
  51.9 0.8 ring_turn_y.1
  52.7 3.0 %collective-permute-start.13 = (bf16[640,128]{1,0:T(8,128)(2,1)S(1)}, bf16[640,128]{1,0:T(8,128)(2,1)S(1)}, u32[]{:S(2)}, u32[]{:S(2)}) collective-permute-start(bf16[640,128]{1,0:T(8,128)(2,1)S(1)} %get-tuple-element.62), channel_id=1, source_target_pairs={{0,32},{1,35},{2,34},{3,33},{4,36},{5,39},{6,38},{7,37},{8,40},{9,... | collective-permute-start | bytes 491528 | tf_op jit(solution)/shard_map/ppermute | solution.py:33
  56.2 1.5 %collective-permute-start.9 = (bf16[768,128]{1,0:T(8,128)(2,1)S(1)}, bf16[768,128]{1,0:T(8,128)(2,1)S(1)}, u32[]{:S(2)}, u32[]{:S(2)}) collective-permute-start(bf16[768,128]{1,0:T(8,128)(2,1)S(1)} %pass_on.5), channel_id=1, source_target_pairs={{0,64},{1,193},{2,66},{3,195},{4,68},{5,197},{6,70},{7,199},{8,72}... | collective-permute-start | bytes 589832 | tf_op jit(solution)/shard_map/ppermute | solution.py:33
  57.7 0.9 collective-permute-done.13.got
  58.6 2.7 %collective-permute-done.14.refs_4_ = bf16[640,128]{1,0:T(8,128)(2,1)S(1)} collective-permute-done((bf16[640,128]{1,0:T(8,128)(2,1)S(1)}, bf16[640,128]{1,0:T(8,128)(2,1)S(1)}, u32[]{:S(2)}, u32[]{:S(2)}) %collective-permute-start.14) | collective-permute-done | bytes 163872 | tf_op jit(solution)/shard_map/ppermute | solution.py:33
  61.3 2.3 %collective-permute-start.15 = (bf16[640,128]{1,0:T(8,128)(2,1)S(1)}, bf16[640,128]{1,0:T(8,128)(2,1)S(1)}, u32[]{:S(2)}, u32[]{:S(2)}) collective-permute-start(bf16[640,128]{1,0:T(8,128)(2,1)S(1)} %pass_on.7), channel_id=1, source_target_pairs={{0,32},{1,35},{2,34},{3,33},{4,36},{5,39},{6,38},{7,37},{8,40},{9,... | collective-permute-start | bytes 491528 | tf_op jit(solution)/shard_map/ppermute | solution.py:33
  63.6 3.1 %collective-permute-done.15.refs_5_ = bf16[640,128]{1,0:T(8,128)(2,1)S(1)} collective-permute-done((bf16[640,128]{1,0:T(8,128)(2,1)S(1)}, bf16[640,128]{1,0:T(8,128)(2,1)S(1)}, u32[]{:S(2)}, u32[]{:S(2)}) %collective-permute-start.15) | collective-permute-done | bytes 163872 | tf_op jit(solution)/shard_map/ppermute | solution.py:33
  66.9 18.3 %all_to_all.10.got = bf16[8,176,128]{2,1,0:T(8,128)(2,1)S(1)} all-to-all(bf16[8,176,128]{2,1,0:T(8,128)(2,1)S(1)} %z_pack.1), channel_id=1, replica_groups=mesh['y'=4,'xl'=2,'z'=8,'xh'=2,'c'=2] {'z'}, dimensions={0} | all-to-all | bytes 720896 | tf_op jit(solution)/shard_map/all_to_all | solution.py:298
  85.2 14.3 %all_to_all.11.got = bf16[8,176,128]{2,1,0:T(8,128)(2,1)S(1)} all-to-all(bf16[8,176,128]{2,1,0:T(8,128)(2,1)S(1)} %z_sum.1), channel_id=1, replica_groups=mesh['y'=4,'xl'=2,'z'=8,'xh'=2,'c'=2] {'y','xl'}, dimensions={0} | all-to-all | bytes 720896 | tf_op jit(solution)/shard_map/all_to_all | solution.py:300
  99.5 0.9 unpack.1
  (24 shorter events, 2.3 us)
Async XLA Ops:
  0.7 1.0 %copy-start.1 = (bf16[256,1024]{1,0:T(8,128)(2,1)S(1)}, bf16[256,1024]{1,0:T(8,128)(2,1)}, u32[]{:S(2)}) copy-start(bf16[256,1024]{1,0:T(8,128)(2,1)} %cm.1) | copy-start | bytes 1572868
  1.8 0.7 copy-start.2
  2.4 1.1 %copy-start.3 = (bf16[256,1536]{1,0:T(8,128)(2,1)S(1)}, bf16[256,1536]{1,0:T(8,128)(2,1)}, u32[]{:S(2)}) copy-start(bf16[256,1536]{1,0:T(8,128)(2,1)} %p.1) | copy-start | bytes 2359300
  3.6 7.9 %copy-start = (bf16[1024,2048]{1,0:T(8,128)(2,1)S(1)}, bf16[1024,2048]{1,0:T(8,128)(2,1)}, u32[]{:S(2)}) copy-start(bf16[1024,2048]{1,0:T(8,128)(2,1)} %up.1) | copy-start | bytes 12582916
  10.8 5.2 %collective-permute-start.1 = (bf16[16,144,256]{2,1,0:T(8,128)(2,1)S(1)}, bf16[16,144,256]{2,1,0:T(8,128)(2,1)S(1)}, u32[]{:S(2)}, u32[]{:S(2)}) collective-permute-start(bf16[16,144,256]{2,1,0:T(8,128)(2,1)S(1)} %get-tuple-element.39), channel_id=1, source_target_pairs={{0,1},{1,0},{2,3},{3,2},{4,5},{5,4},{6,7},{7,6},{8,9},{9,8},{10,11... | collective-permute-start | bytes 3538952 | tf_op jit(solution)/shard_map/ppermute | solution.py:33
  10.9 5.1 %collective-permute-start.3 = (bf16[256,2048]{1,0:T(8,128)(2,1)S(1)}, bf16[256,2048]{1,0:T(8,128)(2,1)S(1)}, u32[]{:S(2)}, u32[]{:S(2)}) collective-permute-start(bf16[256,2048]{1,0:T(8,128)(2,1)S(1)} %get-tuple-element.35.preact_grad.gm), channel_id=1, source_target_pairs={{0,1},{1,0},{2,3},{3,2},{4,5},{5,4},{6,7},{7,6},{8,9},{9,8},{10,11... | collective-permute-start | bytes 3145736 | tf_op jit(solution)/shard_map/ppermute | solution.py:33
  11.4 4.6 %collective-permute-start.2 = (bf16[256,1024]{1,0:T(8,128)(2,1)S(1)}, bf16[256,1024]{1,0:T(8,128)(2,1)S(1)}, u32[]{:S(2)}, u32[]{:S(2)}) collective-permute-start(bf16[256,1024]{1,0:T(8,128)(2,1)S(1)} %copy-done.1), channel_id=1, source_target_pairs={{0,1},{1,0},{2,3},{3,2},{4,5},{5,4},{6,7},{7,6},{8,9},{9,8},{10,11... | collective-permute-start | bytes 1572872 | tf_op jit(solution)/shard_map/ppermute | solution.py:33
  13.1 5.3 %collective-permute-start = (bf16[256,1024]{1,0:T(8,128)(2,1)S(1)}, bf16[256,1024]{1,0:T(8,128)(2,1)S(1)}, u32[]{:S(2)}, u32[]{:S(2)}) collective-permute-start(bf16[256,1024]{1,0:T(8,128)(2,1)S(1)} %norm_back.1.em), channel_id=1, source_target_pairs={{0,1},{1,0},{2,3},{3,2},{4,5},{5,4},{6,7},{7,6},{8,9},{9,8},{10,11... | collective-permute-start | bytes 1572872 | tf_op jit(solution)/shard_map/ppermute | solution.py:33
  18.4 15.9 %collective-permute-start.5 = (bf16[4,768,128]{2,1,0:T(8,128)(2,1)S(1)}, bf16[4,768,128]{2,1,0:T(8,128)(2,1)S(1)}, u32[]{:S(2)}, u32[]{:S(2)}) collective-permute-start(bf16[4,768,128]{2,1,0:T(8,128)(2,1)S(1)} %get-tuple-element.47), channel_id=1, source_target_pairs={{0,32},{1,35},{2,34},{3,33},{4,36},{5,39},{6,38},{7,37},{8,40},{9,... | collective-permute-start | bytes 2359304 | tf_op jit(solution)/shard_map/ppermute | solution.py:33
  21.8 18.1 %collective-permute-start.10 = (bf16[4,640,128]{2,1,0:T(8,128)(2,1)S(1)}, bf16[4,640,128]{2,1,0:T(8,128)(2,1)S(1)}, u32[]{:S(2)}, u32[]{:S(2)}) collective-permute-start(bf16[4,640,128]{2,1,0:T(8,128)(2,1)S(1)} %get-tuple-element.56), channel_id=1, source_target_pairs={{0,64},{1,193},{2,66},{3,195},{4,68},{5,197},{6,70},{7,199},{8,72}... | collective-permute-start | bytes 1966088 | tf_op jit(solution)/shard_map/ppermute | solution.py:33
  23.6 16.3 %collective-permute-start.11 = (bf16[4,640,128]{2,1,0:T(8,128)(2,1)S(1)}, bf16[4,640,128]{2,1,0:T(8,128)(2,1)S(1)}, u32[]{:S(2)}, u32[]{:S(2)}) collective-permute-start(bf16[4,640,128]{2,1,0:T(8,128)(2,1)S(1)} %get-tuple-element.57), channel_id=1, source_target_pairs={{0,192},{1,65},{2,194},{3,67},{4,196},{5,69},{6,198},{7,71},{8,200... | collective-permute-start | bytes 1966088 | tf_op jit(solution)/shard_map/ppermute | solution.py:33
  25.3 17.5 %collective-permute-start.4 = (bf16[4,768,128]{2,1,0:T(8,128)(2,1)S(1)}, bf16[4,768,128]{2,1,0:T(8,128)(2,1)S(1)}, u32[]{:S(2)}, u32[]{:S(2)}) collective-permute-start(bf16[4,768,128]{2,1,0:T(8,128)(2,1)S(1)} %get-tuple-element.45), channel_id=1, source_target_pairs={{0,34},{1,33},{2,32},{3,35},{4,38},{5,37},{6,36},{7,39},{8,42},{9,... | collective-permute-start | bytes 2359304 | tf_op jit(solution)/shard_map/ppermute | solution.py:33
  34.5 12.8 %collective-permute-start.6 = (bf16[4,768,128]{2,1,0:T(8,128)(2,1)S(1)}, bf16[4,768,128]{2,1,0:T(8,128)(2,1)S(1)}, u32[]{:S(2)}, u32[]{:S(2)}) collective-permute-start(bf16[4,768,128]{2,1,0:T(8,128)(2,1)S(1)} %pass_on.4), channel_id=1, source_target_pairs={{0,32},{1,35},{2,34},{3,33},{4,36},{5,39},{6,38},{7,37},{8,40},{9,... | collective-permute-start | bytes 2359304 | tf_op jit(solution)/shard_map/ppermute | solution.py:33
  40.1 11.9 %collective-permute-start.12 = (bf16[4,640,128]{2,1,0:T(8,128)(2,1)S(1)}, bf16[4,640,128]{2,1,0:T(8,128)(2,1)S(1)}, u32[]{:S(2)}, u32[]{:S(2)}) collective-permute-start(bf16[4,640,128]{2,1,0:T(8,128)(2,1)S(1)} %pass_on.6), channel_id=1, source_target_pairs={{0,64},{1,193},{2,66},{3,195},{4,68},{5,197},{6,70},{7,199},{8,72}... | collective-permute-start | bytes 1966088 | tf_op jit(solution)/shard_map/ppermute | solution.py:33
  48.2 8.0 %collective-permute-start.7 = (bf16[768,128]{1,0:T(8,128)(2,1)S(1)}, bf16[768,128]{1,0:T(8,128)(2,1)S(1)}, u32[]{:S(2)}, u32[]{:S(2)}) collective-permute-start(bf16[768,128]{1,0:T(8,128)(2,1)S(1)} %get-tuple-element.49), channel_id=1, source_target_pairs={{0,64},{1,193},{2,66},{3,195},{4,68},{5,197},{6,70},{7,199},{8,72}... | collective-permute-start | bytes 589832 | tf_op jit(solution)/shard_map/ppermute | solution.py:33
  50.3 5.9 %collective-permute-start.8 = (bf16[768,128]{1,0:T(8,128)(2,1)S(1)}, bf16[768,128]{1,0:T(8,128)(2,1)S(1)}, u32[]{:S(2)}, u32[]{:S(2)}) collective-permute-start(bf16[768,128]{1,0:T(8,128)(2,1)S(1)} %get-tuple-element.50), channel_id=1, source_target_pairs={{0,192},{1,65},{2,194},{3,67},{4,196},{5,69},{6,198},{7,71},{8,200... | collective-permute-start | bytes 589832 | tf_op jit(solution)/shard_map/ppermute | solution.py:33
  52.7 5.8 %collective-permute-start.13 = (bf16[640,128]{1,0:T(8,128)(2,1)S(1)}, bf16[640,128]{1,0:T(8,128)(2,1)S(1)}, u32[]{:S(2)}, u32[]{:S(2)}) collective-permute-start(bf16[640,128]{1,0:T(8,128)(2,1)S(1)} %get-tuple-element.62), channel_id=1, source_target_pairs={{0,32},{1,35},{2,34},{3,33},{4,36},{5,39},{6,38},{7,37},{8,40},{9,... | collective-permute-start | bytes 491528 | tf_op jit(solution)/shard_map/ppermute | solution.py:33
  55.7 5.6 %collective-permute-start.14 = (bf16[640,128]{1,0:T(8,128)(2,1)S(1)}, bf16[640,128]{1,0:T(8,128)(2,1)S(1)}, u32[]{:S(2)}, u32[]{:S(2)}) collective-permute-start(bf16[640,128]{1,0:T(8,128)(2,1)S(1)} %get-tuple-element.63), channel_id=1, source_target_pairs={{0,34},{1,33},{2,32},{3,35},{4,38},{5,37},{6,36},{7,39},{8,42},{9,... | collective-permute-start | bytes 491528 | tf_op jit(solution)/shard_map/ppermute | solution.py:33
  56.2 10.5 %collective-permute-start.9 = (bf16[768,128]{1,0:T(8,128)(2,1)S(1)}, bf16[768,128]{1,0:T(8,128)(2,1)S(1)}, u32[]{:S(2)}, u32[]{:S(2)}) collective-permute-start(bf16[768,128]{1,0:T(8,128)(2,1)S(1)} %pass_on.5), channel_id=1, source_target_pairs={{0,64},{1,193},{2,66},{3,195},{4,68},{5,197},{6,70},{7,199},{8,72}... | collective-permute-start | bytes 589832 | tf_op jit(solution)/shard_map/ppermute | solution.py:33
  61.3 5.4 %collective-permute-start.15 = (bf16[640,128]{1,0:T(8,128)(2,1)S(1)}, bf16[640,128]{1,0:T(8,128)(2,1)S(1)}, u32[]{:S(2)}, u32[]{:S(2)}) collective-permute-start(bf16[640,128]{1,0:T(8,128)(2,1)S(1)} %pass_on.7), channel_id=1, source_target_pairs={{0,32},{1,35},{2,34},{3,33},{4,36},{5,39},{6,38},{7,37},{8,40},{9,... | collective-permute-start | bytes 491528 | tf_op jit(solution)/shard_map/ppermute | solution.py:33

commit v7 on v5

--- a/solution.py
+++ b/solution.py
@@ -149,7 +149,7 @@
 
 
 ROWS = 176
-SPLIT = 4
+SPLIT = 5
 CHUNK_X = 512 + SPLIT * 64
 CHUNK_Y = (8 - SPLIT) * 64 + 384
 
@@ -159,9 +159,8 @@
 
 
 def dot2(lefts, rights):
-    acc = jnp.dot(lefts[0], rights[0], preferred_element_type=F32)
-    acc += jnp.dot(lefts[1], rights[1], preferred_element_type=F32)
-    return acc.astype(BF)
+    left, right = jnp.concatenate(lefts, axis=1), jnp.concatenate(rights, axis=0)
+    return jnp.dot(left, right, preferred_element_type=F32).astype(BF)
 
 
 def columns(ref, starts, width):
@@ -312,6 +311,7 @@
     preact_grad, normal, inverse, mine, send = gelu_pass(
         pos, gain, patches, cotangent, stem_weight, up_weight, down_weight
     )
+    send, cot_other = lax.optimization_barrier((send, cot_other))
     other = move(send, "c", 0)
     preact_other = move(preact_grad, "c", 0)
     (embed_grad,) = call(

time: 99.6 us -> 100 us (level)
  waiting for transfers between devices: 30 us -> 27 us
  blocking collectives: 31.5 us -> 33.8 us
  starting transfers between devices: 17.5 us -> 18.9 us
    ppermute x16, waiting for transfers between devices: 30 us -> 27 us  [move(): return lax.ppermute(value, AXES, sorted(pairs))]
    all_to_all x1, blocking collectives: 18.5 us -> 21.3 us  [finish(): got = lax.all_to_all(packed, 'z', 0, 0, tiled=True)]
    ppermute x16, starting transfers between devices: 17.5 us -> 18.9 us  [move(): return lax.ppermute(value, AXES, sorted(pairs))]
  transfers between devices with their start and end apart: 16 -> 16, of which waited for: 9 -> 9; matrix products, arithmetic and copies ran while one was open for 0% -> 0% of each run, Pallas kernels for 8% -> 15%
where the time goes in v7:
time: 100 us; the launch traced here: 99.9 us
  blocking collectives  33.8 us (34%)
  waiting for transfers between devices  27 us (27%)
  starting transfers between devices  18.9 us (19%)
  Pallas kernels  16.5 us (16%)
  local copies, waits for them, and re-layouts  2.87 us (3%)
    ppermute x16, waiting for transfers between devices, move(): return lax.ppermute(value, AXES, sorted(pairs))  27 us
    all_to_all x1, blocking collectives, finish(): got = lax.all_to_all(packed, 'z', 0, 0, tiled=True)  21.3 us
    ppermute x16, starting transfers between devices, move(): return lax.ppermute(value, AXES, sorted(pairs))  18.9 us
    pallas_call x13, Pallas kernels, call(): pl.pallas_call(body, out_shape=[jax.ShapeDtypeStruct(s, d) for s, d in ou...  16.5 us
    all_to_all x1, blocking collectives, finish(): every = lax.all_to_all(copies, ('y', 'xl'), 0, 0, tiled=True)  12.5 us
    unnamed x8, local copies, waits for them, and re-layouts  2.87 us
  transfers between devices with their start and end apart: 16, of which 9 were waited for; matrix products, arithmetic and copies ran while one was open for 0% of the time, Pallas kernels for 15%

profile of v7, /device:TPU:4, one launch (start us, length us, event | category | flops | bytes accessed | tf_op | source)
XLA Modules:
  0.0 99.9 jit_solution(11061804212321967325)
XLA Ops:
  0.8 1.0 %copy-done.1 = bf16[256,1024]{1,0:T(8,128)(2,1)S(1)} copy-done((bf16[256,1024]{1,0:T(8,128)(2,1)S(1)}, bf16[256,1024]{1,0:T(8,128)(2,1)}, u32[]{:S(2)}) %copy-start.1) | copy-done | bytes 524312
  1.9 0.7 copy-done.2
  2.6 1.1 %copy-done.3 = bf16[256,1536]{1,0:T(8,128)(2,1)S(1)} copy-done((bf16[256,1536]{1,0:T(8,128)(2,1)S(1)}, bf16[256,1536]{1,0:T(8,128)(2,1)}, u32[]{:S(2)}) %copy-start.3) | copy-done | bytes 786456
  3.7 7.2 %gelu_pass.1 = (bf16[256,2048]{1,0:T(8,128)(2,1)S(1)}, f32[256,1024]{1,0:T(8,128)S(1)}, f32[256,1]{1,0:T(8,128)S(1)}, bf16[16,144,256]{2,1,0:T(8,128)(2,1)S(1)}, bf16[16,144,256]{2,1,0:T(8,128)(2,1)S(1)}) custom-call(s32[4]{0:T(128)S(1)} %pad_add_fusion.pos, f32[1,1024]{1,0:T(1,128)S(1)} %bitcast.7, bf16[256,1536]{1,0:T(8,128)(2,1)S(1)} %copy-done.3, ...), custom_call_target="tpu_custom_call" | custom-call | flops 8000000000 | bytes 1048576 | tf_op jit(solution)/shard_map/gelu_pass/pallas_call | solution.py:37
  11.6 1.6 %norm_back.1.em = bf16[256,1024]{1,0:T(8,128)(2,1)S(1)} custom-call(f32[1,1024]{1,0:T(1,128)S(1)} %bitcast.8, bf16[256,2048]{1,0:T(8,128)(2,1)S(1)} %get-tuple-element.35.preact_grad.gm, bf16[1024,2048]{1,0:T(8,128)(2,1)S(1)} %copy-done, bf16[256,1024]{1,0:T(8,128)(2,1)S(1)} %copy-done.1, f32[256,1024]{1,0:T(8,128)S(1)} %get-tuple-element.36.normal, ...), custom_call_target="tpu_custom_call" | custom-call | flops 2000000000 | bytes 1048576 | tf_op jit(solution)/shard_map/norm_back/pallas_call | solution.py:37
  13.7 1.8 %collective-permute-done.3.gr = bf16[256,2048]{1,0:T(8,128)(2,1)S(1)} collective-permute-done((bf16[256,2048]{1,0:T(8,128)(2,1)S(1)}, bf16[256,2048]{1,0:T(8,128)(2,1)S(1)}, u32[]{:S(2)}, u32[]{:S(2)}) %collective-permute-start.3) | collective-permute-done | bytes 1048608 | tf_op jit(solution)/shard_map/ppermute | solution.py:33
  15.5 2.5 %terms_x.1 = (bf16[4,832,128]{2,1,0:T(8,128)(2,1)S(1)}, bf16[4,832,128]{2,1,0:T(8,128)(2,1)S(1)}, bf16[4,832,128]{2,1,0:T(8,128)(2,1)S(1)}, bf16[4,832,128]{2,1,0:T(8,128)(2,1)S(1)}) custom-call(s32[4]{0:T(128)S(1)} %pad_add_fusion.pos, bf16[8,2,144,256]{3,2,1,0:T(8,128)(2,1)S(1)} %bitcast.11, bf16[8,2,144,256]{3,2,1,0:T(8,128)(2,1)S(1)} %bitcast.9, ...), custom_call_target="tpu_custom_call" | custom-call | flops 2000000000 | bytes 1048576 | tf_op jit(solution)/shard_map/terms_x/pallas_call | solution.py:37
  18.0 1.3 %collective-permute-start.5 = (bf16[4,832,128]{2,1,0:T(8,128)(2,1)S(1)}, bf16[4,832,128]{2,1,0:T(8,128)(2,1)S(1)}, u32[]{:S(2)}, u32[]{:S(2)}) collective-permute-start(bf16[4,832,128]{2,1,0:T(8,128)(2,1)S(1)} %get-tuple-element.49), channel_id=1, source_target_pairs={{0,32},{1,35},{2,34},{3,33},{4,36},{5,39},{6,38},{7,37},{8,40},{9,... | collective-permute-start | bytes 2555912 | tf_op jit(solution)/shard_map/ppermute | solution.py:33
  19.3 2.0 %terms_y.1 = (bf16[4,576,128]{2,1,0:T(8,128)(2,1)S(1)}, bf16[4,576,128]{2,1,0:T(8,128)(2,1)S(1)}, bf16[4,576,128]{2,1,0:T(8,128)(2,1)S(1)}, bf16[4,576,128]{2,1,0:T(8,128)(2,1)S(1)}) custom-call(s32[4]{0:T(128)S(1)} %pad_add_fusion.pos, bf16[8,2,144,256]{3,2,1,0:T(8,128)(2,1)S(1)} %bitcast.12, bf16[8,2,144,256]{3,2,1,0:T(8,128)(2,1)S(1)} %bitcast.10, ...), custom_call_target="tpu_custom_call" | custom-call | flops 2000000000 | bytes 1048576 | tf_op jit(solution)/shard_map/terms_y/pallas_call | solution.py:37
  21.3 1.8 %collective-permute-start.10 = (bf16[4,576,128]{2,1,0:T(8,128)(2,1)S(1)}, bf16[4,576,128]{2,1,0:T(8,128)(2,1)S(1)}, u32[]{:S(2)}, u32[]{:S(2)}) collective-permute-start(bf16[4,576,128]{2,1,0:T(8,128)(2,1)S(1)} %get-tuple-element.56), channel_id=1, source_target_pairs={{0,64},{1,193},{2,66},{3,195},{4,68},{5,197},{6,70},{7,199},{8,72}... | collective-permute-start | bytes 1769480 | tf_op jit(solution)/shard_map/ppermute | solution.py:33
  23.2 1.7 %collective-permute-start.11 = (bf16[4,576,128]{2,1,0:T(8,128)(2,1)S(1)}, bf16[4,576,128]{2,1,0:T(8,128)(2,1)S(1)}, u32[]{:S(2)}, u32[]{:S(2)}) collective-permute-start(bf16[4,576,128]{2,1,0:T(8,128)(2,1)S(1)} %get-tuple-element.57), channel_id=1, source_target_pairs={{0,192},{1,65},{2,194},{3,67},{4,196},{5,69},{6,198},{7,71},{8,200... | collective-permute-start | bytes 1769480 | tf_op jit(solution)/shard_map/ppermute | solution.py:33
  24.8 0.8 collective-permute-start.4
  25.7 9.5 %collective-permute-done.5.got = bf16[4,832,128]{2,1,0:T(8,128)(2,1)S(1)} collective-permute-done((bf16[4,832,128]{2,1,0:T(8,128)(2,1)S(1)}, bf16[4,832,128]{2,1,0:T(8,128)(2,1)S(1)}, u32[]{:S(2)}, u32[]{:S(2)}) %collective-permute-start.5) | collective-permute-done | bytes 852000 | tf_op jit(solution)/shard_map/ppermute | solution.py:33
  35.4 1.0 collective-permute-start.6
  36.3 1.4 %collective-permute-done.10.got = bf16[4,576,128]{2,1,0:T(8,128)(2,1)S(1)} collective-permute-done((bf16[4,576,128]{2,1,0:T(8,128)(2,1)S(1)}, bf16[4,576,128]{2,1,0:T(8,128)(2,1)S(1)}, u32[]{:S(2)}, u32[]{:S(2)}) %collective-permute-start.10) | collective-permute-done | bytes 589856 | tf_op jit(solution)/shard_map/ppermute | solution.py:33
  37.9 1.6 %collective-permute-start.12 = (bf16[4,576,128]{2,1,0:T(8,128)(2,1)S(1)}, bf16[4,576,128]{2,1,0:T(8,128)(2,1)S(1)}, u32[]{:S(2)}, u32[]{:S(2)}) collective-permute-start(bf16[4,576,128]{2,1,0:T(8,128)(2,1)S(1)} %pass_on.6), channel_id=1, source_target_pairs={{0,64},{1,193},{2,66},{3,195},{4,68},{5,197},{6,70},{7,199},{8,72}... | collective-permute-start | bytes 1769480 | tf_op jit(solution)/shard_map/ppermute | solution.py:33
  39.5 4.4 %collective-permute-done.4.near = bf16[4,832,128]{2,1,0:T(8,128)(2,1)S(1)} collective-permute-done((bf16[4,832,128]{2,1,0:T(8,128)(2,1)S(1)}, bf16[4,832,128]{2,1,0:T(8,128)(2,1)S(1)}, u32[]{:S(2)}, u32[]{:S(2)}) %collective-permute-start.4) | collective-permute-done | bytes 852000 | tf_op jit(solution)/shard_map/ppermute | solution.py:33
  43.8 5.2 %collective-permute-done.6.far = bf16[4,832,128]{2,1,0:T(8,128)(2,1)S(1)} collective-permute-done((bf16[4,832,128]{2,1,0:T(8,128)(2,1)S(1)}, bf16[4,832,128]{2,1,0:T(8,128)(2,1)S(1)}, u32[]{:S(2)}, u32[]{:S(2)}) %collective-permute-start.6) | collective-permute-done | bytes 852000 | tf_op jit(solution)/shard_map/ppermute | solution.py:33
  49.1 0.9 ring_turn_x.1
  49.9 2.0 %collective-permute-start.8 = (bf16[832,128]{1,0:T(8,128)(2,1)S(1)}, bf16[832,128]{1,0:T(8,128)(2,1)S(1)}, u32[]{:S(2)}, u32[]{:S(2)}) collective-permute-start(bf16[832,128]{1,0:T(8,128)(2,1)S(1)} %get-tuple-element.53), channel_id=1, source_target_pairs={{0,64},{1,193},{2,66},{3,195},{4,68},{5,197},{6,70},{7,199},{8,72}... | collective-permute-start | bytes 638984 | tf_op jit(solution)/shard_map/ppermute | solution.py:33
  51.9 0.8 ring_turn_y.1
  52.7 1.0 collective-permute-start.13
  53.7 1.1 %collective-permute-start.14 = (bf16[576,128]{1,0:T(8,128)(2,1)S(1)}, bf16[576,128]{1,0:T(8,128)(2,1)S(1)}, u32[]{:S(2)}, u32[]{:S(2)}) collective-permute-start(bf16[576,128]{1,0:T(8,128)(2,1)S(1)} %get-tuple-element.63), channel_id=1, source_target_pairs={{0,34},{1,33},{2,32},{3,35},{4,38},{5,37},{6,36},{7,39},{8,42},{9,... | collective-permute-start | bytes 442376 | tf_op jit(solution)/shard_map/ppermute | solution.py:33
  54.8 1.3 %collective-permute-start.7 = (bf16[832,128]{1,0:T(8,128)(2,1)S(1)}, bf16[832,128]{1,0:T(8,128)(2,1)S(1)}, u32[]{:S(2)}, u32[]{:S(2)}) collective-permute-start(bf16[832,128]{1,0:T(8,128)(2,1)S(1)} %get-tuple-element.51), channel_id=1, source_target_pairs={{0,192},{1,65},{2,194},{3,67},{4,196},{5,69},{6,198},{7,71},{8,200... | collective-permute-start | bytes 638984 | tf_op jit(solution)/shard_map/ppermute | solution.py:33
  56.1 0.9 collective-permute-done.8.got
  57.1 1.0 %collective-permute-start.9 = (bf16[832,128]{1,0:T(8,128)(2,1)S(1)}, bf16[832,128]{1,0:T(8,128)(2,1)S(1)}, u32[]{:S(2)}, u32[]{:S(2)}) collective-permute-start(bf16[832,128]{1,0:T(8,128)(2,1)S(1)} %pass_on.5), channel_id=1, source_target_pairs={{0,64},{1,193},{2,66},{3,195},{4,68},{5,197},{6,70},{7,199},{8,72}... | collective-permute-start | bytes 638984 | tf_op jit(solution)/shard_map/ppermute | solution.py:33
  58.1 0.9 collective-permute-done.13.got
  59.2 3.0 %collective-permute-start.15 = (bf16[576,128]{1,0:T(8,128)(2,1)S(1)}, bf16[576,128]{1,0:T(8,128)(2,1)S(1)}, u32[]{:S(2)}, u32[]{:S(2)}) collective-permute-start(bf16[576,128]{1,0:T(8,128)(2,1)S(1)} %pass_on.7), channel_id=1, source_target_pairs={{0,32},{1,35},{2,34},{3,33},{4,36},{5,39},{6,38},{7,37},{8,40},{9,... | collective-permute-start | bytes 442376 | tf_op jit(solution)/shard_map/ppermute | solution.py:33
  62.3 2.7 %collective-permute-done.15.refs_5_ = bf16[576,128]{1,0:T(8,128)(2,1)S(1)} collective-permute-done((bf16[576,128]{1,0:T(8,128)(2,1)S(1)}, bf16[576,128]{1,0:T(8,128)(2,1)S(1)}, u32[]{:S(2)}, u32[]{:S(2)}) %collective-permute-start.15) | collective-permute-done | bytes 147488 | tf_op jit(solution)/shard_map/ppermute | solution.py:33
  65.1 21.3 %all_to_all.10.got = bf16[8,176,128]{2,1,0:T(8,128)(2,1)S(1)} all-to-all(bf16[8,176,128]{2,1,0:T(8,128)(2,1)S(1)} %z_pack.1), channel_id=1, replica_groups=mesh['y'=4,'xl'=2,'z'=8,'xh'=2,'c'=2] {'z'}, dimensions={0} | all-to-all | bytes 720896 | tf_op jit(solution)/shard_map/all_to_all | solution.py:297
  86.5 12.5 %all_to_all.11.got = bf16[8,176,128]{2,1,0:T(8,128)(2,1)S(1)} all-to-all(bf16[8,176,128]{2,1,0:T(8,128)(2,1)S(1)} %z_sum.1), channel_id=1, replica_groups=mesh['y'=4,'xl'=2,'z'=8,'xh'=2,'c'=2] {'y','xl'}, dimensions={0} | all-to-all | bytes 720896 | tf_op jit(solution)/shard_map/all_to_all | solution.py:299
  99.0 0.9 unpack.1
  (24 shorter events, 2.1 us)
Async XLA Ops:
  0.6 10.3 %collective-permute-start.1 = (bf16[256,1024]{1,0:T(8,128)(2,1)}, bf16[256,1024]{1,0:T(8,128)(2,1)S(1)}, u32[]{:S(2)}, u32[]{:S(2)}) collective-permute-start(bf16[256,1024]{1,0:T(8,128)(2,1)} %cm.1), channel_id=1, source_target_pairs={{0,1},{1,0},{2,3},{3,2},{4,5},{5,4},{6,7},{7,6},{8,9},{9,8},{10,11... | collective-permute-start | bytes 1572872 | tf_op jit(solution)/shard_map/ppermute | solution.py:33
  0.8 1.0 %copy-start.1 = (bf16[256,1024]{1,0:T(8,128)(2,1)S(1)}, bf16[256,1024]{1,0:T(8,128)(2,1)}, u32[]{:S(2)}) copy-start(bf16[256,1024]{1,0:T(8,128)(2,1)} %cm.1) | copy-start | bytes 1572868
  1.9 0.7 copy-start.2
  2.5 1.1 %copy-start.3 = (bf16[256,1536]{1,0:T(8,128)(2,1)S(1)}, bf16[256,1536]{1,0:T(8,128)(2,1)}, u32[]{:S(2)}) copy-start(bf16[256,1536]{1,0:T(8,128)(2,1)} %p.1) | copy-start | bytes 2359300
  3.7 7.9 %copy-start = (bf16[1024,2048]{1,0:T(8,128)(2,1)S(1)}, bf16[1024,2048]{1,0:T(8,128)(2,1)}, u32[]{:S(2)}) copy-start(bf16[1024,2048]{1,0:T(8,128)(2,1)} %up.1) | copy-start | bytes 12582916
  10.9 4.5 %collective-permute-start.2 = (bf16[16,144,256]{2,1,0:T(8,128)(2,1)S(1)}, bf16[16,144,256]{2,1,0:T(8,128)(2,1)S(1)}, u32[]{:S(2)}, u32[]{:S(2)}) collective-permute-start(bf16[16,144,256]{2,1,0:T(8,128)(2,1)S(1)} %get-tuple-element.40), channel_id=1, source_target_pairs={{0,1},{1,0},{2,3},{3,2},{4,5},{5,4},{6,7},{7,6},{8,9},{9,8},{10,11... | collective-permute-start | bytes 3538952 | tf_op jit(solution)/shard_map/ppermute | solution.py:33
  11.5 4.0 %collective-permute-start.3 = (bf16[256,2048]{1,0:T(8,128)(2,1)S(1)}, bf16[256,2048]{1,0:T(8,128)(2,1)S(1)}, u32[]{:S(2)}, u32[]{:S(2)}) collective-permute-start(bf16[256,2048]{1,0:T(8,128)(2,1)S(1)} %get-tuple-element.35.preact_grad.gm), channel_id=1, source_target_pairs={{0,1},{1,0},{2,3},{3,2},{4,5},{5,4},{6,7},{7,6},{8,9},{9,8},{10,11... | collective-permute-start | bytes 3145736 | tf_op jit(solution)/shard_map/ppermute | solution.py:33
  13.2 4.8 %collective-permute-start = (bf16[256,1024]{1,0:T(8,128)(2,1)S(1)}, bf16[256,1024]{1,0:T(8,128)(2,1)S(1)}, u32[]{:S(2)}, u32[]{:S(2)}) collective-permute-start(bf16[256,1024]{1,0:T(8,128)(2,1)S(1)} %norm_back.1.em), channel_id=1, source_target_pairs={{0,1},{1,0},{2,3},{3,2},{4,5},{5,4},{6,7},{7,6},{8,9},{9,8},{10,11... | collective-permute-start | bytes 1572872 | tf_op jit(solution)/shard_map/ppermute | solution.py:33
  18.0 17.2 %collective-permute-start.5 = (bf16[4,832,128]{2,1,0:T(8,128)(2,1)S(1)}, bf16[4,832,128]{2,1,0:T(8,128)(2,1)S(1)}, u32[]{:S(2)}, u32[]{:S(2)}) collective-permute-start(bf16[4,832,128]{2,1,0:T(8,128)(2,1)S(1)} %get-tuple-element.49), channel_id=1, source_target_pairs={{0,32},{1,35},{2,34},{3,33},{4,36},{5,39},{6,38},{7,37},{8,40},{9,... | collective-permute-start | bytes 2555912 | tf_op jit(solution)/shard_map/ppermute | solution.py:33
  21.3 16.4 %collective-permute-start.10 = (bf16[4,576,128]{2,1,0:T(8,128)(2,1)S(1)}, bf16[4,576,128]{2,1,0:T(8,128)(2,1)S(1)}, u32[]{:S(2)}, u32[]{:S(2)}) collective-permute-start(bf16[4,576,128]{2,1,0:T(8,128)(2,1)S(1)} %get-tuple-element.56), channel_id=1, source_target_pairs={{0,64},{1,193},{2,66},{3,195},{4,68},{5,197},{6,70},{7,199},{8,72}... | collective-permute-start | bytes 1769480 | tf_op jit(solution)/shard_map/ppermute | solution.py:33
  23.2 14.6 %collective-permute-start.11 = (bf16[4,576,128]{2,1,0:T(8,128)(2,1)S(1)}, bf16[4,576,128]{2,1,0:T(8,128)(2,1)S(1)}, u32[]{:S(2)}, u32[]{:S(2)}) collective-permute-start(bf16[4,576,128]{2,1,0:T(8,128)(2,1)S(1)} %get-tuple-element.57), channel_id=1, source_target_pairs={{0,192},{1,65},{2,194},{3,67},{4,196},{5,69},{6,198},{7,71},{8,200... | collective-permute-start | bytes 1769480 | tf_op jit(solution)/shard_map/ppermute | solution.py:33
  24.8 19.0 %collective-permute-start.4 = (bf16[4,832,128]{2,1,0:T(8,128)(2,1)S(1)}, bf16[4,832,128]{2,1,0:T(8,128)(2,1)S(1)}, u32[]{:S(2)}, u32[]{:S(2)}) collective-permute-start(bf16[4,832,128]{2,1,0:T(8,128)(2,1)S(1)} %get-tuple-element.47), channel_id=1, source_target_pairs={{0,34},{1,33},{2,32},{3,35},{4,38},{5,37},{6,36},{7,39},{8,42},{9,... | collective-permute-start | bytes 2555912 | tf_op jit(solution)/shard_map/ppermute | solution.py:33
  35.4 13.7 %collective-permute-start.6 = (bf16[4,832,128]{2,1,0:T(8,128)(2,1)S(1)}, bf16[4,832,128]{2,1,0:T(8,128)(2,1)S(1)}, u32[]{:S(2)}, u32[]{:S(2)}) collective-permute-start(bf16[4,832,128]{2,1,0:T(8,128)(2,1)S(1)} %pass_on.4), channel_id=1, source_target_pairs={{0,32},{1,35},{2,34},{3,33},{4,36},{5,39},{6,38},{7,37},{8,40},{9,... | collective-permute-start | bytes 2555912 | tf_op jit(solution)/shard_map/ppermute | solution.py:33
  37.9 14.0 %collective-permute-start.12 = (bf16[4,576,128]{2,1,0:T(8,128)(2,1)S(1)}, bf16[4,576,128]{2,1,0:T(8,128)(2,1)S(1)}, u32[]{:S(2)}, u32[]{:S(2)}) collective-permute-start(bf16[4,576,128]{2,1,0:T(8,128)(2,1)S(1)} %pass_on.6), channel_id=1, source_target_pairs={{0,64},{1,193},{2,66},{3,195},{4,68},{5,197},{6,70},{7,199},{8,72}... | collective-permute-start | bytes 1769480 | tf_op jit(solution)/shard_map/ppermute | solution.py:33
  49.9 7.1 %collective-permute-start.8 = (bf16[832,128]{1,0:T(8,128)(2,1)S(1)}, bf16[832,128]{1,0:T(8,128)(2,1)S(1)}, u32[]{:S(2)}, u32[]{:S(2)}) collective-permute-start(bf16[832,128]{1,0:T(8,128)(2,1)S(1)} %get-tuple-element.53), channel_id=1, source_target_pairs={{0,64},{1,193},{2,66},{3,195},{4,68},{5,197},{6,70},{7,199},{8,72}... | collective-permute-start | bytes 638984 | tf_op jit(solution)/shard_map/ppermute | solution.py:33
  52.7 6.4 %collective-permute-start.13 = (bf16[576,128]{1,0:T(8,128)(2,1)S(1)}, bf16[576,128]{1,0:T(8,128)(2,1)S(1)}, u32[]{:S(2)}, u32[]{:S(2)}) collective-permute-start(bf16[576,128]{1,0:T(8,128)(2,1)S(1)} %get-tuple-element.62), channel_id=1, source_target_pairs={{0,32},{1,35},{2,34},{3,33},{4,36},{5,39},{6,38},{7,37},{8,40},{9,... | collective-permute-start | bytes 442376 | tf_op jit(solution)/shard_map/ppermute | solution.py:33
  53.7 5.5 %collective-permute-start.14 = (bf16[576,128]{1,0:T(8,128)(2,1)S(1)}, bf16[576,128]{1,0:T(8,128)(2,1)S(1)}, u32[]{:S(2)}, u32[]{:S(2)}) collective-permute-start(bf16[576,128]{1,0:T(8,128)(2,1)S(1)} %get-tuple-element.63), channel_id=1, source_target_pairs={{0,34},{1,33},{2,32},{3,35},{4,38},{5,37},{6,36},{7,39},{8,42},{9,... | collective-permute-start | bytes 442376 | tf_op jit(solution)/shard_map/ppermute | solution.py:33
  54.8 10.1 %collective-permute-start.7 = (bf16[832,128]{1,0:T(8,128)(2,1)S(1)}, bf16[832,128]{1,0:T(8,128)(2,1)S(1)}, u32[]{:S(2)}, u32[]{:S(2)}) collective-permute-start(bf16[832,128]{1,0:T(8,128)(2,1)S(1)} %get-tuple-element.51), channel_id=1, source_target_pairs={{0,192},{1,65},{2,194},{3,67},{4,196},{5,69},{6,198},{7,71},{8,200... | collective-permute-start | bytes 638984 | tf_op jit(solution)/shard_map/ppermute | solution.py:33
  57.1 7.9 %collective-permute-start.9 = (bf16[832,128]{1,0:T(8,128)(2,1)S(1)}, bf16[832,128]{1,0:T(8,128)(2,1)S(1)}, u32[]{:S(2)}, u32[]{:S(2)}) collective-permute-start(bf16[832,128]{1,0:T(8,128)(2,1)S(1)} %pass_on.5), channel_id=1, source_target_pairs={{0,64},{1,193},{2,66},{3,195},{4,68},{5,197},{6,70},{7,199},{8,72}... | collective-permute-start | bytes 638984 | tf_op jit(solution)/shard_map/ppermute | solution.py:33
  59.2 5.7 %collective-permute-start.15 = (bf16[576,128]{1,0:T(8,128)(2,1)S(1)}, bf16[576,128]{1,0:T(8,128)(2,1)S(1)}, u32[]{:S(2)}, u32[]{:S(2)}) collective-permute-start(bf16[576,128]{1,0:T(8,128)(2,1)S(1)} %pass_on.7), channel_id=1, source_target_pairs={{0,32},{1,35},{2,34},{3,33},{4,36},{5,39},{6,38},{7,37},{8,40},{9,... | collective-permute-start | bytes 442376 | tf_op jit(solution)/shard_map/ppermute | solution.py:33

commit v8 on v7

--- a/solution.py
+++ b/solution.py
@@ -48,7 +48,18 @@
     )(*operands)
 
 
-SHARE = 144
+SHARE = 96
+
+
+def turn_patches_body(pos, p, mine, send, t):
+    pt = p[...].T
+    for b in range(16):
+        for half in range(2):
+            at = (b * 2 + half) * 48
+            t[b, half] = pt[at : at + 48]
+    c = pos[3]
+    mine[...] = t[:, c]
+    send[...] = t[:, 1 - c]
 
 
 def gelu_pass_body(
@@ -68,11 +79,6 @@
     for copy in copies:
         copy.start()
 
-    pt = p[...].T
-    for b in range(16):
-        for half in range(2):
-            at = (b * 2 + half) * 48
-            t[b, half, 96:144] = pt[at : at + 48]
     acc = None
     for k in range(3):
         copies[k].wait()
@@ -149,7 +155,7 @@
 
 
 ROWS = 176
-SPLIT = 5
+SPLIT = 4
 CHUNK_X = 512 + SPLIT * 64
 CHUNK_Y = (8 - SPLIT) * 64 + 384
 
@@ -190,7 +196,7 @@
                     dst[yy, at : at + 32] = acc[z * 32 : z * 32 + 32, col : col + 128]
 
 
-def terms_y_body(pos, lm, lr, gm, gr, em, er, *outs):
+def terms_y_body(pos, lm, lr, pm, pr, gm, gr, em, er, *outs):
     for rel in range(4):
         to = chunk_of(pos[1], pos, rel)
         dst = outs[rel]
@@ -205,7 +211,7 @@
                     at = z * 64 + k * 32
                     dst[xx, at : at + 32] = acc[row : row + 32, col : col + 128]
         acc = dot2(
-            [ref[:, :, 96:144].reshape(768, 256) for ref in (lm, lr)],
+            [ref[...].reshape(768, 256) for ref in (pm, pr)],
             [columns(ref, [to * 128, 512 + to * 128], 128) for ref in (em, er)],
         )
         for z in range(8):
@@ -307,11 +313,22 @@
     pos = pos.astype(jnp.int32)
 
     gain = ln_gain.reshape(1, 1024)
+    patches_mine, patches_send = call(
+        turn_patches_body,
+        [((16, 48, 256), BF)] * 2,
+        [pltpu.VMEM((16, 2, 48, 256), BF)],
+        "turn_patches",
+        pos,
+        patches,
+        limit=12,
+        gflop=2,
+    )
+    patches_other = move(patches_send, "c", 0)
     cot_other = move(cotangent, "c", 0)
     preact_grad, normal, inverse, mine, send = gelu_pass(
         pos, gain, patches, cotangent, stem_weight, up_weight, down_weight
     )
-    send, cot_other = lax.optimization_barrier((send, cot_other))
+    send, cot_other, patches_other = lax.optimization_barrier((send, cot_other, patches_other))
     other = move(send, "c", 0)
     preact_other = move(preact_grad, "c", 0)
     (embed_grad,) = call(
@@ -339,7 +356,7 @@
     )
     embed_other, *part_x = lax.optimization_barrier((embed_other, *part_x))
     part_y = call(
-        terms_y_body, outs_y, [], "terms_y", pos, *left, *grads, embed_grad, embed_other, limit=16, gflop=2
+        terms_y_body, outs_y, [], "terms_y", pos, *left, patches_mine, patches_other, *grads, embed_grad, embed_other, limit=16, gflop=2
     )
     return tuple(finish(reduce_xy(pos, (part_x, part_y))))
 

time: 100 us -> 98.1 us (0.981)
  blocking collectives: 33.8 us -> 31.6 us
  waiting for transfers between devices: 27 us -> 29 us
  local copies, waits for them, and re-layouts: 2.87 us -> 1.15 us
  starting transfers between devices: 18.9 us -> 17.8 us
    all_to_all x1, blocking collectives: 21.3 us -> 18.5 us  [finish(): got = lax.all_to_all(packed, 'z', 0, 0, tiled=True)]
    ppermute x16 -> x17, waiting for transfers between devices: 27 us -> 29 us  [move(): return lax.ppermute(value, AXES, sorted(pairs))]
    unnamed x8 -> x10, local copies, waits for them, and re-layouts: 2.87 us -> 1.15 us
    ppermute x16 -> x17, starting transfers between devices: 18.9 us -> 17.8 us  [move(): return lax.ppermute(value, AXES, sorted(pairs))]
    pallas_call x13 -> x14, Pallas kernels: 16.5 us -> 17.1 us  [call(): pl.pallas_call(body, out_shape=[jax.ShapeDtypeStruct(s, d) for s, d in ou...]
  transfers between devices with their start and end apart: 16 -> 17, of which waited for: 9 -> 10; matrix products, arithmetic and copies ran while one was open for 0% -> 0% of each run, Pallas kernels for 15% -> 16%
where the time goes in v8:
time: 98.1 us; the launch traced here: 97.6 us
  blocking collectives  31.6 us (32%)
  waiting for transfers between devices  29 us (30%)
  starting transfers between devices  17.8 us (18%)
  Pallas kernels  17.1 us (17%)
  local copies, waits for them, and re-layouts  1.15 us (1%)
    ppermute x17, waiting for transfers between devices, move(): return lax.ppermute(value, AXES, sorted(pairs))  29 us
    all_to_all x1, blocking collectives, finish(): got = lax.all_to_all(packed, 'z', 0, 0, tiled=True)  18.5 us
    ppermute x17, starting transfers between devices, move(): return lax.ppermute(value, AXES, sorted(pairs))  17.8 us
    pallas_call x14, Pallas kernels, call(): pl.pallas_call(body, out_shape=[jax.ShapeDtypeStruct(s, d) for s, d in ou...  17.1 us
    all_to_all x1, blocking collectives, finish(): every = lax.all_to_all(copies, ('y', 'xl'), 0, 0, tiled=True)  13.1 us
  transfers between devices with their start and end apart: 17, of which 10 were waited for; matrix products, arithmetic and copies ran while one was open for 0% of the time, Pallas kernels for 16%

profile of v8, /device:TPU:4, one launch (start us, length us, event | category | flops | bytes accessed | tf_op | source)
XLA Modules:
  0.0 97.6 jit_solution(157702173193727953)
XLA Ops:
  0.8 1.1 %copy-done.3 = bf16[256,1536]{1,0:T(8,128)(2,1)S(1)} copy-done((bf16[256,1536]{1,0:T(8,128)(2,1)S(1)}, bf16[256,1536]{1,0:T(8,128)(2,1)}, u32[]{:S(2)}) %copy-start.3) | copy-done | bytes 786456
  2.0 0.8 turn_patches.1
  2.8 0.6 collective-permute-start.2
  3.4 7.1 %gelu_pass.1 = (bf16[256,2048]{1,0:T(8,128)(2,1)S(1)}, f32[256,1024]{1,0:T(8,128)S(1)}, f32[256,1]{1,0:T(8,128)S(1)}, bf16[16,96,256]{2,1,0:T(8,128)(2,1)S(1)}, bf16[16,96,256]{2,1,0:T(8,128)(2,1)S(1)}) custom-call(s32[4]{0:T(128)S(1)} %pad_add_fusion.pos, f32[1,1024]{1,0:T(1,128)S(1)} %bitcast.7, bf16[256,1536]{1,0:T(8,128)(2,1)S(1)} %copy-done.4, ...), custom_call_target="tpu_custom_call" | custom-call | flops 8000000000 | bytes 1048576 | tf_op jit(solution)/shard_map/gelu_pass/pallas_call | solution.py:37
  10.8 0.4 collective-permute-start.3
  11.1 1.6 %norm_back.1.em = bf16[256,1024]{1,0:T(8,128)(2,1)S(1)} custom-call(f32[1,1024]{1,0:T(1,128)S(1)} %bitcast.8, bf16[256,2048]{1,0:T(8,128)(2,1)S(1)} %get-tuple-element.38.preact_grad.gm, bf16[1024,2048]{1,0:T(8,128)(2,1)S(1)} %copy-done, bf16[256,1024]{1,0:T(8,128)(2,1)S(1)} %copy-done.1, f32[256,1024]{1,0:T(8,128)S(1)} %get-tuple-element.39.normal, ...), custom_call_target="tpu_custom_call" | custom-call | flops 2000000000 | bytes 1048576 | tf_op jit(solution)/shard_map/norm_back/pallas_call | solution.py:37
  13.3 1.1 %collective-permute-done.3 = bf16[16,96,256]{2,1,0:T(8,128)(2,1)S(1)} collective-permute-done((bf16[16,96,256]{2,1,0:T(8,128)(2,1)S(1)}, bf16[16,96,256]{2,1,0:T(8,128)(2,1)S(1)}, u32[]{:S(2)}, u32[]{:S(2)}) %collective-permute-start.3) | collective-permute-done | bytes 786464 | tf_op jit(solution)/shard_map/ppermute | solution.py:33
  14.4 2.4 %terms_x.1 = (bf16[4,768,128]{2,1,0:T(8,128)(2,1)S(1)}, bf16[4,768,128]{2,1,0:T(8,128)(2,1)S(1)}, bf16[4,768,128]{2,1,0:T(8,128)(2,1)S(1)}, bf16[4,768,128]{2,1,0:T(8,128)(2,1)S(1)}) custom-call(s32[4]{0:T(128)S(1)} %pad_add_fusion.pos, bf16[8,2,96,256]{3,2,1,0:T(8,128)(2,1)S(1)} %bitcast.11, bf16[8,2,96,256]{3,2,1,0:T(8,128)(2,1)S(1)} %bitcast.9, ...), custom_call_target="tpu_custom_call" | custom-call | flops 2000000000 | bytes 1048576 | tf_op jit(solution)/shard_map/terms_x/pallas_call | solution.py:37
  16.8 1.3 %collective-permute-start.6 = (bf16[4,768,128]{2,1,0:T(8,128)(2,1)S(1)}, bf16[4,768,128]{2,1,0:T(8,128)(2,1)S(1)}, u32[]{:S(2)}, u32[]{:S(2)}) collective-permute-start(bf16[4,768,128]{2,1,0:T(8,128)(2,1)S(1)} %get-tuple-element.53), channel_id=1, source_target_pairs={{0,32},{1,35},{2,34},{3,33},{4,36},{5,39},{6,38},{7,37},{8,40},{9,... | collective-permute-start | bytes 2359304 | tf_op jit(solution)/shard_map/ppermute | solution.py:33
  18.1 2.1 %terms_y.1 = (bf16[4,640,128]{2,1,0:T(8,128)(2,1)S(1)}, bf16[4,640,128]{2,1,0:T(8,128)(2,1)S(1)}, bf16[4,640,128]{2,1,0:T(8,128)(2,1)S(1)}, bf16[4,640,128]{2,1,0:T(8,128)(2,1)S(1)}) custom-call(s32[4]{0:T(128)S(1)} %pad_add_fusion.pos, bf16[8,2,96,256]{3,2,1,0:T(8,128)(2,1)S(1)} %bitcast.12, bf16[8,2,96,256]{3,2,1,0:T(8,128)(2,1)S(1)} %bitcast.10, ...), custom_call_target="tpu_custom_call" | custom-call | flops 2000000000 | bytes 1048576 | tf_op jit(solution)/shard_map/terms_y/pallas_call | solution.py:37
  20.2 1.8 %collective-permute-start.11 = (bf16[4,640,128]{2,1,0:T(8,128)(2,1)S(1)}, bf16[4,640,128]{2,1,0:T(8,128)(2,1)S(1)}, u32[]{:S(2)}, u32[]{:S(2)}) collective-permute-start(bf16[4,640,128]{2,1,0:T(8,128)(2,1)S(1)} %get-tuple-element.62), channel_id=1, source_target_pairs={{0,64},{1,193},{2,66},{3,195},{4,68},{5,197},{6,70},{7,199},{8,72}... | collective-permute-start | bytes 1966088 | tf_op jit(solution)/shard_map/ppermute | solution.py:33
  22.1 1.7 %collective-permute-start.12 = (bf16[4,640,128]{2,1,0:T(8,128)(2,1)S(1)}, bf16[4,640,128]{2,1,0:T(8,128)(2,1)S(1)}, u32[]{:S(2)}, u32[]{:S(2)}) collective-permute-start(bf16[4,640,128]{2,1,0:T(8,128)(2,1)S(1)} %get-tuple-element.63), channel_id=1, source_target_pairs={{0,192},{1,65},{2,194},{3,67},{4,196},{5,69},{6,198},{7,71},{8,200... | collective-permute-start | bytes 1966088 | tf_op jit(solution)/shard_map/ppermute | solution.py:33
  23.7 0.8 collective-permute-start.5
  24.6 8.1 %collective-permute-done.6.got = bf16[4,768,128]{2,1,0:T(8,128)(2,1)S(1)} collective-permute-done((bf16[4,768,128]{2,1,0:T(8,128)(2,1)S(1)}, bf16[4,768,128]{2,1,0:T(8,128)(2,1)S(1)}, u32[]{:S(2)}, u32[]{:S(2)}) %collective-permute-start.6) | collective-permute-done | bytes 786464 | tf_op jit(solution)/shard_map/ppermute | solution.py:33
  32.9 1.0 %collective-permute-start.7 = (bf16[4,768,128]{2,1,0:T(8,128)(2,1)S(1)}, bf16[4,768,128]{2,1,0:T(8,128)(2,1)S(1)}, u32[]{:S(2)}, u32[]{:S(2)}) collective-permute-start(bf16[4,768,128]{2,1,0:T(8,128)(2,1)S(1)} %pass_on.4), channel_id=1, source_target_pairs={{0,32},{1,35},{2,34},{3,33},{4,36},{5,39},{6,38},{7,37},{8,40},{9,... | collective-permute-start | bytes 2359304 | tf_op jit(solution)/shard_map/ppermute | solution.py:33
  33.9 4.5 %collective-permute-done.11.got = bf16[4,640,128]{2,1,0:T(8,128)(2,1)S(1)} collective-permute-done((bf16[4,640,128]{2,1,0:T(8,128)(2,1)S(1)}, bf16[4,640,128]{2,1,0:T(8,128)(2,1)S(1)}, u32[]{:S(2)}, u32[]{:S(2)}) %collective-permute-start.11) | collective-permute-done | bytes 655392 | tf_op jit(solution)/shard_map/ppermute | solution.py:33
  38.5 1.1 %collective-permute-start.13 = (bf16[4,640,128]{2,1,0:T(8,128)(2,1)S(1)}, bf16[4,640,128]{2,1,0:T(8,128)(2,1)S(1)}, u32[]{:S(2)}, u32[]{:S(2)}) collective-permute-start(bf16[4,640,128]{2,1,0:T(8,128)(2,1)S(1)} %pass_on.6), channel_id=1, source_target_pairs={{0,64},{1,193},{2,66},{3,195},{4,68},{5,197},{6,70},{7,199},{8,72}... | collective-permute-start | bytes 1966088 | tf_op jit(solution)/shard_map/ppermute | solution.py:33
  39.6 1.6 %collective-permute-done.5.near = bf16[4,768,128]{2,1,0:T(8,128)(2,1)S(1)} collective-permute-done((bf16[4,768,128]{2,1,0:T(8,128)(2,1)S(1)}, bf16[4,768,128]{2,1,0:T(8,128)(2,1)S(1)}, u32[]{:S(2)}, u32[]{:S(2)}) %collective-permute-start.5) | collective-permute-done | bytes 786464 | tf_op jit(solution)/shard_map/ppermute | solution.py:33
  41.2 4.5 %collective-permute-done.7.far = bf16[4,768,128]{2,1,0:T(8,128)(2,1)S(1)} collective-permute-done((bf16[4,768,128]{2,1,0:T(8,128)(2,1)S(1)}, bf16[4,768,128]{2,1,0:T(8,128)(2,1)S(1)}, u32[]{:S(2)}, u32[]{:S(2)}) %collective-permute-start.7) | collective-permute-done | bytes 786464 | tf_op jit(solution)/shard_map/ppermute | solution.py:33
  45.7 0.8 ring_turn_x.1
  46.6 2.1 %collective-permute-start.9 = (bf16[768,128]{1,0:T(8,128)(2,1)S(1)}, bf16[768,128]{1,0:T(8,128)(2,1)S(1)}, u32[]{:S(2)}, u32[]{:S(2)}) collective-permute-start(bf16[768,128]{1,0:T(8,128)(2,1)S(1)} %get-tuple-element.57), channel_id=1, source_target_pairs={{0,64},{1,193},{2,66},{3,195},{4,68},{5,197},{6,70},{7,199},{8,72}... | collective-permute-start | bytes 589832 | tf_op jit(solution)/shard_map/ppermute | solution.py:33
  48.7 1.7 %collective-permute-done.13.far = bf16[4,640,128]{2,1,0:T(8,128)(2,1)S(1)} collective-permute-done((bf16[4,640,128]{2,1,0:T(8,128)(2,1)S(1)}, bf16[4,640,128]{2,1,0:T(8,128)(2,1)S(1)}, u32[]{:S(2)}, u32[]{:S(2)}) %collective-permute-start.13) | collective-permute-done | bytes 655392 | tf_op jit(solution)/shard_map/ppermute | solution.py:33
  50.4 0.8 ring_turn_y.1
  51.2 3.0 %collective-permute-start.14 = (bf16[640,128]{1,0:T(8,128)(2,1)S(1)}, bf16[640,128]{1,0:T(8,128)(2,1)S(1)}, u32[]{:S(2)}, u32[]{:S(2)}) collective-permute-start(bf16[640,128]{1,0:T(8,128)(2,1)S(1)} %get-tuple-element.68), channel_id=1, source_target_pairs={{0,32},{1,35},{2,34},{3,33},{4,36},{5,39},{6,38},{7,37},{8,40},{9,... | collective-permute-start | bytes 491528 | tf_op jit(solution)/shard_map/ppermute | solution.py:33
  54.4 2.0 %collective-permute-start.10 = (bf16[768,128]{1,0:T(8,128)(2,1)S(1)}, bf16[768,128]{1,0:T(8,128)(2,1)S(1)}, u32[]{:S(2)}, u32[]{:S(2)}) collective-permute-start(bf16[768,128]{1,0:T(8,128)(2,1)S(1)} %pass_on.5), channel_id=1, source_target_pairs={{0,64},{1,193},{2,66},{3,195},{4,68},{5,197},{6,70},{7,199},{8,72}... | collective-permute-start | bytes 589832 | tf_op jit(solution)/shard_map/ppermute | solution.py:33
  56.3 0.7 collective-permute-done.14.got
  57.0 2.5 %collective-permute-done.15.refs_4_ = bf16[640,128]{1,0:T(8,128)(2,1)S(1)} collective-permute-done((bf16[640,128]{1,0:T(8,128)(2,1)S(1)}, bf16[640,128]{1,0:T(8,128)(2,1)S(1)}, u32[]{:S(2)}, u32[]{:S(2)}) %collective-permute-start.15) | collective-permute-done | bytes 163872 | tf_op jit(solution)/shard_map/ppermute | solution.py:33
  59.5 1.4 %collective-permute-start.16 = (bf16[640,128]{1,0:T(8,128)(2,1)S(1)}, bf16[640,128]{1,0:T(8,128)(2,1)S(1)}, u32[]{:S(2)}, u32[]{:S(2)}) collective-permute-start(bf16[640,128]{1,0:T(8,128)(2,1)S(1)} %pass_on.7), channel_id=1, source_target_pairs={{0,32},{1,35},{2,34},{3,33},{4,36},{5,39},{6,38},{7,37},{8,40},{9,... | collective-permute-start | bytes 491528 | tf_op jit(solution)/shard_map/ppermute | solution.py:33
  60.9 4.0 %collective-permute-done.16.refs_5_ = bf16[640,128]{1,0:T(8,128)(2,1)S(1)} collective-permute-done((bf16[640,128]{1,0:T(8,128)(2,1)S(1)}, bf16[640,128]{1,0:T(8,128)(2,1)S(1)}, u32[]{:S(2)}, u32[]{:S(2)}) %collective-permute-start.16) | collective-permute-done | bytes 163872 | tf_op jit(solution)/shard_map/ppermute | solution.py:33
  65.1 18.5 %all_to_all.10.got = bf16[8,176,128]{2,1,0:T(8,128)(2,1)S(1)} all-to-all(bf16[8,176,128]{2,1,0:T(8,128)(2,1)S(1)} %z_pack.1), channel_id=1, replica_groups=mesh['y'=4,'xl'=2,'z'=8,'xh'=2,'c'=2] {'z'}, dimensions={0} | all-to-all | bytes 720896 | tf_op jit(solution)/shard_map/all_to_all | solution.py:303
  83.6 13.1 %all_to_all.11.got = bf16[8,176,128]{2,1,0:T(8,128)(2,1)S(1)} all-to-all(bf16[8,176,128]{2,1,0:T(8,128)(2,1)S(1)} %z_sum.1), channel_id=1, replica_groups=mesh['y'=4,'xl'=2,'z'=8,'xh'=2,'c'=2] {'y','xl'}, dimensions={0} | all-to-all | bytes 720896 | tf_op jit(solution)/shard_map/all_to_all | solution.py:305
  96.7 0.9 unpack.1
  (29 shorter events, 1.8 us)
Async XLA Ops:
  0.6 2.8 %copy-start.1 = (bf16[256,1024]{1,0:T(8,128)(2,1)S(1)}, bf16[256,1024]{1,0:T(8,128)(2,1)}, u32[]{:S(2)}) copy-start(bf16[256,1024]{1,0:T(8,128)(2,1)} %cm.1) | copy-start | bytes 1572868
  0.6 2.8 %copy-start.2 = (f32[1024]{0:T(1024)S(1)}, f32[1024]{0:T(1024)}, u32[]{:S(2)}) copy-start(f32[1024]{0:T(1024)} %param.8) | copy-start | bytes 12292
  0.7 10.1 %collective-permute-start.1 = (bf16[256,1024]{1,0:T(8,128)(2,1)}, bf16[256,1024]{1,0:T(8,128)(2,1)S(1)}, u32[]{:S(2)}, u32[]{:S(2)}) collective-permute-start(bf16[256,1024]{1,0:T(8,128)(2,1)} %cm.1), channel_id=1, source_target_pairs={{0,1},{1,0},{2,3},{3,2},{4,5},{5,4},{6,7},{7,6},{8,9},{9,8},{10,11... | collective-permute-start | bytes 1572872 | tf_op jit(solution)/shard_map/ppermute | solution.py:33
  0.8 1.1 %copy-start.3 = (bf16[256,1536]{1,0:T(8,128)(2,1)S(1)}, bf16[256,1536]{1,0:T(8,128)(2,1)}, u32[]{:S(2)}) copy-start(bf16[256,1536]{1,0:T(8,128)(2,1)} %p.3) | copy-start | bytes 2359300
  2.0 1.4 %copy-start.4 = (bf16[256,1536]{1,0:T(8,128)(2,1)S(1)}, bf16[256,1536]{1,0:T(8,128)(2,1)}, u32[]{:S(2)}) copy-start(bf16[256,1536]{1,0:T(8,128)(2,1)} %p.3) | copy-start | bytes 2359300
  2.8 8.0 %collective-permute-start.2 = (bf16[16,48,256]{2,1,0:T(8,128)(2,1)S(1)}, bf16[16,48,256]{2,1,0:T(8,128)(2,1)S(1)}, u32[]{:S(2)}, u32[]{:S(2)}) collective-permute-start(bf16[16,48,256]{2,1,0:T(8,128)(2,1)S(1)} %get-tuple-element.43), channel_id=1, source_target_pairs={{0,1},{1,0},{2,3},{3,2},{4,5},{5,4},{6,7},{7,6},{8,9},{9,8},{10,11... | collective-permute-start | bytes 1179656 | tf_op jit(solution)/shard_map/ppermute | solution.py:33
  3.4 7.7 %copy-start = (bf16[1024,2048]{1,0:T(8,128)(2,1)S(1)}, bf16[1024,2048]{1,0:T(8,128)(2,1)}, u32[]{:S(2)}) copy-start(bf16[1024,2048]{1,0:T(8,128)(2,1)} %up.1) | copy-start | bytes 12582916
  10.5 2.7 %collective-permute-start.4 = (bf16[256,2048]{1,0:T(8,128)(2,1)S(1)}, bf16[256,2048]{1,0:T(8,128)(2,1)S(1)}, u32[]{:S(2)}, u32[]{:S(2)}) collective-permute-start(bf16[256,2048]{1,0:T(8,128)(2,1)S(1)} %get-tuple-element.38.preact_grad.gm), channel_id=1, source_target_pairs={{0,1},{1,0},{2,3},{3,2},{4,5},{5,4},{6,7},{7,6},{8,9},{9,8},{10,11... | collective-permute-start | bytes 3145736 | tf_op jit(solution)/shard_map/ppermute | solution.py:33
  10.8 3.6 %collective-permute-start.3 = (bf16[16,96,256]{2,1,0:T(8,128)(2,1)S(1)}, bf16[16,96,256]{2,1,0:T(8,128)(2,1)S(1)}, u32[]{:S(2)}, u32[]{:S(2)}) collective-permute-start(bf16[16,96,256]{2,1,0:T(8,128)(2,1)S(1)} %get-tuple-element.44), channel_id=1, source_target_pairs={{0,1},{1,0},{2,3},{3,2},{4,5},{5,4},{6,7},{7,6},{8,9},{9,8},{10,11... | collective-permute-start | bytes 2359304 | tf_op jit(solution)/shard_map/ppermute | solution.py:33
  12.7 4.1 %collective-permute-start = (bf16[256,1024]{1,0:T(8,128)(2,1)S(1)}, bf16[256,1024]{1,0:T(8,128)(2,1)S(1)}, u32[]{:S(2)}, u32[]{:S(2)}) collective-permute-start(bf16[256,1024]{1,0:T(8,128)(2,1)S(1)} %norm_back.1.em), channel_id=1, source_target_pairs={{0,1},{1,0},{2,3},{3,2},{4,5},{5,4},{6,7},{7,6},{8,9},{9,8},{10,11... | collective-permute-start | bytes 1572872 | tf_op jit(solution)/shard_map/ppermute | solution.py:33
  16.8 15.8 %collective-permute-start.6 = (bf16[4,768,128]{2,1,0:T(8,128)(2,1)S(1)}, bf16[4,768,128]{2,1,0:T(8,128)(2,1)S(1)}, u32[]{:S(2)}, u32[]{:S(2)}) collective-permute-start(bf16[4,768,128]{2,1,0:T(8,128)(2,1)S(1)} %get-tuple-element.53), channel_id=1, source_target_pairs={{0,32},{1,35},{2,34},{3,33},{4,36},{5,39},{6,38},{7,37},{8,40},{9,... | collective-permute-start | bytes 2359304 | tf_op jit(solution)/shard_map/ppermute | solution.py:33
  20.2 18.1 %collective-permute-start.11 = (bf16[4,640,128]{2,1,0:T(8,128)(2,1)S(1)}, bf16[4,640,128]{2,1,0:T(8,128)(2,1)S(1)}, u32[]{:S(2)}, u32[]{:S(2)}) collective-permute-start(bf16[4,640,128]{2,1,0:T(8,128)(2,1)S(1)} %get-tuple-element.62), channel_id=1, source_target_pairs={{0,64},{1,193},{2,66},{3,195},{4,68},{5,197},{6,70},{7,199},{8,72}... | collective-permute-start | bytes 1966088 | tf_op jit(solution)/shard_map/ppermute | solution.py:33
  22.1 16.3 %collective-permute-start.12 = (bf16[4,640,128]{2,1,0:T(8,128)(2,1)S(1)}, bf16[4,640,128]{2,1,0:T(8,128)(2,1)S(1)}, u32[]{:S(2)}, u32[]{:S(2)}) collective-permute-start(bf16[4,640,128]{2,1,0:T(8,128)(2,1)S(1)} %get-tuple-element.63), channel_id=1, source_target_pairs={{0,192},{1,65},{2,194},{3,67},{4,196},{5,69},{6,198},{7,71},{8,200... | collective-permute-start | bytes 1966088 | tf_op jit(solution)/shard_map/ppermute | solution.py:33
  23.7 17.5 %collective-permute-start.5 = (bf16[4,768,128]{2,1,0:T(8,128)(2,1)S(1)}, bf16[4,768,128]{2,1,0:T(8,128)(2,1)S(1)}, u32[]{:S(2)}, u32[]{:S(2)}) collective-permute-start(bf16[4,768,128]{2,1,0:T(8,128)(2,1)S(1)} %get-tuple-element.51), channel_id=1, source_target_pairs={{0,34},{1,33},{2,32},{3,35},{4,38},{5,37},{6,36},{7,39},{8,42},{9,... | collective-permute-start | bytes 2359304 | tf_op jit(solution)/shard_map/ppermute | solution.py:33
  32.9 12.9 %collective-permute-start.7 = (bf16[4,768,128]{2,1,0:T(8,128)(2,1)S(1)}, bf16[4,768,128]{2,1,0:T(8,128)(2,1)S(1)}, u32[]{:S(2)}, u32[]{:S(2)}) collective-permute-start(bf16[4,768,128]{2,1,0:T(8,128)(2,1)S(1)} %pass_on.4), channel_id=1, source_target_pairs={{0,32},{1,35},{2,34},{3,33},{4,36},{5,39},{6,38},{7,37},{8,40},{9,... | collective-permute-start | bytes 2359304 | tf_op jit(solution)/shard_map/ppermute | solution.py:33
  38.5 11.9 %collective-permute-start.13 = (bf16[4,640,128]{2,1,0:T(8,128)(2,1)S(1)}, bf16[4,640,128]{2,1,0:T(8,128)(2,1)S(1)}, u32[]{:S(2)}, u32[]{:S(2)}) collective-permute-start(bf16[4,640,128]{2,1,0:T(8,128)(2,1)S(1)} %pass_on.6), channel_id=1, source_target_pairs={{0,64},{1,193},{2,66},{3,195},{4,68},{5,197},{6,70},{7,199},{8,72}... | collective-permute-start | bytes 1966088 | tf_op jit(solution)/shard_map/ppermute | solution.py:33
  46.6 7.7 %collective-permute-start.9 = (bf16[768,128]{1,0:T(8,128)(2,1)S(1)}, bf16[768,128]{1,0:T(8,128)(2,1)S(1)}, u32[]{:S(2)}, u32[]{:S(2)}) collective-permute-start(bf16[768,128]{1,0:T(8,128)(2,1)S(1)} %get-tuple-element.57), channel_id=1, source_target_pairs={{0,64},{1,193},{2,66},{3,195},{4,68},{5,197},{6,70},{7,199},{8,72}... | collective-permute-start | bytes 589832 | tf_op jit(solution)/shard_map/ppermute | solution.py:33
  51.2 5.8 %collective-permute-start.14 = (bf16[640,128]{1,0:T(8,128)(2,1)S(1)}, bf16[640,128]{1,0:T(8,128)(2,1)S(1)}, u32[]{:S(2)}, u32[]{:S(2)}) collective-permute-start(bf16[640,128]{1,0:T(8,128)(2,1)S(1)} %get-tuple-element.68), channel_id=1, source_target_pairs={{0,32},{1,35},{2,34},{3,33},{4,36},{5,39},{6,38},{7,37},{8,40},{9,... | collective-permute-start | bytes 491528 | tf_op jit(solution)/shard_map/ppermute | solution.py:33
  54.2 5.3 %collective-permute-start.15 = (bf16[640,128]{1,0:T(8,128)(2,1)S(1)}, bf16[640,128]{1,0:T(8,128)(2,1)S(1)}, u32[]{:S(2)}, u32[]{:S(2)}) collective-permute-start(bf16[640,128]{1,0:T(8,128)(2,1)S(1)} %get-tuple-element.69), channel_id=1, source_target_pairs={{0,34},{1,33},{2,32},{3,35},{4,38},{5,37},{6,36},{7,39},{8,42},{9,... | collective-permute-start | bytes 491528 | tf_op jit(solution)/shard_map/ppermute | solution.py:33
  54.2 10.8 %collective-permute-start.8 = (bf16[768,128]{1,0:T(8,128)(2,1)S(1)}, bf16[768,128]{1,0:T(8,128)(2,1)S(1)}, u32[]{:S(2)}, u32[]{:S(2)}) collective-permute-start(bf16[768,128]{1,0:T(8,128)(2,1)S(1)} %get-tuple-element.55), channel_id=1, source_target_pairs={{0,192},{1,65},{2,194},{3,67},{4,196},{5,69},{6,198},{7,71},{8,200... | collective-permute-start | bytes 589832 | tf_op jit(solution)/shard_map/ppermute | solution.py:33
  54.4 10.6 %collective-permute-start.10 = (bf16[768,128]{1,0:T(8,128)(2,1)S(1)}, bf16[768,128]{1,0:T(8,128)(2,1)S(1)}, u32[]{:S(2)}, u32[]{:S(2)}) collective-permute-start(bf16[768,128]{1,0:T(8,128)(2,1)S(1)} %pass_on.5), channel_id=1, source_target_pairs={{0,64},{1,193},{2,66},{3,195},{4,68},{5,197},{6,70},{7,199},{8,72}... | collective-permute-start | bytes 589832 | tf_op jit(solution)/shard_map/ppermute | solution.py:33
  59.5 5.4 %collective-permute-start.16 = (bf16[640,128]{1,0:T(8,128)(2,1)S(1)}, bf16[640,128]{1,0:T(8,128)(2,1)S(1)}, u32[]{:S(2)}, u32[]{:S(2)}) collective-permute-start(bf16[640,128]{1,0:T(8,128)(2,1)S(1)} %pass_on.7), channel_id=1, source_target_pairs={{0,32},{1,35},{2,34},{3,33},{4,36},{5,39},{6,38},{7,37},{8,40},{9,... | collective-permute-start | bytes 491528 | tf_op jit(solution)/shard_map/ppermute | solution.py:33

commit v9 on v8

--- a/solution.py
+++ b/solution.py
@@ -63,14 +63,11 @@
 
 
 def gelu_pass_body(
-    pos, gain, p, g, stem_any, up_any, down_any,
+    pos, gain, p, g, w, up_any, down_any,
     preact_grad, normal, inverse, mine, send,
-    w, u, d, t, sem,
+    u, d, t, sem,
 ):
     plan = []
-    for k in range(3):
-        rows = pl.ds(k * 512, 512)
-        plan.append((stem_any.at[rows], w.at[rows]))
     for k in range(2):
         cols = pl.ds(k * 1024, 1024)
         plan.append((up_any.at[:, cols], u.at[:, cols]))
@@ -79,13 +76,7 @@
     for copy in copies:
         copy.start()
 
-    acc = None
-    for k in range(3):
-        copies[k].wait()
-        part = jnp.dot(
-            p[:, k * 512 : k * 512 + 512], w[k * 512 : k * 512 + 512], preferred_element_type=F32
-        )
-        acc = part if acc is None else acc + part
+    acc = jnp.dot(p[...], w[...], preferred_element_type=F32)
     embed = acc.astype(BF).astype(F32)
     center = jnp.mean(embed, axis=1, keepdims=True)
     shifted = embed - center
@@ -101,8 +92,8 @@
             t[b, half, 64:96] = nt[at * 32 : at * 32 + 32]
     for j in range(8):
         if j % 4 == 0:
-            copies[3 + j // 2].wait()
-            copies[4 + j // 2].wait()
+            copies[j // 2].wait()
+            copies[j // 2 + 1].wait()
         cols = slice(j * 256, j * 256 + 256)
         pre = jnp.dot(normed, u[:, cols], preferred_element_type=F32)
         grad = lax.dot_general(g[...], d[cols], OVER_COLUMNS, preferred_element_type=F32)
@@ -123,11 +114,10 @@
         gelu_pass_body,
         outs + [((16, SHARE, 256), BF)] * 2,
         [
-            pltpu.VMEM((1536, 1024), BF),
             pltpu.VMEM((1024, 2048), BF),
             pltpu.VMEM((2048, 1024), BF),
             pltpu.VMEM((16, 2, SHARE, 256), BF),
-            pltpu.SemaphoreType.DMA((7,)),
+            pltpu.SemaphoreType.DMA((4,)),
         ],
         "gelu_pass",
         pos,
@@ -137,8 +127,8 @@
         stem_weight,
         up_weight,
         down_weight,
-        limit=48,
-        specs=[SMEM] + [VMEM] * 3 + [pl.BlockSpec(memory_space=pl.ANY)] * 3,
+        limit=46,
+        specs=[SMEM] + [VMEM] * 4 + [pl.BlockSpec(memory_space=pl.ANY)] * 2,
         gflop=8,
     )
 

time: 98.1 us -> 98.4 us (level)
  no operation moved by 1% of the time
where the time goes in v9:
time: 98.4 us; the launch traced here: 98.2 us
  blocking collectives  32.1 us (33%)
  waiting for transfers between devices  28.1 us (29%)
  starting transfers between devices  18.6 us (19%)
  Pallas kernels  17.2 us (17%)
  local copies, waits for them, and re-layouts  1.31 us (1%)
    ppermute x17, waiting for transfers between devices, move(): return lax.ppermute(value, AXES, sorted(pairs))  28.1 us
    all_to_all x1, blocking collectives, finish(): got = lax.all_to_all(packed, 'z', 0, 0, tiled=True)  18.9 us
    ppermute x17, starting transfers between devices, move(): return lax.ppermute(value, AXES, sorted(pairs))  18.6 us
    pallas_call x14, Pallas kernels, call(): pl.pallas_call(body, out_shape=[jax.ShapeDtypeStruct(s, d) for s, d in ou...  17.2 us
    all_to_all x1, blocking collectives, finish(): every = lax.all_to_all(copies, ('y', 'xl'), 0, 0, tiled=True)  13.2 us
  transfers between devices with their start and end apart: 17, of which 10 were waited for; matrix products, arithmetic and copies ran while one was open for 0% of the time, Pallas kernels for 16%

profile of v9, /device:TPU:4, one launch (start us, length us, event | category | flops | bytes accessed | tf_op | source)
XLA Modules:
  0.0 98.2 jit_solution(4680713948259949949)
XLA Ops:
  0.8 1.3 %copy-done.4 = bf16[256,1536]{1,0:T(8,128)(2,1)S(1)} copy-done((bf16[256,1536]{1,0:T(8,128)(2,1)S(1)}, bf16[256,1536]{1,0:T(8,128)(2,1)}, u32[]{:S(2)}) %copy-start.4) | copy-done | bytes 786456
  2.1 0.8 turn_patches.1
  3.0 0.6 collective-permute-start.2
  3.6 7.2 %gelu_pass.1 = (bf16[256,2048]{1,0:T(8,128)(2,1)S(1)}, f32[256,1024]{1,0:T(8,128)S(1)}, f32[256,1]{1,0:T(8,128)S(1)}, bf16[16,96,256]{2,1,0:T(8,128)(2,1)S(1)}, bf16[16,96,256]{2,1,0:T(8,128)(2,1)S(1)}) custom-call(s32[4]{0:T(128)S(1)} %pad_add_fusion.pos, f32[1,1024]{1,0:T(1,128)S(1)} %bitcast.7, bf16[256,1536]{1,0:T(8,128)(2,1)S(1)} %copy-done.5, ...), custom_call_target="tpu_custom_call" | custom-call | flops 8000000000 | bytes 1048576 | tf_op jit(solution)/shard_map/gelu_pass/pallas_call | solution.py:37
  11.4 1.6 %norm_back.1.em = bf16[256,1024]{1,0:T(8,128)(2,1)S(1)} custom-call(f32[1,1024]{1,0:T(1,128)S(1)} %bitcast.8, bf16[256,2048]{1,0:T(8,128)(2,1)S(1)} %get-tuple-element.38.preact_grad.gm, bf16[1024,2048]{1,0:T(8,128)(2,1)S(1)} %copy-done, bf16[256,1024]{1,0:T(8,128)(2,1)S(1)} %copy-done.1, f32[256,1024]{1,0:T(8,128)S(1)} %get-tuple-element.39.normal, ...), custom_call_target="tpu_custom_call" | custom-call | flops 2000000000 | bytes 1048576 | tf_op jit(solution)/shard_map/norm_back/pallas_call | solution.py:37
  13.5 1.1 %collective-permute-done.3 = bf16[16,96,256]{2,1,0:T(8,128)(2,1)S(1)} collective-permute-done((bf16[16,96,256]{2,1,0:T(8,128)(2,1)S(1)}, bf16[16,96,256]{2,1,0:T(8,128)(2,1)S(1)}, u32[]{:S(2)}, u32[]{:S(2)}) %collective-permute-start.3) | collective-permute-done | bytes 786464 | tf_op jit(solution)/shard_map/ppermute | solution.py:33
  14.7 2.4 %terms_x.1 = (bf16[4,768,128]{2,1,0:T(8,128)(2,1)S(1)}, bf16[4,768,128]{2,1,0:T(8,128)(2,1)S(1)}, bf16[4,768,128]{2,1,0:T(8,128)(2,1)S(1)}, bf16[4,768,128]{2,1,0:T(8,128)(2,1)S(1)}) custom-call(s32[4]{0:T(128)S(1)} %pad_add_fusion.pos, bf16[8,2,96,256]{3,2,1,0:T(8,128)(2,1)S(1)} %bitcast.11, bf16[8,2,96,256]{3,2,1,0:T(8,128)(2,1)S(1)} %bitcast.9, ...), custom_call_target="tpu_custom_call" | custom-call | flops 2000000000 | bytes 1048576 | tf_op jit(solution)/shard_map/terms_x/pallas_call | solution.py:37
  17.1 1.3 %collective-permute-start.6 = (bf16[4,768,128]{2,1,0:T(8,128)(2,1)S(1)}, bf16[4,768,128]{2,1,0:T(8,128)(2,1)S(1)}, u32[]{:S(2)}, u32[]{:S(2)}) collective-permute-start(bf16[4,768,128]{2,1,0:T(8,128)(2,1)S(1)} %get-tuple-element.53), channel_id=1, source_target_pairs={{0,32},{1,35},{2,34},{3,33},{4,36},{5,39},{6,38},{7,37},{8,40},{9,... | collective-permute-start | bytes 2359304 | tf_op jit(solution)/shard_map/ppermute | solution.py:33
  18.3 2.1 %terms_y.1 = (bf16[4,640,128]{2,1,0:T(8,128)(2,1)S(1)}, bf16[4,640,128]{2,1,0:T(8,128)(2,1)S(1)}, bf16[4,640,128]{2,1,0:T(8,128)(2,1)S(1)}, bf16[4,640,128]{2,1,0:T(8,128)(2,1)S(1)}) custom-call(s32[4]{0:T(128)S(1)} %pad_add_fusion.pos, bf16[8,2,96,256]{3,2,1,0:T(8,128)(2,1)S(1)} %bitcast.12, bf16[8,2,96,256]{3,2,1,0:T(8,128)(2,1)S(1)} %bitcast.10, ...), custom_call_target="tpu_custom_call" | custom-call | flops 2000000000 | bytes 1048576 | tf_op jit(solution)/shard_map/terms_y/pallas_call | solution.py:37
  20.5 1.9 %collective-permute-start.11 = (bf16[4,640,128]{2,1,0:T(8,128)(2,1)S(1)}, bf16[4,640,128]{2,1,0:T(8,128)(2,1)S(1)}, u32[]{:S(2)}, u32[]{:S(2)}) collective-permute-start(bf16[4,640,128]{2,1,0:T(8,128)(2,1)S(1)} %get-tuple-element.62), channel_id=1, source_target_pairs={{0,64},{1,193},{2,66},{3,195},{4,68},{5,197},{6,70},{7,199},{8,72}... | collective-permute-start | bytes 1966088 | tf_op jit(solution)/shard_map/ppermute | solution.py:33
  22.3 1.6 %collective-permute-start.12 = (bf16[4,640,128]{2,1,0:T(8,128)(2,1)S(1)}, bf16[4,640,128]{2,1,0:T(8,128)(2,1)S(1)}, u32[]{:S(2)}, u32[]{:S(2)}) collective-permute-start(bf16[4,640,128]{2,1,0:T(8,128)(2,1)S(1)} %get-tuple-element.63), channel_id=1, source_target_pairs={{0,192},{1,65},{2,194},{3,67},{4,196},{5,69},{6,198},{7,71},{8,200... | collective-permute-start | bytes 1966088 | tf_op jit(solution)/shard_map/ppermute | solution.py:33
  24.0 0.8 collective-permute-start.5
  24.8 7.9 %collective-permute-done.6.got = bf16[4,768,128]{2,1,0:T(8,128)(2,1)S(1)} collective-permute-done((bf16[4,768,128]{2,1,0:T(8,128)(2,1)S(1)}, bf16[4,768,128]{2,1,0:T(8,128)(2,1)S(1)}, u32[]{:S(2)}, u32[]{:S(2)}) %collective-permute-start.6) | collective-permute-done | bytes 786464 | tf_op jit(solution)/shard_map/ppermute | solution.py:33
  32.9 1.0 collective-permute-start.7
  33.9 4.5 %collective-permute-done.11.got = bf16[4,640,128]{2,1,0:T(8,128)(2,1)S(1)} collective-permute-done((bf16[4,640,128]{2,1,0:T(8,128)(2,1)S(1)}, bf16[4,640,128]{2,1,0:T(8,128)(2,1)S(1)}, u32[]{:S(2)}, u32[]{:S(2)}) %collective-permute-start.11) | collective-permute-done | bytes 655392 | tf_op jit(solution)/shard_map/ppermute | solution.py:33
  38.5 1.6 %collective-permute-start.13 = (bf16[4,640,128]{2,1,0:T(8,128)(2,1)S(1)}, bf16[4,640,128]{2,1,0:T(8,128)(2,1)S(1)}, u32[]{:S(2)}, u32[]{:S(2)}) collective-permute-start(bf16[4,640,128]{2,1,0:T(8,128)(2,1)S(1)} %pass_on.6), channel_id=1, source_target_pairs={{0,64},{1,193},{2,66},{3,195},{4,68},{5,197},{6,70},{7,199},{8,72}... | collective-permute-start | bytes 1966088 | tf_op jit(solution)/shard_map/ppermute | solution.py:33
  40.0 1.6 %collective-permute-done.5.near = bf16[4,768,128]{2,1,0:T(8,128)(2,1)S(1)} collective-permute-done((bf16[4,768,128]{2,1,0:T(8,128)(2,1)S(1)}, bf16[4,768,128]{2,1,0:T(8,128)(2,1)S(1)}, u32[]{:S(2)}, u32[]{:S(2)}) %collective-permute-start.5) | collective-permute-done | bytes 786464 | tf_op jit(solution)/shard_map/ppermute | solution.py:33
  41.6 4.4 %collective-permute-done.7.far = bf16[4,768,128]{2,1,0:T(8,128)(2,1)S(1)} collective-permute-done((bf16[4,768,128]{2,1,0:T(8,128)(2,1)S(1)}, bf16[4,768,128]{2,1,0:T(8,128)(2,1)S(1)}, u32[]{:S(2)}, u32[]{:S(2)}) %collective-permute-start.7) | collective-permute-done | bytes 786464 | tf_op jit(solution)/shard_map/ppermute | solution.py:33
  46.0 0.8 ring_turn_x.1
  46.8 1.9 %collective-permute-start.9 = (bf16[768,128]{1,0:T(8,128)(2,1)S(1)}, bf16[768,128]{1,0:T(8,128)(2,1)S(1)}, u32[]{:S(2)}, u32[]{:S(2)}) collective-permute-start(bf16[768,128]{1,0:T(8,128)(2,1)S(1)} %get-tuple-element.57), channel_id=1, source_target_pairs={{0,64},{1,193},{2,66},{3,195},{4,68},{5,197},{6,70},{7,199},{8,72}... | collective-permute-start | bytes 589832 | tf_op jit(solution)/shard_map/ppermute | solution.py:33
  48.8 1.6 %collective-permute-done.13.far = bf16[4,640,128]{2,1,0:T(8,128)(2,1)S(1)} collective-permute-done((bf16[4,640,128]{2,1,0:T(8,128)(2,1)S(1)}, bf16[4,640,128]{2,1,0:T(8,128)(2,1)S(1)}, u32[]{:S(2)}, u32[]{:S(2)}) %collective-permute-start.13) | collective-permute-done | bytes 655392 | tf_op jit(solution)/shard_map/ppermute | solution.py:33
  50.4 0.8 ring_turn_y.1
  51.1 3.1 %collective-permute-start.14 = (bf16[640,128]{1,0:T(8,128)(2,1)S(1)}, bf16[640,128]{1,0:T(8,128)(2,1)S(1)}, u32[]{:S(2)}, u32[]{:S(2)}) collective-permute-start(bf16[640,128]{1,0:T(8,128)(2,1)S(1)} %get-tuple-element.68), channel_id=1, source_target_pairs={{0,32},{1,35},{2,34},{3,33},{4,36},{5,39},{6,38},{7,37},{8,40},{9,... | collective-permute-start | bytes 491528 | tf_op jit(solution)/shard_map/ppermute | solution.py:33
  54.3 0.5 collective-permute-start.8
  54.8 1.6 %collective-permute-start.10 = (bf16[768,128]{1,0:T(8,128)(2,1)S(1)}, bf16[768,128]{1,0:T(8,128)(2,1)S(1)}, u32[]{:S(2)}, u32[]{:S(2)}) collective-permute-start(bf16[768,128]{1,0:T(8,128)(2,1)S(1)} %pass_on.5), channel_id=1, source_target_pairs={{0,64},{1,193},{2,66},{3,195},{4,68},{5,197},{6,70},{7,199},{8,72}... | collective-permute-start | bytes 589832 | tf_op jit(solution)/shard_map/ppermute | solution.py:33
  56.4 0.7 collective-permute-done.14.got
  57.1 2.5 %collective-permute-done.15.refs_4_ = bf16[640,128]{1,0:T(8,128)(2,1)S(1)} collective-permute-done((bf16[640,128]{1,0:T(8,128)(2,1)S(1)}, bf16[640,128]{1,0:T(8,128)(2,1)S(1)}, u32[]{:S(2)}, u32[]{:S(2)}) %collective-permute-start.15) | collective-permute-done | bytes 163872 | tf_op jit(solution)/shard_map/ppermute | solution.py:33
  59.6 1.6 %collective-permute-start.16 = (bf16[640,128]{1,0:T(8,128)(2,1)S(1)}, bf16[640,128]{1,0:T(8,128)(2,1)S(1)}, u32[]{:S(2)}, u32[]{:S(2)}) collective-permute-start(bf16[640,128]{1,0:T(8,128)(2,1)S(1)} %pass_on.7), channel_id=1, source_target_pairs={{0,32},{1,35},{2,34},{3,33},{4,36},{5,39},{6,38},{7,37},{8,40},{9,... | collective-permute-start | bytes 491528 | tf_op jit(solution)/shard_map/ppermute | solution.py:33
  61.3 3.8 %collective-permute-done.16.refs_5_ = bf16[640,128]{1,0:T(8,128)(2,1)S(1)} collective-permute-done((bf16[640,128]{1,0:T(8,128)(2,1)S(1)}, bf16[640,128]{1,0:T(8,128)(2,1)S(1)}, u32[]{:S(2)}, u32[]{:S(2)}) %collective-permute-start.16) | collective-permute-done | bytes 163872 | tf_op jit(solution)/shard_map/ppermute | solution.py:33
  65.2 18.9 %all_to_all.10.got = bf16[8,176,128]{2,1,0:T(8,128)(2,1)S(1)} all-to-all(bf16[8,176,128]{2,1,0:T(8,128)(2,1)S(1)} %z_pack.1), channel_id=1, replica_groups=mesh['y'=4,'xl'=2,'z'=8,'xh'=2,'c'=2] {'z'}, dimensions={0} | all-to-all | bytes 720896 | tf_op jit(solution)/shard_map/all_to_all | solution.py:293
  84.1 13.2 %all_to_all.11.got = bf16[8,176,128]{2,1,0:T(8,128)(2,1)S(1)} all-to-all(bf16[8,176,128]{2,1,0:T(8,128)(2,1)S(1)} %z_sum.1), channel_id=1, replica_groups=mesh['y'=4,'xl'=2,'z'=8,'xh'=2,'c'=2] {'y','xl'}, dimensions={0} | all-to-all | bytes 720896 | tf_op jit(solution)/shard_map/all_to_all | solution.py:295
  97.3 0.9 unpack.1
  (31 shorter events, 2.0 us)
Async XLA Ops:
  0.6 2.9 %copy-start.1 = (bf16[256,1024]{1,0:T(8,128)(2,1)S(1)}, bf16[256,1024]{1,0:T(8,128)(2,1)}, u32[]{:S(2)}) copy-start(bf16[256,1024]{1,0:T(8,128)(2,1)} %cm.1) | copy-start | bytes 1572868
  0.6 2.9 %copy-start.2 = (f32[1024]{0:T(1024)S(1)}, f32[1024]{0:T(1024)}, u32[]{:S(2)}) copy-start(f32[1024]{0:T(1024)} %param.8) | copy-start | bytes 12292
  0.7 10.6 %collective-permute-start.1 = (bf16[256,1024]{1,0:T(8,128)(2,1)}, bf16[256,1024]{1,0:T(8,128)(2,1)S(1)}, u32[]{:S(2)}, u32[]{:S(2)}) collective-permute-start(bf16[256,1024]{1,0:T(8,128)(2,1)} %cm.1), channel_id=1, source_target_pairs={{0,1},{1,0},{2,3},{3,2},{4,5},{5,4},{6,7},{7,6},{8,9},{9,8},{10,11... | collective-permute-start | bytes 1572872 | tf_op jit(solution)/shard_map/ppermute | solution.py:33
  0.8 2.8 %copy-start.3 = (bf16[1536,1024]{1,0:T(8,128)(2,1)S(1)}, bf16[1536,1024]{1,0:T(8,128)(2,1)}, u32[]{:S(2)}) copy-start(bf16[1536,1024]{1,0:T(8,128)(2,1)} %w.1) | copy-start | bytes 9437188
  0.8 1.3 %copy-start.4 = (bf16[256,1536]{1,0:T(8,128)(2,1)S(1)}, bf16[256,1536]{1,0:T(8,128)(2,1)}, u32[]{:S(2)}) copy-start(bf16[256,1536]{1,0:T(8,128)(2,1)} %p.3) | copy-start | bytes 2359300
  2.1 1.4 %copy-start.5 = (bf16[256,1536]{1,0:T(8,128)(2,1)S(1)}, bf16[256,1536]{1,0:T(8,128)(2,1)}, u32[]{:S(2)}) copy-start(bf16[256,1536]{1,0:T(8,128)(2,1)} %p.3) | copy-start | bytes 2359300
  3.0 8.2 %collective-permute-start.2 = (bf16[16,48,256]{2,1,0:T(8,128)(2,1)S(1)}, bf16[16,48,256]{2,1,0:T(8,128)(2,1)S(1)}, u32[]{:S(2)}, u32[]{:S(2)}) collective-permute-start(bf16[16,48,256]{2,1,0:T(8,128)(2,1)S(1)} %get-tuple-element.43), channel_id=1, source_target_pairs={{0,1},{1,0},{2,3},{3,2},{4,5},{5,4},{6,7},{7,6},{8,9},{9,8},{10,11... | collective-permute-start | bytes 1179656 | tf_op jit(solution)/shard_map/ppermute | solution.py:33
  3.6 7.8 %copy-start = (bf16[1024,2048]{1,0:T(8,128)(2,1)S(1)}, bf16[1024,2048]{1,0:T(8,128)(2,1)}, u32[]{:S(2)}) copy-start(bf16[1024,2048]{1,0:T(8,128)(2,1)} %up.1) | copy-start | bytes 12582916
  10.8 2.7 %collective-permute-start.4 = (bf16[256,2048]{1,0:T(8,128)(2,1)S(1)}, bf16[256,2048]{1,0:T(8,128)(2,1)S(1)}, u32[]{:S(2)}, u32[]{:S(2)}) collective-permute-start(bf16[256,2048]{1,0:T(8,128)(2,1)S(1)} %get-tuple-element.38.preact_grad.gm), channel_id=1, source_target_pairs={{0,1},{1,0},{2,3},{3,2},{4,5},{5,4},{6,7},{7,6},{8,9},{9,8},{10,11... | collective-permute-start | bytes 3145736 | tf_op jit(solution)/shard_map/ppermute | solution.py:33
  11.2 3.4 %collective-permute-start.3 = (bf16[16,96,256]{2,1,0:T(8,128)(2,1)S(1)}, bf16[16,96,256]{2,1,0:T(8,128)(2,1)S(1)}, u32[]{:S(2)}, u32[]{:S(2)}) collective-permute-start(bf16[16,96,256]{2,1,0:T(8,128)(2,1)S(1)} %get-tuple-element.44), channel_id=1, source_target_pairs={{0,1},{1,0},{2,3},{3,2},{4,5},{5,4},{6,7},{7,6},{8,9},{9,8},{10,11... | collective-permute-start | bytes 2359304 | tf_op jit(solution)/shard_map/ppermute | solution.py:33
  13.0 4.1 %collective-permute-start = (bf16[256,1024]{1,0:T(8,128)(2,1)S(1)}, bf16[256,1024]{1,0:T(8,128)(2,1)S(1)}, u32[]{:S(2)}, u32[]{:S(2)}) collective-permute-start(bf16[256,1024]{1,0:T(8,128)(2,1)S(1)} %norm_back.1.em), channel_id=1, source_target_pairs={{0,1},{1,0},{2,3},{3,2},{4,5},{5,4},{6,7},{7,6},{8,9},{9,8},{10,11... | collective-permute-start | bytes 1572872 | tf_op jit(solution)/shard_map/ppermute | solution.py:33
  17.1 15.6 %collective-permute-start.6 = (bf16[4,768,128]{2,1,0:T(8,128)(2,1)S(1)}, bf16[4,768,128]{2,1,0:T(8,128)(2,1)S(1)}, u32[]{:S(2)}, u32[]{:S(2)}) collective-permute-start(bf16[4,768,128]{2,1,0:T(8,128)(2,1)S(1)} %get-tuple-element.53), channel_id=1, source_target_pairs={{0,32},{1,35},{2,34},{3,33},{4,36},{5,39},{6,38},{7,37},{8,40},{9,... | collective-permute-start | bytes 2359304 | tf_op jit(solution)/shard_map/ppermute | solution.py:33
  20.5 17.9 %collective-permute-start.11 = (bf16[4,640,128]{2,1,0:T(8,128)(2,1)S(1)}, bf16[4,640,128]{2,1,0:T(8,128)(2,1)S(1)}, u32[]{:S(2)}, u32[]{:S(2)}) collective-permute-start(bf16[4,640,128]{2,1,0:T(8,128)(2,1)S(1)} %get-tuple-element.62), channel_id=1, source_target_pairs={{0,64},{1,193},{2,66},{3,195},{4,68},{5,197},{6,70},{7,199},{8,72}... | collective-permute-start | bytes 1966088 | tf_op jit(solution)/shard_map/ppermute | solution.py:33
  22.3 16.0 %collective-permute-start.12 = (bf16[4,640,128]{2,1,0:T(8,128)(2,1)S(1)}, bf16[4,640,128]{2,1,0:T(8,128)(2,1)S(1)}, u32[]{:S(2)}, u32[]{:S(2)}) collective-permute-start(bf16[4,640,128]{2,1,0:T(8,128)(2,1)S(1)} %get-tuple-element.63), channel_id=1, source_target_pairs={{0,192},{1,65},{2,194},{3,67},{4,196},{5,69},{6,198},{7,71},{8,200... | collective-permute-start | bytes 1966088 | tf_op jit(solution)/shard_map/ppermute | solution.py:33
  24.0 17.6 %collective-permute-start.5 = (bf16[4,768,128]{2,1,0:T(8,128)(2,1)S(1)}, bf16[4,768,128]{2,1,0:T(8,128)(2,1)S(1)}, u32[]{:S(2)}, u32[]{:S(2)}) collective-permute-start(bf16[4,768,128]{2,1,0:T(8,128)(2,1)S(1)} %get-tuple-element.51), channel_id=1, source_target_pairs={{0,34},{1,33},{2,32},{3,35},{4,38},{5,37},{6,36},{7,39},{8,42},{9,... | collective-permute-start | bytes 2359304 | tf_op jit(solution)/shard_map/ppermute | solution.py:33
  32.9 13.1 %collective-permute-start.7 = (bf16[4,768,128]{2,1,0:T(8,128)(2,1)S(1)}, bf16[4,768,128]{2,1,0:T(8,128)(2,1)S(1)}, u32[]{:S(2)}, u32[]{:S(2)}) collective-permute-start(bf16[4,768,128]{2,1,0:T(8,128)(2,1)S(1)} %pass_on.4), channel_id=1, source_target_pairs={{0,32},{1,35},{2,34},{3,33},{4,36},{5,39},{6,38},{7,37},{8,40},{9,... | collective-permute-start | bytes 2359304 | tf_op jit(solution)/shard_map/ppermute | solution.py:33
  38.5 11.9 %collective-permute-start.13 = (bf16[4,640,128]{2,1,0:T(8,128)(2,1)S(1)}, bf16[4,640,128]{2,1,0:T(8,128)(2,1)S(1)}, u32[]{:S(2)}, u32[]{:S(2)}) collective-permute-start(bf16[4,640,128]{2,1,0:T(8,128)(2,1)S(1)} %pass_on.6), channel_id=1, source_target_pairs={{0,64},{1,193},{2,66},{3,195},{4,68},{5,197},{6,70},{7,199},{8,72}... | collective-permute-start | bytes 1966088 | tf_op jit(solution)/shard_map/ppermute | solution.py:33
  46.8 7.9 %collective-permute-start.9 = (bf16[768,128]{1,0:T(8,128)(2,1)S(1)}, bf16[768,128]{1,0:T(8,128)(2,1)S(1)}, u32[]{:S(2)}, u32[]{:S(2)}) collective-permute-start(bf16[768,128]{1,0:T(8,128)(2,1)S(1)} %get-tuple-element.57), channel_id=1, source_target_pairs={{0,64},{1,193},{2,66},{3,195},{4,68},{5,197},{6,70},{7,199},{8,72}... | collective-permute-start | bytes 589832 | tf_op jit(solution)/shard_map/ppermute | solution.py:33
  51.1 6.0 %collective-permute-start.14 = (bf16[640,128]{1,0:T(8,128)(2,1)S(1)}, bf16[640,128]{1,0:T(8,128)(2,1)S(1)}, u32[]{:S(2)}, u32[]{:S(2)}) collective-permute-start(bf16[640,128]{1,0:T(8,128)(2,1)S(1)} %get-tuple-element.68), channel_id=1, source_target_pairs={{0,32},{1,35},{2,34},{3,33},{4,36},{5,39},{6,38},{7,37},{8,40},{9,... | collective-permute-start | bytes 491528 | tf_op jit(solution)/shard_map/ppermute | solution.py:33
  54.3 5.3 %collective-permute-start.15 = (bf16[640,128]{1,0:T(8,128)(2,1)S(1)}, bf16[640,128]{1,0:T(8,128)(2,1)S(1)}, u32[]{:S(2)}, u32[]{:S(2)}) collective-permute-start(bf16[640,128]{1,0:T(8,128)(2,1)S(1)} %get-tuple-element.69), channel_id=1, source_target_pairs={{0,34},{1,33},{2,32},{3,35},{4,38},{5,37},{6,36},{7,39},{8,42},{9,... | collective-permute-start | bytes 491528 | tf_op jit(solution)/shard_map/ppermute | solution.py:33
  54.3 10.8 %collective-permute-start.8 = (bf16[768,128]{1,0:T(8,128)(2,1)S(1)}, bf16[768,128]{1,0:T(8,128)(2,1)S(1)}, u32[]{:S(2)}, u32[]{:S(2)}) collective-permute-start(bf16[768,128]{1,0:T(8,128)(2,1)S(1)} %get-tuple-element.55), channel_id=1, source_target_pairs={{0,192},{1,65},{2,194},{3,67},{4,196},{5,69},{6,198},{7,71},{8,200... | collective-permute-start | bytes 589832 | tf_op jit(solution)/shard_map/ppermute | solution.py:33
  54.8 10.2 %collective-permute-start.10 = (bf16[768,128]{1,0:T(8,128)(2,1)S(1)}, bf16[768,128]{1,0:T(8,128)(2,1)S(1)}, u32[]{:S(2)}, u32[]{:S(2)}) collective-permute-start(bf16[768,128]{1,0:T(8,128)(2,1)S(1)} %pass_on.5), channel_id=1, source_target_pairs={{0,64},{1,193},{2,66},{3,195},{4,68},{5,197},{6,70},{7,199},{8,72}... | collective-permute-start | bytes 589832 | tf_op jit(solution)/shard_map/ppermute | solution.py:33
  59.6 5.4 %collective-permute-start.16 = (bf16[640,128]{1,0:T(8,128)(2,1)S(1)}, bf16[640,128]{1,0:T(8,128)(2,1)S(1)}, u32[]{:S(2)}, u32[]{:S(2)}) collective-permute-start(bf16[640,128]{1,0:T(8,128)(2,1)S(1)} %pass_on.7), channel_id=1, source_target_pairs={{0,32},{1,35},{2,34},{3,33},{4,36},{5,39},{6,38},{7,37},{8,40},{9,... | collective-permute-start | bytes 491528 | tf_op jit(solution)/shard_map/ppermute | solution.py:33

commit v10 on v8

--- a/solution.py
+++ b/solution.py
@@ -156,8 +156,13 @@
 
 ROWS = 176
 SPLIT = 4
-CHUNK_X = 512 + SPLIT * 64
-CHUNK_Y = (8 - SPLIT) * 64 + 384
+CHUNK_X = 512 + SPLIT * 64 + 32
+CHUNK_Y = (8 - SPLIT) * 64 - 32 + 384
+
+
+def up_rows(z, k):
+    at = z * 64 + k * 32
+    return ("x", 512 + at) if at < SPLIT * 64 + 32 else ("y", at - SPLIT * 64 - 32)
 
 
 def chunk_of(me, pos, rel):
@@ -186,13 +191,14 @@
         for yy in range(4):
             dst[yy, 0:512] = acc[:, yy * 128 : yy * 128 + 128]
         acc = dot2(
-            [ref[0:SPLIT, xh, 64:96].reshape(SPLIT * 32, 256) for ref in (lm, lr)],
+            [ref[0 : SPLIT + 1, xh, 64:96].reshape(SPLIT * 32 + 32, 256) for ref in (lm, lr)],
             [columns(ref, [(yy * 2 + xl) * 256 for yy in range(4)], 256) for ref in (gm, gr)],
         )
-        for z in range(SPLIT):
-            for yy in range(4):
-                for k in range(2):
-                    at, col = 512 + z * 64 + k * 32, (yy * 2 + k) * 128
+        for z in range(SPLIT + 1):
+            for k in range(2):
+                part, at = up_rows(z, k)
+                for yy in range(4 if part == "x" else 0):
+                    col = (yy * 2 + k) * 128
                     dst[yy, at : at + 32] = acc[z * 32 : z * 32 + 32, col : col + 128]
 
 
@@ -204,11 +210,11 @@
             [ref[SPLIT:8, :, 64:96].reshape((8 - SPLIT) * 64, 256) for ref in (lm, lr)],
             [columns(ref, [to * 512], 512) for ref in (gm, gr)],
         )
-        for z in range(8 - SPLIT):
-            for xx in range(4):
-                for k in range(2):
-                    row, col = (z * 2 + xx // 2) * 32, (xx % 2 * 2 + k) * 128
-                    at = z * 64 + k * 32
+        for z in range(SPLIT, 8):
+            for k in range(2):
+                part, at = up_rows(z, k)
+                for xx in range(4 if part == "y" else 0):
+                    row, col = ((z - SPLIT) * 2 + xx // 2) * 32, (xx % 2 * 2 + k) * 128
                     dst[xx, at : at + 32] = acc[row : row + 32, col : col + 128]
         acc = dot2(
             [ref[...].reshape(768, 256) for ref in (pm, pr)],
@@ -270,8 +276,10 @@
     x, y = (add3(*(ref[...] for ref in refs[3 * p : 3 * p + 3])) for p in range(2))
     for z in range(8):
         out[z, 0:64] = x[z * 64 : z * 64 + 64]
-        up, at = (x, 512 + z * 64) if z < SPLIT else (y, (z - SPLIT) * 64)
-        out[z, 64:128] = up[at : at + 64]
+        for k in range(2):
+            part, at = up_rows(z, k)
+            up = x if part == "x" else y
+            out[z, 64 + k * 32 : 96 + k * 32] = up[at : at + 32]
         at = CHUNK_Y - 384 + z * 48
         out[z, 128:176] = y[at : at + 48]
 

time: 98.1 us -> 98.1 us (level)
  blocking collectives: 31.6 us -> 33 us
  waiting for transfers between devices: 29 us -> 27.9 us
    all_to_all x1, blocking collectives: 18.5 us -> 20.2 us  [finish(): got = lax.all_to_all(packed, 'z', 0, 0, tiled=True)]
    ppermute x17, waiting for transfers between devices: 29 us -> 27.9 us  [move(): return lax.ppermute(value, AXES, sorted(pairs))]
  transfers between devices with their start and end apart: 17 -> 17, of which waited for: 10 -> 10; matrix products, arithmetic and copies ran while one was open for 0% -> 0% of each run, Pallas kernels for 16% -> 17%
where the time goes in v10:
time: 98.1 us; the launch traced here: 97.9 us
  blocking collectives  33 us (34%)
  waiting for transfers between devices  27.9 us (28%)
  starting transfers between devices  17.7 us (18%)
  Pallas kernels  17.3 us (18%)
  local copies, waits for them, and re-layouts  1.15 us (1%)
    ppermute x17, waiting for transfers between devices, move(): return lax.ppermute(value, AXES, sorted(pairs))  27.9 us
    all_to_all x1, blocking collectives, finish(): got = lax.all_to_all(packed, 'z', 0, 0, tiled=True)  20.2 us
    ppermute x17, starting transfers between devices, move(): return lax.ppermute(value, AXES, sorted(pairs))  17.7 us
    pallas_call x14, Pallas kernels, call(): pl.pallas_call(body, out_shape=[jax.ShapeDtypeStruct(s, d) for s, d in ou...  17.3 us
    all_to_all x1, blocking collectives, finish(): every = lax.all_to_all(copies, ('y', 'xl'), 0, 0, tiled=True)  12.8 us
  transfers between devices with their start and end apart: 17, of which 10 were waited for; matrix products, arithmetic and copies ran while one was open for 0% of the time, Pallas kernels for 17%

profile of v10, /device:TPU:4, one launch (start us, length us, event | category | flops | bytes accessed | tf_op | source)
XLA Modules:
  0.0 97.9 jit_solution(14040185648454334936)
XLA Ops:
  0.8 1.1 %copy-done.3 = bf16[256,1536]{1,0:T(8,128)(2,1)S(1)} copy-done((bf16[256,1536]{1,0:T(8,128)(2,1)S(1)}, bf16[256,1536]{1,0:T(8,128)(2,1)}, u32[]{:S(2)}) %copy-start.3) | copy-done | bytes 786456
  2.0 0.8 turn_patches.1
  2.8 0.6 collective-permute-start.2
  3.4 7.1 %gelu_pass.1 = (bf16[256,2048]{1,0:T(8,128)(2,1)S(1)}, f32[256,1024]{1,0:T(8,128)S(1)}, f32[256,1]{1,0:T(8,128)S(1)}, bf16[16,96,256]{2,1,0:T(8,128)(2,1)S(1)}, bf16[16,96,256]{2,1,0:T(8,128)(2,1)S(1)}) custom-call(s32[4]{0:T(128)S(1)} %pad_add_fusion.pos, f32[1,1024]{1,0:T(1,128)S(1)} %bitcast.7, bf16[256,1536]{1,0:T(8,128)(2,1)S(1)} %copy-done.4, ...), custom_call_target="tpu_custom_call" | custom-call | flops 8000000000 | bytes 1048576 | tf_op jit(solution)/shard_map/gelu_pass/pallas_call | solution.py:37
  11.1 1.6 %norm_back.1.em = bf16[256,1024]{1,0:T(8,128)(2,1)S(1)} custom-call(f32[1,1024]{1,0:T(1,128)S(1)} %bitcast.8, bf16[256,2048]{1,0:T(8,128)(2,1)S(1)} %get-tuple-element.38.preact_grad.gm, bf16[1024,2048]{1,0:T(8,128)(2,1)S(1)} %copy-done, bf16[256,1024]{1,0:T(8,128)(2,1)S(1)} %copy-done.1, f32[256,1024]{1,0:T(8,128)S(1)} %get-tuple-element.39.normal, ...), custom_call_target="tpu_custom_call" | custom-call | flops 2000000000 | bytes 1048576 | tf_op jit(solution)/shard_map/norm_back/pallas_call | solution.py:37
  13.3 1.1 %collective-permute-done.3 = bf16[16,96,256]{2,1,0:T(8,128)(2,1)S(1)} collective-permute-done((bf16[16,96,256]{2,1,0:T(8,128)(2,1)S(1)}, bf16[16,96,256]{2,1,0:T(8,128)(2,1)S(1)}, u32[]{:S(2)}, u32[]{:S(2)}) %collective-permute-start.3) | collective-permute-done | bytes 786464 | tf_op jit(solution)/shard_map/ppermute | solution.py:33
  14.4 2.5 %terms_x.1 = (bf16[4,800,128]{2,1,0:T(8,128)(2,1)S(1)}, bf16[4,800,128]{2,1,0:T(8,128)(2,1)S(1)}, bf16[4,800,128]{2,1,0:T(8,128)(2,1)S(1)}, bf16[4,800,128]{2,1,0:T(8,128)(2,1)S(1)}) custom-call(s32[4]{0:T(128)S(1)} %pad_add_fusion.pos, bf16[8,2,96,256]{3,2,1,0:T(8,128)(2,1)S(1)} %bitcast.11, bf16[8,2,96,256]{3,2,1,0:T(8,128)(2,1)S(1)} %bitcast.9, ...), custom_call_target="tpu_custom_call" | custom-call | flops 2000000000 | bytes 1048576 | tf_op jit(solution)/shard_map/terms_x/pallas_call | solution.py:37
  16.9 1.3 %collective-permute-start.6 = (bf16[4,800,128]{2,1,0:T(8,128)(2,1)S(1)}, bf16[4,800,128]{2,1,0:T(8,128)(2,1)S(1)}, u32[]{:S(2)}, u32[]{:S(2)}) collective-permute-start(bf16[4,800,128]{2,1,0:T(8,128)(2,1)S(1)} %get-tuple-element.53), channel_id=1, source_target_pairs={{0,32},{1,35},{2,34},{3,33},{4,36},{5,39},{6,38},{7,37},{8,40},{9,... | collective-permute-start | bytes 2457608 | tf_op jit(solution)/shard_map/ppermute | solution.py:33
  18.2 2.1 %terms_y.1 = (bf16[4,608,128]{2,1,0:T(8,128)(2,1)S(1)}, bf16[4,608,128]{2,1,0:T(8,128)(2,1)S(1)}, bf16[4,608,128]{2,1,0:T(8,128)(2,1)S(1)}, bf16[4,608,128]{2,1,0:T(8,128)(2,1)S(1)}) custom-call(s32[4]{0:T(128)S(1)} %pad_add_fusion.pos, bf16[8,2,96,256]{3,2,1,0:T(8,128)(2,1)S(1)} %bitcast.12, bf16[8,2,96,256]{3,2,1,0:T(8,128)(2,1)S(1)} %bitcast.10, ...), custom_call_target="tpu_custom_call" | custom-call | flops 2000000000 | bytes 1048576 | tf_op jit(solution)/shard_map/terms_y/pallas_call | solution.py:37
  20.4 1.8 %collective-permute-start.11 = (bf16[4,608,128]{2,1,0:T(8,128)(2,1)S(1)}, bf16[4,608,128]{2,1,0:T(8,128)(2,1)S(1)}, u32[]{:S(2)}, u32[]{:S(2)}) collective-permute-start(bf16[4,608,128]{2,1,0:T(8,128)(2,1)S(1)} %get-tuple-element.62), channel_id=1, source_target_pairs={{0,64},{1,193},{2,66},{3,195},{4,68},{5,197},{6,70},{7,199},{8,72}... | collective-permute-start | bytes 1867784 | tf_op jit(solution)/shard_map/ppermute | solution.py:33
  22.2 1.7 %collective-permute-start.12 = (bf16[4,608,128]{2,1,0:T(8,128)(2,1)S(1)}, bf16[4,608,128]{2,1,0:T(8,128)(2,1)S(1)}, u32[]{:S(2)}, u32[]{:S(2)}) collective-permute-start(bf16[4,608,128]{2,1,0:T(8,128)(2,1)S(1)} %get-tuple-element.63), channel_id=1, source_target_pairs={{0,192},{1,65},{2,194},{3,67},{4,196},{5,69},{6,198},{7,71},{8,200... | collective-permute-start | bytes 1867784 | tf_op jit(solution)/shard_map/ppermute | solution.py:33
  23.9 0.8 collective-permute-start.5
  24.7 8.8 %collective-permute-done.6.got = bf16[4,800,128]{2,1,0:T(8,128)(2,1)S(1)} collective-permute-done((bf16[4,800,128]{2,1,0:T(8,128)(2,1)S(1)}, bf16[4,800,128]{2,1,0:T(8,128)(2,1)S(1)}, u32[]{:S(2)}, u32[]{:S(2)}) %collective-permute-start.6) | collective-permute-done | bytes 819232 | tf_op jit(solution)/shard_map/ppermute | solution.py:33
  33.7 1.0 %collective-permute-start.7 = (bf16[4,800,128]{2,1,0:T(8,128)(2,1)S(1)}, bf16[4,800,128]{2,1,0:T(8,128)(2,1)S(1)}, u32[]{:S(2)}, u32[]{:S(2)}) collective-permute-start(bf16[4,800,128]{2,1,0:T(8,128)(2,1)S(1)} %pass_on.4), channel_id=1, source_target_pairs={{0,32},{1,35},{2,34},{3,33},{4,36},{5,39},{6,38},{7,37},{8,40},{9,... | collective-permute-start | bytes 2457608 | tf_op jit(solution)/shard_map/ppermute | solution.py:33
  34.7 3.1 %collective-permute-done.11.got = bf16[4,608,128]{2,1,0:T(8,128)(2,1)S(1)} collective-permute-done((bf16[4,608,128]{2,1,0:T(8,128)(2,1)S(1)}, bf16[4,608,128]{2,1,0:T(8,128)(2,1)S(1)}, u32[]{:S(2)}, u32[]{:S(2)}) %collective-permute-start.11) | collective-permute-done | bytes 622624 | tf_op jit(solution)/shard_map/ppermute | solution.py:33
  37.9 1.1 %collective-permute-start.13 = (bf16[4,608,128]{2,1,0:T(8,128)(2,1)S(1)}, bf16[4,608,128]{2,1,0:T(8,128)(2,1)S(1)}, u32[]{:S(2)}, u32[]{:S(2)}) collective-permute-start(bf16[4,608,128]{2,1,0:T(8,128)(2,1)S(1)} %pass_on.6), channel_id=1, source_target_pairs={{0,64},{1,193},{2,66},{3,195},{4,68},{5,197},{6,70},{7,199},{8,72}... | collective-permute-start | bytes 1867784 | tf_op jit(solution)/shard_map/ppermute | solution.py:33
  39.0 3.2 %collective-permute-done.5.near = bf16[4,800,128]{2,1,0:T(8,128)(2,1)S(1)} collective-permute-done((bf16[4,800,128]{2,1,0:T(8,128)(2,1)S(1)}, bf16[4,800,128]{2,1,0:T(8,128)(2,1)S(1)}, u32[]{:S(2)}, u32[]{:S(2)}) %collective-permute-start.5) | collective-permute-done | bytes 819232 | tf_op jit(solution)/shard_map/ppermute | solution.py:33
  42.2 4.7 %collective-permute-done.7.far = bf16[4,800,128]{2,1,0:T(8,128)(2,1)S(1)} collective-permute-done((bf16[4,800,128]{2,1,0:T(8,128)(2,1)S(1)}, bf16[4,800,128]{2,1,0:T(8,128)(2,1)S(1)}, u32[]{:S(2)}, u32[]{:S(2)}) %collective-permute-start.7) | collective-permute-done | bytes 819232 | tf_op jit(solution)/shard_map/ppermute | solution.py:33
  46.9 0.8 ring_turn_x.1
  47.8 2.1 %collective-permute-start.9 = (bf16[800,128]{1,0:T(8,128)(2,1)S(1)}, bf16[800,128]{1,0:T(8,128)(2,1)S(1)}, u32[]{:S(2)}, u32[]{:S(2)}) collective-permute-start(bf16[800,128]{1,0:T(8,128)(2,1)S(1)} %get-tuple-element.57), channel_id=1, source_target_pairs={{0,64},{1,193},{2,66},{3,195},{4,68},{5,197},{6,70},{7,199},{8,72}... | collective-permute-start | bytes 614408 | tf_op jit(solution)/shard_map/ppermute | solution.py:33
  49.9 0.8 ring_turn_y.1
  50.7 2.5 %collective-permute-start.14 = (bf16[608,128]{1,0:T(8,128)(2,1)S(1)}, bf16[608,128]{1,0:T(8,128)(2,1)S(1)}, u32[]{:S(2)}, u32[]{:S(2)}) collective-permute-start(bf16[608,128]{1,0:T(8,128)(2,1)S(1)} %get-tuple-element.68), channel_id=1, source_target_pairs={{0,32},{1,35},{2,34},{3,33},{4,36},{5,39},{6,38},{7,37},{8,40},{9,... | collective-permute-start | bytes 466952 | tf_op jit(solution)/shard_map/ppermute | solution.py:33
  53.2 0.8 collective-permute-start.8
  54.0 0.8 collective-permute-done.9.got
  54.9 1.4 %collective-permute-start.10 = (bf16[800,128]{1,0:T(8,128)(2,1)S(1)}, bf16[800,128]{1,0:T(8,128)(2,1)S(1)}, u32[]{:S(2)}, u32[]{:S(2)}) collective-permute-start(bf16[800,128]{1,0:T(8,128)(2,1)S(1)} %pass_on.5), channel_id=1, source_target_pairs={{0,64},{1,193},{2,66},{3,195},{4,68},{5,197},{6,70},{7,199},{8,72}... | collective-permute-start | bytes 614408 | tf_op jit(solution)/shard_map/ppermute | solution.py:33
  56.3 0.7 collective-permute-done.14.got
  56.9 1.5 %collective-permute-done.15.refs_4_ = bf16[608,128]{1,0:T(8,128)(2,1)S(1)} collective-permute-done((bf16[608,128]{1,0:T(8,128)(2,1)S(1)}, bf16[608,128]{1,0:T(8,128)(2,1)S(1)}, u32[]{:S(2)}, u32[]{:S(2)}) %collective-permute-start.15) | collective-permute-done | bytes 155680 | tf_op jit(solution)/shard_map/ppermute | solution.py:33
  58.5 1.7 %collective-permute-start.16 = (bf16[608,128]{1,0:T(8,128)(2,1)S(1)}, bf16[608,128]{1,0:T(8,128)(2,1)S(1)}, u32[]{:S(2)}, u32[]{:S(2)}) collective-permute-start(bf16[608,128]{1,0:T(8,128)(2,1)S(1)} %pass_on.7), channel_id=1, source_target_pairs={{0,32},{1,35},{2,34},{3,33},{4,36},{5,39},{6,38},{7,37},{8,40},{9,... | collective-permute-start | bytes 466952 | tf_op jit(solution)/shard_map/ppermute | solution.py:33
  60.1 3.6 %collective-permute-done.16.refs_5_ = bf16[608,128]{1,0:T(8,128)(2,1)S(1)} collective-permute-done((bf16[608,128]{1,0:T(8,128)(2,1)S(1)}, bf16[608,128]{1,0:T(8,128)(2,1)S(1)}, u32[]{:S(2)}, u32[]{:S(2)}) %collective-permute-start.16) | collective-permute-done | bytes 155680 | tf_op jit(solution)/shard_map/ppermute | solution.py:33
  63.9 20.2 %all_to_all.10.got = bf16[8,176,128]{2,1,0:T(8,128)(2,1)S(1)} all-to-all(bf16[8,176,128]{2,1,0:T(8,128)(2,1)S(1)} %z_pack.1), channel_id=1, replica_groups=mesh['y'=4,'xl'=2,'z'=8,'xh'=2,'c'=2] {'z'}, dimensions={0} | all-to-all | bytes 720896 | tf_op jit(solution)/shard_map/all_to_all | solution.py:311
  84.2 12.8 %all_to_all.11.got = bf16[8,176,128]{2,1,0:T(8,128)(2,1)S(1)} all-to-all(bf16[8,176,128]{2,1,0:T(8,128)(2,1)S(1)} %z_sum.1), channel_id=1, replica_groups=mesh['y'=4,'xl'=2,'z'=8,'xh'=2,'c'=2] {'y','xl'}, dimensions={0} | all-to-all | bytes 720896 | tf_op jit(solution)/shard_map/all_to_all | solution.py:313
  97.0 0.9 unpack.1
  (29 shorter events, 2.0 us)
Async XLA Ops:
  0.6 2.8 %copy-start.1 = (bf16[256,1024]{1,0:T(8,128)(2,1)S(1)}, bf16[256,1024]{1,0:T(8,128)(2,1)}, u32[]{:S(2)}) copy-start(bf16[256,1024]{1,0:T(8,128)(2,1)} %cm.1) | copy-start | bytes 1572868
  0.6 2.8 %copy-start.2 = (f32[1024]{0:T(1024)S(1)}, f32[1024]{0:T(1024)}, u32[]{:S(2)}) copy-start(f32[1024]{0:T(1024)} %param.8) | copy-start | bytes 12292
  0.7 10.1 %collective-permute-start.1 = (bf16[256,1024]{1,0:T(8,128)(2,1)}, bf16[256,1024]{1,0:T(8,128)(2,1)S(1)}, u32[]{:S(2)}, u32[]{:S(2)}) collective-permute-start(bf16[256,1024]{1,0:T(8,128)(2,1)} %cm.1), channel_id=1, source_target_pairs={{0,1},{1,0},{2,3},{3,2},{4,5},{5,4},{6,7},{7,6},{8,9},{9,8},{10,11... | collective-permute-start | bytes 1572872 | tf_op jit(solution)/shard_map/ppermute | solution.py:33
  0.8 1.1 %copy-start.3 = (bf16[256,1536]{1,0:T(8,128)(2,1)S(1)}, bf16[256,1536]{1,0:T(8,128)(2,1)}, u32[]{:S(2)}) copy-start(bf16[256,1536]{1,0:T(8,128)(2,1)} %p.3) | copy-start | bytes 2359300
  2.0 1.4 %copy-start.4 = (bf16[256,1536]{1,0:T(8,128)(2,1)S(1)}, bf16[256,1536]{1,0:T(8,128)(2,1)}, u32[]{:S(2)}) copy-start(bf16[256,1536]{1,0:T(8,128)(2,1)} %p.3) | copy-start | bytes 2359300
  2.8 8.0 %collective-permute-start.2 = (bf16[16,48,256]{2,1,0:T(8,128)(2,1)S(1)}, bf16[16,48,256]{2,1,0:T(8,128)(2,1)S(1)}, u32[]{:S(2)}, u32[]{:S(2)}) collective-permute-start(bf16[16,48,256]{2,1,0:T(8,128)(2,1)S(1)} %get-tuple-element.43), channel_id=1, source_target_pairs={{0,1},{1,0},{2,3},{3,2},{4,5},{5,4},{6,7},{7,6},{8,9},{9,8},{10,11... | collective-permute-start | bytes 1179656 | tf_op jit(solution)/shard_map/ppermute | solution.py:33
  3.4 7.7 %copy-start = (bf16[1024,2048]{1,0:T(8,128)(2,1)S(1)}, bf16[1024,2048]{1,0:T(8,128)(2,1)}, u32[]{:S(2)}) copy-start(bf16[1024,2048]{1,0:T(8,128)(2,1)} %up.1) | copy-start | bytes 12582916
  10.5 2.7 %collective-permute-start.4 = (bf16[256,2048]{1,0:T(8,128)(2,1)S(1)}, bf16[256,2048]{1,0:T(8,128)(2,1)S(1)}, u32[]{:S(2)}, u32[]{:S(2)}) collective-permute-start(bf16[256,2048]{1,0:T(8,128)(2,1)S(1)} %get-tuple-element.38.preact_grad.gm), channel_id=1, source_target_pairs={{0,1},{1,0},{2,3},{3,2},{4,5},{5,4},{6,7},{7,6},{8,9},{9,8},{10,11... | collective-permute-start | bytes 3145736 | tf_op jit(solution)/shard_map/ppermute | solution.py:33
  10.8 3.6 %collective-permute-start.3 = (bf16[16,96,256]{2,1,0:T(8,128)(2,1)S(1)}, bf16[16,96,256]{2,1,0:T(8,128)(2,1)S(1)}, u32[]{:S(2)}, u32[]{:S(2)}) collective-permute-start(bf16[16,96,256]{2,1,0:T(8,128)(2,1)S(1)} %get-tuple-element.44), channel_id=1, source_target_pairs={{0,1},{1,0},{2,3},{3,2},{4,5},{5,4},{6,7},{7,6},{8,9},{9,8},{10,11... | collective-permute-start | bytes 2359304 | tf_op jit(solution)/shard_map/ppermute | solution.py:33
  12.7 4.2 %collective-permute-start = (bf16[256,1024]{1,0:T(8,128)(2,1)S(1)}, bf16[256,1024]{1,0:T(8,128)(2,1)S(1)}, u32[]{:S(2)}, u32[]{:S(2)}) collective-permute-start(bf16[256,1024]{1,0:T(8,128)(2,1)S(1)} %norm_back.1.em), channel_id=1, source_target_pairs={{0,1},{1,0},{2,3},{3,2},{4,5},{5,4},{6,7},{7,6},{8,9},{9,8},{10,11... | collective-permute-start | bytes 1572872 | tf_op jit(solution)/shard_map/ppermute | solution.py:33
  16.9 16.5 %collective-permute-start.6 = (bf16[4,800,128]{2,1,0:T(8,128)(2,1)S(1)}, bf16[4,800,128]{2,1,0:T(8,128)(2,1)S(1)}, u32[]{:S(2)}, u32[]{:S(2)}) collective-permute-start(bf16[4,800,128]{2,1,0:T(8,128)(2,1)S(1)} %get-tuple-element.53), channel_id=1, source_target_pairs={{0,32},{1,35},{2,34},{3,33},{4,36},{5,39},{6,38},{7,37},{8,40},{9,... | collective-permute-start | bytes 2457608 | tf_op jit(solution)/shard_map/ppermute | solution.py:33
  20.4 17.4 %collective-permute-start.11 = (bf16[4,608,128]{2,1,0:T(8,128)(2,1)S(1)}, bf16[4,608,128]{2,1,0:T(8,128)(2,1)S(1)}, u32[]{:S(2)}, u32[]{:S(2)}) collective-permute-start(bf16[4,608,128]{2,1,0:T(8,128)(2,1)S(1)} %get-tuple-element.62), channel_id=1, source_target_pairs={{0,64},{1,193},{2,66},{3,195},{4,68},{5,197},{6,70},{7,199},{8,72}... | collective-permute-start | bytes 1867784 | tf_op jit(solution)/shard_map/ppermute | solution.py:33
  22.2 15.6 %collective-permute-start.12 = (bf16[4,608,128]{2,1,0:T(8,128)(2,1)S(1)}, bf16[4,608,128]{2,1,0:T(8,128)(2,1)S(1)}, u32[]{:S(2)}, u32[]{:S(2)}) collective-permute-start(bf16[4,608,128]{2,1,0:T(8,128)(2,1)S(1)} %get-tuple-element.63), channel_id=1, source_target_pairs={{0,192},{1,65},{2,194},{3,67},{4,196},{5,69},{6,198},{7,71},{8,200... | collective-permute-start | bytes 1867784 | tf_op jit(solution)/shard_map/ppermute | solution.py:33
  23.9 18.3 %collective-permute-start.5 = (bf16[4,800,128]{2,1,0:T(8,128)(2,1)S(1)}, bf16[4,800,128]{2,1,0:T(8,128)(2,1)S(1)}, u32[]{:S(2)}, u32[]{:S(2)}) collective-permute-start(bf16[4,800,128]{2,1,0:T(8,128)(2,1)S(1)} %get-tuple-element.51), channel_id=1, source_target_pairs={{0,34},{1,33},{2,32},{3,35},{4,38},{5,37},{6,36},{7,39},{8,42},{9,... | collective-permute-start | bytes 2457608 | tf_op jit(solution)/shard_map/ppermute | solution.py:33
  33.7 13.2 %collective-permute-start.7 = (bf16[4,800,128]{2,1,0:T(8,128)(2,1)S(1)}, bf16[4,800,128]{2,1,0:T(8,128)(2,1)S(1)}, u32[]{:S(2)}, u32[]{:S(2)}) collective-permute-start(bf16[4,800,128]{2,1,0:T(8,128)(2,1)S(1)} %pass_on.4), channel_id=1, source_target_pairs={{0,32},{1,35},{2,34},{3,33},{4,36},{5,39},{6,38},{7,37},{8,40},{9,... | collective-permute-start | bytes 2457608 | tf_op jit(solution)/shard_map/ppermute | solution.py:33
  37.9 12.0 %collective-permute-start.13 = (bf16[4,608,128]{2,1,0:T(8,128)(2,1)S(1)}, bf16[4,608,128]{2,1,0:T(8,128)(2,1)S(1)}, u32[]{:S(2)}, u32[]{:S(2)}) collective-permute-start(bf16[4,608,128]{2,1,0:T(8,128)(2,1)S(1)} %pass_on.6), channel_id=1, source_target_pairs={{0,64},{1,193},{2,66},{3,195},{4,68},{5,197},{6,70},{7,199},{8,72}... | collective-permute-start | bytes 1867784 | tf_op jit(solution)/shard_map/ppermute | solution.py:33
  47.8 7.0 %collective-permute-start.9 = (bf16[800,128]{1,0:T(8,128)(2,1)S(1)}, bf16[800,128]{1,0:T(8,128)(2,1)S(1)}, u32[]{:S(2)}, u32[]{:S(2)}) collective-permute-start(bf16[800,128]{1,0:T(8,128)(2,1)S(1)} %get-tuple-element.57), channel_id=1, source_target_pairs={{0,64},{1,193},{2,66},{3,195},{4,68},{5,197},{6,70},{7,199},{8,72}... | collective-permute-start | bytes 614408 | tf_op jit(solution)/shard_map/ppermute | solution.py:33
  50.7 6.3 %collective-permute-start.14 = (bf16[608,128]{1,0:T(8,128)(2,1)S(1)}, bf16[608,128]{1,0:T(8,128)(2,1)S(1)}, u32[]{:S(2)}, u32[]{:S(2)}) collective-permute-start(bf16[608,128]{1,0:T(8,128)(2,1)S(1)} %get-tuple-element.68), channel_id=1, source_target_pairs={{0,32},{1,35},{2,34},{3,33},{4,36},{5,39},{6,38},{7,37},{8,40},{9,... | collective-permute-start | bytes 466952 | tf_op jit(solution)/shard_map/ppermute | solution.py:33
  53.2 5.2 %collective-permute-start.15 = (bf16[608,128]{1,0:T(8,128)(2,1)S(1)}, bf16[608,128]{1,0:T(8,128)(2,1)S(1)}, u32[]{:S(2)}, u32[]{:S(2)}) collective-permute-start(bf16[608,128]{1,0:T(8,128)(2,1)S(1)} %get-tuple-element.69), channel_id=1, source_target_pairs={{0,34},{1,33},{2,32},{3,35},{4,38},{5,37},{6,36},{7,39},{8,42},{9,... | collective-permute-start | bytes 466952 | tf_op jit(solution)/shard_map/ppermute | solution.py:33
  53.2 10.6 %collective-permute-start.8 = (bf16[800,128]{1,0:T(8,128)(2,1)S(1)}, bf16[800,128]{1,0:T(8,128)(2,1)S(1)}, u32[]{:S(2)}, u32[]{:S(2)}) collective-permute-start(bf16[800,128]{1,0:T(8,128)(2,1)S(1)} %get-tuple-element.55), channel_id=1, source_target_pairs={{0,192},{1,65},{2,194},{3,67},{4,196},{5,69},{6,198},{7,71},{8,200... | collective-permute-start | bytes 614408 | tf_op jit(solution)/shard_map/ppermute | solution.py:33
  54.9 8.9 %collective-permute-start.10 = (bf16[800,128]{1,0:T(8,128)(2,1)S(1)}, bf16[800,128]{1,0:T(8,128)(2,1)S(1)}, u32[]{:S(2)}, u32[]{:S(2)}) collective-permute-start(bf16[800,128]{1,0:T(8,128)(2,1)S(1)} %pass_on.5), channel_id=1, source_target_pairs={{0,64},{1,193},{2,66},{3,195},{4,68},{5,197},{6,70},{7,199},{8,72}... | collective-permute-start | bytes 614408 | tf_op jit(solution)/shard_map/ppermute | solution.py:33
  58.5 5.3 %collective-permute-start.16 = (bf16[608,128]{1,0:T(8,128)(2,1)S(1)}, bf16[608,128]{1,0:T(8,128)(2,1)S(1)}, u32[]{:S(2)}, u32[]{:S(2)}) collective-permute-start(bf16[608,128]{1,0:T(8,128)(2,1)S(1)} %pass_on.7), channel_id=1, source_target_pairs={{0,32},{1,35},{2,34},{3,33},{4,36},{5,39},{6,38},{7,37},{8,40},{9,... | collective-permute-start | bytes 466952 | tf_op jit(solution)/shard_map/ppermute | solution.py:33

commit v11 on v10

--- a/solution.py
+++ b/solution.py
@@ -99,19 +99,19 @@
         for half in range(2):
             at = b * 2 + half
             t[b, half, 64:96] = nt[at * 32 : at * 32 + 32]
-    for j in range(8):
-        if j % 4 == 0:
-            copies[3 + j // 2].wait()
-            copies[4 + j // 2].wait()
-        cols = slice(j * 256, j * 256 + 256)
+    for j in range(4):
+        if j % 2 == 0:
+            copies[3 + j].wait()
+            copies[4 + j].wait()
+        cols = slice(j * 512, j * 512 + 512)
         pre = jnp.dot(normed, u[:, cols], preferred_element_type=F32)
         grad = lax.dot_general(g[...], d[cols], OVER_COLUMNS, preferred_element_type=F32)
         cdf = 0.5 * (1.0 + lax.erf(pre * math.sqrt(0.5)))
         slope = cdf + pre * jnp.exp(-0.5 * pre * pre) * (1.0 / math.sqrt(2.0 * math.pi))
         preact_grad[:, cols] = (grad * slope).astype(BF)
         ht = (pre * cdf).astype(BF).T
-        for q in range(4):
-            t[j * 2 + q // 2, q % 2, 0:64] = ht[q * 64 : q * 64 + 64]
+        for q in range(8):
+            t[j * 4 + q // 2, q % 2, 0:64] = ht[q * 64 : q * 64 + 64]
     c = pos[3]
     mine[...] = t[:, c]
     send[...] = t[:, 1 - c]

time: 98.1 us -> 98 us (level)
  transfers between devices with their start and end apart: 17 -> 17, of which waited for: 10 -> 10; matrix products, arithmetic and copies ran while one was open for 0% -> 0% of each run, Pallas kernels for 17% -> 16%
where the time goes in v11:
time: 98 us; the launch traced here: 97.7 us
  blocking collectives  33 us (34%)
  waiting for transfers between devices  27.9 us (28%)
  starting transfers between devices  17.7 us (18%)
  Pallas kernels  17.1 us (17%)
  local copies, waits for them, and re-layouts  1.15 us (1%)
    ppermute x17, waiting for transfers between devices, move(): return lax.ppermute(value, AXES, sorted(pairs))  27.9 us
    all_to_all x1, blocking collectives, finish(): got = lax.all_to_all(packed, 'z', 0, 0, tiled=True)  20.2 us
    ppermute x17, starting transfers between devices, move(): return lax.ppermute(value, AXES, sorted(pairs))  17.7 us
    pallas_call x14, Pallas kernels, call(): pl.pallas_call(body, out_shape=[jax.ShapeDtypeStruct(s, d) for s, d in ou...  17.1 us
    all_to_all x1, blocking collectives, finish(): every = lax.all_to_all(copies, ('y', 'xl'), 0, 0, tiled=True)  12.8 us
  transfers between devices with their start and end apart: 17, of which 10 were waited for; matrix products, arithmetic and copies ran while one was open for 0% of the time, Pallas kernels for 16%

profile of v11, /device:TPU:4, one launch (start us, length us, event | category | flops | bytes accessed | tf_op | source)
XLA Modules:
  0.0 97.7 jit_solution(4117060727765347827)
XLA Ops:
  0.8 1.1 %copy-done.3 = bf16[256,1536]{1,0:T(8,128)(2,1)S(1)} copy-done((bf16[256,1536]{1,0:T(8,128)(2,1)S(1)}, bf16[256,1536]{1,0:T(8,128)(2,1)}, u32[]{:S(2)}) %copy-start.3) | copy-done | bytes 786456
  2.0 0.8 turn_patches.1
  2.8 0.6 collective-permute-start.2
  3.4 7.0 %gelu_pass.1 = (bf16[256,2048]{1,0:T(8,128)(2,1)S(1)}, f32[256,1024]{1,0:T(8,128)S(1)}, f32[256,1]{1,0:T(8,128)S(1)}, bf16[16,96,256]{2,1,0:T(8,128)(2,1)S(1)}, bf16[16,96,256]{2,1,0:T(8,128)(2,1)S(1)}) custom-call(s32[4]{0:T(128)S(1)} %pad_add_fusion.pos, f32[1,1024]{1,0:T(1,128)S(1)} %bitcast.7, bf16[256,1536]{1,0:T(8,128)(2,1)S(1)} %copy-done.4, ...), custom_call_target="tpu_custom_call" | custom-call | flops 8000000000 | bytes 1048576 | tf_op jit(solution)/shard_map/gelu_pass/pallas_call | solution.py:37
  11.0 1.6 %norm_back.1.em = bf16[256,1024]{1,0:T(8,128)(2,1)S(1)} custom-call(f32[1,1024]{1,0:T(1,128)S(1)} %bitcast.8, bf16[256,2048]{1,0:T(8,128)(2,1)S(1)} %get-tuple-element.38.preact_grad.gm, bf16[1024,2048]{1,0:T(8,128)(2,1)S(1)} %copy-done, bf16[256,1024]{1,0:T(8,128)(2,1)S(1)} %copy-done.1, f32[256,1024]{1,0:T(8,128)S(1)} %get-tuple-element.39.normal, ...), custom_call_target="tpu_custom_call" | custom-call | flops 2000000000 | bytes 1048576 | tf_op jit(solution)/shard_map/norm_back/pallas_call | solution.py:37
  13.2 1.1 %collective-permute-done.3 = bf16[16,96,256]{2,1,0:T(8,128)(2,1)S(1)} collective-permute-done((bf16[16,96,256]{2,1,0:T(8,128)(2,1)S(1)}, bf16[16,96,256]{2,1,0:T(8,128)(2,1)S(1)}, u32[]{:S(2)}, u32[]{:S(2)}) %collective-permute-start.3) | collective-permute-done | bytes 786464 | tf_op jit(solution)/shard_map/ppermute | solution.py:33
  14.3 2.5 %terms_x.1 = (bf16[4,800,128]{2,1,0:T(8,128)(2,1)S(1)}, bf16[4,800,128]{2,1,0:T(8,128)(2,1)S(1)}, bf16[4,800,128]{2,1,0:T(8,128)(2,1)S(1)}, bf16[4,800,128]{2,1,0:T(8,128)(2,1)S(1)}) custom-call(s32[4]{0:T(128)S(1)} %pad_add_fusion.pos, bf16[8,2,96,256]{3,2,1,0:T(8,128)(2,1)S(1)} %bitcast.11, bf16[8,2,96,256]{3,2,1,0:T(8,128)(2,1)S(1)} %bitcast.9, ...), custom_call_target="tpu_custom_call" | custom-call | flops 2000000000 | bytes 1048576 | tf_op jit(solution)/shard_map/terms_x/pallas_call | solution.py:37
  16.8 1.3 %collective-permute-start.6 = (bf16[4,800,128]{2,1,0:T(8,128)(2,1)S(1)}, bf16[4,800,128]{2,1,0:T(8,128)(2,1)S(1)}, u32[]{:S(2)}, u32[]{:S(2)}) collective-permute-start(bf16[4,800,128]{2,1,0:T(8,128)(2,1)S(1)} %get-tuple-element.53), channel_id=1, source_target_pairs={{0,32},{1,35},{2,34},{3,33},{4,36},{5,39},{6,38},{7,37},{8,40},{9,... | collective-permute-start | bytes 2457608 | tf_op jit(solution)/shard_map/ppermute | solution.py:33
  18.1 2.1 %terms_y.1 = (bf16[4,608,128]{2,1,0:T(8,128)(2,1)S(1)}, bf16[4,608,128]{2,1,0:T(8,128)(2,1)S(1)}, bf16[4,608,128]{2,1,0:T(8,128)(2,1)S(1)}, bf16[4,608,128]{2,1,0:T(8,128)(2,1)S(1)}) custom-call(s32[4]{0:T(128)S(1)} %pad_add_fusion.pos, bf16[8,2,96,256]{3,2,1,0:T(8,128)(2,1)S(1)} %bitcast.12, bf16[8,2,96,256]{3,2,1,0:T(8,128)(2,1)S(1)} %bitcast.10, ...), custom_call_target="tpu_custom_call" | custom-call | flops 2000000000 | bytes 1048576 | tf_op jit(solution)/shard_map/terms_y/pallas_call | solution.py:37
  20.2 1.9 %collective-permute-start.11 = (bf16[4,608,128]{2,1,0:T(8,128)(2,1)S(1)}, bf16[4,608,128]{2,1,0:T(8,128)(2,1)S(1)}, u32[]{:S(2)}, u32[]{:S(2)}) collective-permute-start(bf16[4,608,128]{2,1,0:T(8,128)(2,1)S(1)} %get-tuple-element.62), channel_id=1, source_target_pairs={{0,64},{1,193},{2,66},{3,195},{4,68},{5,197},{6,70},{7,199},{8,72}... | collective-permute-start | bytes 1867784 | tf_op jit(solution)/shard_map/ppermute | solution.py:33
  22.1 1.6 %collective-permute-start.12 = (bf16[4,608,128]{2,1,0:T(8,128)(2,1)S(1)}, bf16[4,608,128]{2,1,0:T(8,128)(2,1)S(1)}, u32[]{:S(2)}, u32[]{:S(2)}) collective-permute-start(bf16[4,608,128]{2,1,0:T(8,128)(2,1)S(1)} %get-tuple-element.63), channel_id=1, source_target_pairs={{0,192},{1,65},{2,194},{3,67},{4,196},{5,69},{6,198},{7,71},{8,200... | collective-permute-start | bytes 1867784 | tf_op jit(solution)/shard_map/ppermute | solution.py:33
  23.7 0.8 collective-permute-start.5
  24.6 8.8 %collective-permute-done.6.got = bf16[4,800,128]{2,1,0:T(8,128)(2,1)S(1)} collective-permute-done((bf16[4,800,128]{2,1,0:T(8,128)(2,1)S(1)}, bf16[4,800,128]{2,1,0:T(8,128)(2,1)S(1)}, u32[]{:S(2)}, u32[]{:S(2)}) %collective-permute-start.6) | collective-permute-done | bytes 819232 | tf_op jit(solution)/shard_map/ppermute | solution.py:33
  33.6 1.0 %collective-permute-start.7 = (bf16[4,800,128]{2,1,0:T(8,128)(2,1)S(1)}, bf16[4,800,128]{2,1,0:T(8,128)(2,1)S(1)}, u32[]{:S(2)}, u32[]{:S(2)}) collective-permute-start(bf16[4,800,128]{2,1,0:T(8,128)(2,1)S(1)} %pass_on.4), channel_id=1, source_target_pairs={{0,32},{1,35},{2,34},{3,33},{4,36},{5,39},{6,38},{7,37},{8,40},{9,... | collective-permute-start | bytes 2457608 | tf_op jit(solution)/shard_map/ppermute | solution.py:33
  34.6 3.1 %collective-permute-done.11.got = bf16[4,608,128]{2,1,0:T(8,128)(2,1)S(1)} collective-permute-done((bf16[4,608,128]{2,1,0:T(8,128)(2,1)S(1)}, bf16[4,608,128]{2,1,0:T(8,128)(2,1)S(1)}, u32[]{:S(2)}, u32[]{:S(2)}) %collective-permute-start.11) | collective-permute-done | bytes 622624 | tf_op jit(solution)/shard_map/ppermute | solution.py:33
  37.8 1.1 %collective-permute-start.13 = (bf16[4,608,128]{2,1,0:T(8,128)(2,1)S(1)}, bf16[4,608,128]{2,1,0:T(8,128)(2,1)S(1)}, u32[]{:S(2)}, u32[]{:S(2)}) collective-permute-start(bf16[4,608,128]{2,1,0:T(8,128)(2,1)S(1)} %pass_on.6), channel_id=1, source_target_pairs={{0,64},{1,193},{2,66},{3,195},{4,68},{5,197},{6,70},{7,199},{8,72}... | collective-permute-start | bytes 1867784 | tf_op jit(solution)/shard_map/ppermute | solution.py:33
  38.9 3.2 %collective-permute-done.5.near = bf16[4,800,128]{2,1,0:T(8,128)(2,1)S(1)} collective-permute-done((bf16[4,800,128]{2,1,0:T(8,128)(2,1)S(1)}, bf16[4,800,128]{2,1,0:T(8,128)(2,1)S(1)}, u32[]{:S(2)}, u32[]{:S(2)}) %collective-permute-start.5) | collective-permute-done | bytes 819232 | tf_op jit(solution)/shard_map/ppermute | solution.py:33
  42.1 4.7 %collective-permute-done.7.far = bf16[4,800,128]{2,1,0:T(8,128)(2,1)S(1)} collective-permute-done((bf16[4,800,128]{2,1,0:T(8,128)(2,1)S(1)}, bf16[4,800,128]{2,1,0:T(8,128)(2,1)S(1)}, u32[]{:S(2)}, u32[]{:S(2)}) %collective-permute-start.7) | collective-permute-done | bytes 819232 | tf_op jit(solution)/shard_map/ppermute | solution.py:33
  46.8 0.8 ring_turn_x.1
  47.6 2.1 %collective-permute-start.9 = (bf16[800,128]{1,0:T(8,128)(2,1)S(1)}, bf16[800,128]{1,0:T(8,128)(2,1)S(1)}, u32[]{:S(2)}, u32[]{:S(2)}) collective-permute-start(bf16[800,128]{1,0:T(8,128)(2,1)S(1)} %get-tuple-element.57), channel_id=1, source_target_pairs={{0,64},{1,193},{2,66},{3,195},{4,68},{5,197},{6,70},{7,199},{8,72}... | collective-permute-start | bytes 614408 | tf_op jit(solution)/shard_map/ppermute | solution.py:33
  49.8 0.8 ring_turn_y.1
  50.5 2.5 %collective-permute-start.14 = (bf16[608,128]{1,0:T(8,128)(2,1)S(1)}, bf16[608,128]{1,0:T(8,128)(2,1)S(1)}, u32[]{:S(2)}, u32[]{:S(2)}) collective-permute-start(bf16[608,128]{1,0:T(8,128)(2,1)S(1)} %get-tuple-element.68), channel_id=1, source_target_pairs={{0,32},{1,35},{2,34},{3,33},{4,36},{5,39},{6,38},{7,37},{8,40},{9,... | collective-permute-start | bytes 466952 | tf_op jit(solution)/shard_map/ppermute | solution.py:33
  53.1 0.8 collective-permute-start.8
  53.8 0.8 collective-permute-done.9.got
  54.7 1.4 %collective-permute-start.10 = (bf16[800,128]{1,0:T(8,128)(2,1)S(1)}, bf16[800,128]{1,0:T(8,128)(2,1)S(1)}, u32[]{:S(2)}, u32[]{:S(2)}) collective-permute-start(bf16[800,128]{1,0:T(8,128)(2,1)S(1)} %pass_on.5), channel_id=1, source_target_pairs={{0,64},{1,193},{2,66},{3,195},{4,68},{5,197},{6,70},{7,199},{8,72}... | collective-permute-start | bytes 614408 | tf_op jit(solution)/shard_map/ppermute | solution.py:33
  56.2 0.7 collective-permute-done.14.got
  56.8 1.5 %collective-permute-done.15.refs_4_ = bf16[608,128]{1,0:T(8,128)(2,1)S(1)} collective-permute-done((bf16[608,128]{1,0:T(8,128)(2,1)S(1)}, bf16[608,128]{1,0:T(8,128)(2,1)S(1)}, u32[]{:S(2)}, u32[]{:S(2)}) %collective-permute-start.15) | collective-permute-done | bytes 155680 | tf_op jit(solution)/shard_map/ppermute | solution.py:33
  58.4 1.6 %collective-permute-start.16 = (bf16[608,128]{1,0:T(8,128)(2,1)S(1)}, bf16[608,128]{1,0:T(8,128)(2,1)S(1)}, u32[]{:S(2)}, u32[]{:S(2)}) collective-permute-start(bf16[608,128]{1,0:T(8,128)(2,1)S(1)} %pass_on.7), channel_id=1, source_target_pairs={{0,32},{1,35},{2,34},{3,33},{4,36},{5,39},{6,38},{7,37},{8,40},{9,... | collective-permute-start | bytes 466952 | tf_op jit(solution)/shard_map/ppermute | solution.py:33
  60.0 3.7 %collective-permute-done.16.refs_5_ = bf16[608,128]{1,0:T(8,128)(2,1)S(1)} collective-permute-done((bf16[608,128]{1,0:T(8,128)(2,1)S(1)}, bf16[608,128]{1,0:T(8,128)(2,1)S(1)}, u32[]{:S(2)}, u32[]{:S(2)}) %collective-permute-start.16) | collective-permute-done | bytes 155680 | tf_op jit(solution)/shard_map/ppermute | solution.py:33
  63.8 20.2 %all_to_all.10.got = bf16[8,176,128]{2,1,0:T(8,128)(2,1)S(1)} all-to-all(bf16[8,176,128]{2,1,0:T(8,128)(2,1)S(1)} %z_pack.1), channel_id=1, replica_groups=mesh['y'=4,'xl'=2,'z'=8,'xh'=2,'c'=2] {'z'}, dimensions={0} | all-to-all | bytes 720896 | tf_op jit(solution)/shard_map/all_to_all | solution.py:311
  84.0 12.8 %all_to_all.11.got = bf16[8,176,128]{2,1,0:T(8,128)(2,1)S(1)} all-to-all(bf16[8,176,128]{2,1,0:T(8,128)(2,1)S(1)} %z_sum.1), channel_id=1, replica_groups=mesh['y'=4,'xl'=2,'z'=8,'xh'=2,'c'=2] {'y','xl'}, dimensions={0} | all-to-all | bytes 720896 | tf_op jit(solution)/shard_map/all_to_all | solution.py:313
  96.8 0.9 unpack.1
  (29 shorter events, 2.0 us)
Async XLA Ops:
  0.6 2.8 %copy-start.1 = (bf16[256,1024]{1,0:T(8,128)(2,1)S(1)}, bf16[256,1024]{1,0:T(8,128)(2,1)}, u32[]{:S(2)}) copy-start(bf16[256,1024]{1,0:T(8,128)(2,1)} %cm.1) | copy-start | bytes 1572868
  0.6 2.8 %copy-start.2 = (f32[1024]{0:T(1024)S(1)}, f32[1024]{0:T(1024)}, u32[]{:S(2)}) copy-start(f32[1024]{0:T(1024)} %param.8) | copy-start | bytes 12292
  0.7 10.0 %collective-permute-start.1 = (bf16[256,1024]{1,0:T(8,128)(2,1)}, bf16[256,1024]{1,0:T(8,128)(2,1)S(1)}, u32[]{:S(2)}, u32[]{:S(2)}) collective-permute-start(bf16[256,1024]{1,0:T(8,128)(2,1)} %cm.1), channel_id=1, source_target_pairs={{0,1},{1,0},{2,3},{3,2},{4,5},{5,4},{6,7},{7,6},{8,9},{9,8},{10,11... | collective-permute-start | bytes 1572872 | tf_op jit(solution)/shard_map/ppermute | solution.py:33
  0.8 1.1 %copy-start.3 = (bf16[256,1536]{1,0:T(8,128)(2,1)S(1)}, bf16[256,1536]{1,0:T(8,128)(2,1)}, u32[]{:S(2)}) copy-start(bf16[256,1536]{1,0:T(8,128)(2,1)} %p.3) | copy-start | bytes 2359300
  2.0 1.4 %copy-start.4 = (bf16[256,1536]{1,0:T(8,128)(2,1)S(1)}, bf16[256,1536]{1,0:T(8,128)(2,1)}, u32[]{:S(2)}) copy-start(bf16[256,1536]{1,0:T(8,128)(2,1)} %p.3) | copy-start | bytes 2359300
  2.8 7.8 %collective-permute-start.2 = (bf16[16,48,256]{2,1,0:T(8,128)(2,1)S(1)}, bf16[16,48,256]{2,1,0:T(8,128)(2,1)S(1)}, u32[]{:S(2)}, u32[]{:S(2)}) collective-permute-start(bf16[16,48,256]{2,1,0:T(8,128)(2,1)S(1)} %get-tuple-element.43), channel_id=1, source_target_pairs={{0,1},{1,0},{2,3},{3,2},{4,5},{5,4},{6,7},{7,6},{8,9},{9,8},{10,11... | collective-permute-start | bytes 1179656 | tf_op jit(solution)/shard_map/ppermute | solution.py:33
  3.4 7.6 %copy-start = (bf16[1024,2048]{1,0:T(8,128)(2,1)S(1)}, bf16[1024,2048]{1,0:T(8,128)(2,1)}, u32[]{:S(2)}) copy-start(bf16[1024,2048]{1,0:T(8,128)(2,1)} %up.1) | copy-start | bytes 12582916
  10.4 2.7 %collective-permute-start.4 = (bf16[256,2048]{1,0:T(8,128)(2,1)S(1)}, bf16[256,2048]{1,0:T(8,128)(2,1)S(1)}, u32[]{:S(2)}, u32[]{:S(2)}) collective-permute-start(bf16[256,2048]{1,0:T(8,128)(2,1)S(1)} %get-tuple-element.38.preact_grad.gm), channel_id=1, source_target_pairs={{0,1},{1,0},{2,3},{3,2},{4,5},{5,4},{6,7},{7,6},{8,9},{9,8},{10,11... | collective-permute-start | bytes 3145736 | tf_op jit(solution)/shard_map/ppermute | solution.py:33
  10.7 3.6 %collective-permute-start.3 = (bf16[16,96,256]{2,1,0:T(8,128)(2,1)S(1)}, bf16[16,96,256]{2,1,0:T(8,128)(2,1)S(1)}, u32[]{:S(2)}, u32[]{:S(2)}) collective-permute-start(bf16[16,96,256]{2,1,0:T(8,128)(2,1)S(1)} %get-tuple-element.44), channel_id=1, source_target_pairs={{0,1},{1,0},{2,3},{3,2},{4,5},{5,4},{6,7},{7,6},{8,9},{9,8},{10,11... | collective-permute-start | bytes 2359304 | tf_op jit(solution)/shard_map/ppermute | solution.py:33
  12.6 4.2 %collective-permute-start = (bf16[256,1024]{1,0:T(8,128)(2,1)S(1)}, bf16[256,1024]{1,0:T(8,128)(2,1)S(1)}, u32[]{:S(2)}, u32[]{:S(2)}) collective-permute-start(bf16[256,1024]{1,0:T(8,128)(2,1)S(1)} %norm_back.1.em), channel_id=1, source_target_pairs={{0,1},{1,0},{2,3},{3,2},{4,5},{5,4},{6,7},{7,6},{8,9},{9,8},{10,11... | collective-permute-start | bytes 1572872 | tf_op jit(solution)/shard_map/ppermute | solution.py:33
  16.8 16.5 %collective-permute-start.6 = (bf16[4,800,128]{2,1,0:T(8,128)(2,1)S(1)}, bf16[4,800,128]{2,1,0:T(8,128)(2,1)S(1)}, u32[]{:S(2)}, u32[]{:S(2)}) collective-permute-start(bf16[4,800,128]{2,1,0:T(8,128)(2,1)S(1)} %get-tuple-element.53), channel_id=1, source_target_pairs={{0,32},{1,35},{2,34},{3,33},{4,36},{5,39},{6,38},{7,37},{8,40},{9,... | collective-permute-start | bytes 2457608 | tf_op jit(solution)/shard_map/ppermute | solution.py:33
  20.2 17.4 %collective-permute-start.11 = (bf16[4,608,128]{2,1,0:T(8,128)(2,1)S(1)}, bf16[4,608,128]{2,1,0:T(8,128)(2,1)S(1)}, u32[]{:S(2)}, u32[]{:S(2)}) collective-permute-start(bf16[4,608,128]{2,1,0:T(8,128)(2,1)S(1)} %get-tuple-element.62), channel_id=1, source_target_pairs={{0,64},{1,193},{2,66},{3,195},{4,68},{5,197},{6,70},{7,199},{8,72}... | collective-permute-start | bytes 1867784 | tf_op jit(solution)/shard_map/ppermute | solution.py:33
  22.1 15.5 %collective-permute-start.12 = (bf16[4,608,128]{2,1,0:T(8,128)(2,1)S(1)}, bf16[4,608,128]{2,1,0:T(8,128)(2,1)S(1)}, u32[]{:S(2)}, u32[]{:S(2)}) collective-permute-start(bf16[4,608,128]{2,1,0:T(8,128)(2,1)S(1)} %get-tuple-element.63), channel_id=1, source_target_pairs={{0,192},{1,65},{2,194},{3,67},{4,196},{5,69},{6,198},{7,71},{8,200... | collective-permute-start | bytes 1867784 | tf_op jit(solution)/shard_map/ppermute | solution.py:33
  23.7 18.3 %collective-permute-start.5 = (bf16[4,800,128]{2,1,0:T(8,128)(2,1)S(1)}, bf16[4,800,128]{2,1,0:T(8,128)(2,1)S(1)}, u32[]{:S(2)}, u32[]{:S(2)}) collective-permute-start(bf16[4,800,128]{2,1,0:T(8,128)(2,1)S(1)} %get-tuple-element.51), channel_id=1, source_target_pairs={{0,34},{1,33},{2,32},{3,35},{4,38},{5,37},{6,36},{7,39},{8,42},{9,... | collective-permute-start | bytes 2457608 | tf_op jit(solution)/shard_map/ppermute | solution.py:33
  33.6 13.2 %collective-permute-start.7 = (bf16[4,800,128]{2,1,0:T(8,128)(2,1)S(1)}, bf16[4,800,128]{2,1,0:T(8,128)(2,1)S(1)}, u32[]{:S(2)}, u32[]{:S(2)}) collective-permute-start(bf16[4,800,128]{2,1,0:T(8,128)(2,1)S(1)} %pass_on.4), channel_id=1, source_target_pairs={{0,32},{1,35},{2,34},{3,33},{4,36},{5,39},{6,38},{7,37},{8,40},{9,... | collective-permute-start | bytes 2457608 | tf_op jit(solution)/shard_map/ppermute | solution.py:33
  37.8 12.0 %collective-permute-start.13 = (bf16[4,608,128]{2,1,0:T(8,128)(2,1)S(1)}, bf16[4,608,128]{2,1,0:T(8,128)(2,1)S(1)}, u32[]{:S(2)}, u32[]{:S(2)}) collective-permute-start(bf16[4,608,128]{2,1,0:T(8,128)(2,1)S(1)} %pass_on.6), channel_id=1, source_target_pairs={{0,64},{1,193},{2,66},{3,195},{4,68},{5,197},{6,70},{7,199},{8,72}... | collective-permute-start | bytes 1867784 | tf_op jit(solution)/shard_map/ppermute | solution.py:33
  47.6 7.0 %collective-permute-start.9 = (bf16[800,128]{1,0:T(8,128)(2,1)S(1)}, bf16[800,128]{1,0:T(8,128)(2,1)S(1)}, u32[]{:S(2)}, u32[]{:S(2)}) collective-permute-start(bf16[800,128]{1,0:T(8,128)(2,1)S(1)} %get-tuple-element.57), channel_id=1, source_target_pairs={{0,64},{1,193},{2,66},{3,195},{4,68},{5,197},{6,70},{7,199},{8,72}... | collective-permute-start | bytes 614408 | tf_op jit(solution)/shard_map/ppermute | solution.py:33
  50.5 6.3 %collective-permute-start.14 = (bf16[608,128]{1,0:T(8,128)(2,1)S(1)}, bf16[608,128]{1,0:T(8,128)(2,1)S(1)}, u32[]{:S(2)}, u32[]{:S(2)}) collective-permute-start(bf16[608,128]{1,0:T(8,128)(2,1)S(1)} %get-tuple-element.68), channel_id=1, source_target_pairs={{0,32},{1,35},{2,34},{3,33},{4,36},{5,39},{6,38},{7,37},{8,40},{9,... | collective-permute-start | bytes 466952 | tf_op jit(solution)/shard_map/ppermute | solution.py:33
  53.1 5.2 %collective-permute-start.15 = (bf16[608,128]{1,0:T(8,128)(2,1)S(1)}, bf16[608,128]{1,0:T(8,128)(2,1)S(1)}, u32[]{:S(2)}, u32[]{:S(2)}) collective-permute-start(bf16[608,128]{1,0:T(8,128)(2,1)S(1)} %get-tuple-element.69), channel_id=1, source_target_pairs={{0,34},{1,33},{2,32},{3,35},{4,38},{5,37},{6,36},{7,39},{8,42},{9,... | collective-permute-start | bytes 466952 | tf_op jit(solution)/shard_map/ppermute | solution.py:33
  53.1 10.6 %collective-permute-start.8 = (bf16[800,128]{1,0:T(8,128)(2,1)S(1)}, bf16[800,128]{1,0:T(8,128)(2,1)S(1)}, u32[]{:S(2)}, u32[]{:S(2)}) collective-permute-start(bf16[800,128]{1,0:T(8,128)(2,1)S(1)} %get-tuple-element.55), channel_id=1, source_target_pairs={{0,192},{1,65},{2,194},{3,67},{4,196},{5,69},{6,198},{7,71},{8,200... | collective-permute-start | bytes 614408 | tf_op jit(solution)/shard_map/ppermute | solution.py:33
  54.7 8.9 %collective-permute-start.10 = (bf16[800,128]{1,0:T(8,128)(2,1)S(1)}, bf16[800,128]{1,0:T(8,128)(2,1)S(1)}, u32[]{:S(2)}, u32[]{:S(2)}) collective-permute-start(bf16[800,128]{1,0:T(8,128)(2,1)S(1)} %pass_on.5), channel_id=1, source_target_pairs={{0,64},{1,193},{2,66},{3,195},{4,68},{5,197},{6,70},{7,199},{8,72}... | collective-permute-start | bytes 614408 | tf_op jit(solution)/shard_map/ppermute | solution.py:33
  58.4 5.3 %collective-permute-start.16 = (bf16[608,128]{1,0:T(8,128)(2,1)S(1)}, bf16[608,128]{1,0:T(8,128)(2,1)S(1)}, u32[]{:S(2)}, u32[]{:S(2)}) collective-permute-start(bf16[608,128]{1,0:T(8,128)(2,1)S(1)} %pass_on.7), channel_id=1, source_target_pairs={{0,32},{1,35},{2,34},{3,33},{4,36},{5,39},{6,38},{7,37},{8,40},{9,... | collective-permute-start | bytes 466952 | tf_op jit(solution)/shard_map/ppermute | solution.py:33
